TPU v7x, 512 devices: a whole 4x4x16 slice. The times are simulated.
512 devices in a mesh: band: 32 (over z, core), fft: 16 (over y, x).
Axes of the slice: x: 4, y: 4, z: 16, core: 2. Of those that a mesh axis runs over, the one named last changes fastest.
Arguments:
- orbitals: bfloat16 [32, 128, 128, 128], P('band', 'fft'), may hold values from -6 to 6
- kernel: float32 [128, 128, 128], P(None, 'fft'), may hold values from 0.05 to 1
Outputs:
- exchange: float32 [32, 128, 128, 128], P('band', 'fft')
All inputs are finite; a program needn't handle non-finite values.
Results may differ from a plain program's by a relative error of at most 0.0095.
Values may be sent and summed in bfloat16 or wider, within the bound.
No kernel may reach another device: no remote copies, remote signals or barrier semaphores. Data moves between devices by JAX's collectives and lax.ppermute only.
A program may use at most 64 MiB of HBM per device.

v0:
```python
import math

import jax
import jax.numpy as jnp
import numpy as np
from jax import lax
from jax.sharding import PartitionSpec as P


def from_behind(shard, axis, by):
    devices = lax.axis_size(axis)
    return lax.ppermute(shard, axis, [(i, (i + by) % devices) for i in range(devices)])


def make_tables(length):
    index = jnp.arange(length, dtype=jnp.int32)
    phase = index[:, None] * index[None, :] % length
    angle = phase.astype(jnp.float32) * (2.0 * math.pi / length)
    factor = 1.0 / math.sqrt(length)
    return (
        (jnp.cos(angle) * factor).astype(jnp.bfloat16),
        (jnp.sin(angle) * factor).astype(jnp.bfloat16),
    )


def contract(spec, field, table):
    return jnp.einsum(spec, field, table, preferred_element_type=jnp.float32)


def section(real_part, imag_part, cosm, sinm, spec, sign):
    out_real = contract(spec, real_part, cosm) - sign * contract(spec, imag_part, sinm)
    out_imag = contract(spec, imag_part, cosm) + sign * contract(spec, real_part, sinm)
    return (out_real.astype(jnp.bfloat16), out_imag.astype(jnp.bfloat16))


def pair_lists(count):
    first, second, mirrored = ([], [], [])
    i = 0
    j = 0
    first.append(i)
    second.append(j)
    mirrored.append(j != i)
    i = 0
    j = 0
    first.append(i)
    second.append(count + j)
    mirrored.append(True)
    return (first, second, mirrored)


def pair_terms(both, kernel, first, second, mirrored, targets):
    length = both.shape[2]
    cosm, sinm = make_tables(length)
    left_rows = both[np.array(first)]
    right_rows = both[np.array(second)]
    density = (left_rows.astype(jnp.float32) * right_rows.astype(jnp.float32)).astype(jnp.bfloat16)
    real_part = contract("pxyz,zk->pxyk", density, cosm).astype(jnp.bfloat16)
    imag_part = (-contract("pxyz,zk->pxyk", density, sinm)).astype(jnp.bfloat16)
    real_part, imag_part = section(real_part, imag_part, cosm, sinm, "pxyz,yk->pxkz", -1.0)
    line_real = lax.all_to_all(real_part, "fft", split_axis=2, concat_axis=1, tiled=True)
    line_imag = lax.all_to_all(imag_part, "fft", split_axis=2, concat_axis=1, tiled=True)
    line_real, line_imag = section(line_real, line_imag, cosm, sinm, "pxyz,xk->pkyz", -1.0)
    line_real = (line_real.astype(jnp.float32) * kernel).astype(jnp.bfloat16)
    line_imag = (line_imag.astype(jnp.float32) * kernel).astype(jnp.bfloat16)
    line_real, line_imag = section(line_real, line_imag, cosm, sinm, "pxyz,xk->pkyz", 1.0)
    real_part = lax.all_to_all(line_real, "fft", split_axis=1, concat_axis=2, tiled=True)
    imag_part = lax.all_to_all(line_imag, "fft", split_axis=1, concat_axis=2, tiled=True)
    real_part, imag_part = section(real_part, imag_part, cosm, sinm, "pxyz,yk->pxkz", 1.0)
    potential = (
        contract("pxyz,zk->pxyk", real_part, cosm) - contract("pxyz,zk->pxyk", imag_part, sinm)
    ).astype(jnp.bfloat16)
    potential = potential.astype(jnp.float32)
    totals = [jnp.zeros(both.shape[1:], jnp.float32) for target in range(targets)]
    for pair in range(len(first)):
        totals[first[pair]] = totals[first[pair]] + potential[pair] * right_rows[pair].astype(
            jnp.float32
        )
        if mirrored[pair]:
            totals[second[pair]] = totals[second[pair]] + potential[pair] * left_rows[pair].astype(
                jnp.float32
            )
    return jnp.stack(totals)


def per_device(orbitals, kernel):
    count = orbitals.shape[0]
    following = from_behind(orbitals, "band", -1)
    both = jnp.concatenate([orbitals, following], axis=0)
    first, second, mirrored = pair_lists(count)
    totals = pair_terms(both, kernel, first, second, mirrored, 2 * count)
    returned = from_behind(totals[count:].astype(jnp.bfloat16), "band", 1).astype(jnp.float32)
    return totals[:count] + returned


def solution(mesh):
    in_specs = (P("band", "fft", None, None), P(None, "fft", None))
    out_specs = P("band", "fft", None, None)
    return jax.shard_map(
        per_device, mesh=mesh, in_specs=in_specs, out_specs=out_specs, check_vma=False
    )
```

profile of v0, /device:TPU:2, one launch (start us, length us, event | category | flops | bytes accessed | tf_op | source)
XLA Modules:
  0.0 95.2 jit_solution(7118584144735119748)
XLA Ops:
  0.0 8.9 %collective-permute-start = (bf16[1,8,128,128]{3,2,1,0:T(8,128)(2,1)}, bf16[1,8,128,128]{3,2,1,0:T(8,128)(2,1)S(1)}, u32[]{:S(2)}, u32[]{:S(2)}) collective-permute-start(bf16[1,8,128,128]{3,2,1,0:T(8,128)(2,1)} %param.6), channel_id=1, source_target_pairs={{0,496},{16,0},{32,16},{48,32},{64,48},{80,64},{96,80},{112,96},{1... | collective-permute-start | bytes 786440 | tf_op jit(solution)/shard_map/ppermute | solution.py:12
  8.9 1.0 %constant_dynamic-update-slice_fusion.1 = bf16[2,8,128,128]{3,2,1,0:T(8,128)(2,1)S(1)} fusion(bf16[1,8,128,128]{3,2,1,0:T(8,128)(2,1)} %param.6), kind=kLoop, calls=%fused_computation.88 | loop fusion | bytes 524288
  9.9 3.2 %collective-permute-done = bf16[1,8,128,128]{3,2,1,0:T(8,128)(2,1)S(1)} collective-permute-done((bf16[1,8,128,128]{3,2,1,0:T(8,128)(2,1)}, bf16[1,8,128,128]{3,2,1,0:T(8,128)(2,1)S(1)}, u32[]{:S(2)}, u32[]{:S(2)}) %collective-permute-start) | collective-permute-done | bytes 262176 | tf_op jit(solution)/shard_map/ppermute | solution.py:12
  13.2 0.6 gather_fusion.1
  13.8 0.6 gather_fusion
  14.5 0.5 fusion.14
  15.0 0.5 convolution_convert_fusion
  15.6 0.6 fusion.70
  16.2 0.6 fusion.28
  16.8 1.1 %copy.69 = bf16[2,8,128,128]{3,1,0,2:T(8,128)(2,1)} copy(bf16[2,8,128,128]{3,2,1,0:T(8,128)(2,1)S(1)} %fusion.28) | data formatting | bytes 1048576 | tf_op jit(solution)/shard_map/convert_element_type | solution.py:33
  17.9 7.5 %all-to-all-start.1 = ((bf16[2,8,128,128]{3,1,0,2:T(8,128)(2,1)}), bf16[2,8,128,128]{3,1,0,2:T(8,128)(2,1)S(1)}, u32[]{:S(2)}, u32[]{:S(2)}) async-start(bf16[2,8,128,128]{3,1,0,2:T(8,128)(2,1)} %copy.69), calls=%async_computation.1 | async-start | bytes 1048576 | tf_op jit(solution)/shard_map/all_to_all | solution.py:61
  25.4 0.6 fusion.72
  26.0 0.6 fusion.29
  26.5 1.1 %copy.64 = bf16[2,8,128,128]{3,1,0,2:T(8,128)(2,1)} copy(bf16[2,8,128,128]{3,2,1,0:T(8,128)(2,1)S(1)} %fusion.29) | data formatting | bytes 1048576 | tf_op jit(solution)/shard_map/convert_element_type | solution.py:33
  27.7 0.0 copy-start.1
  27.7 6.5 %all-to-all-done.1 = bf16[2,8,128,128]{3,1,0,2:T(8,128)(2,1)S(1)} async-done(((bf16[2,8,128,128]{3,1,0,2:T(8,128)(2,1)}), bf16[2,8,128,128]{3,1,0,2:T(8,128)(2,1)S(1)}, u32[]{:S(2)}, u32[]{:S(2)}) %all-to-all-start.1) | async-done | bytes 524320 | tf_op jit(solution)/shard_map/all_to_all | solution.py:61
  34.2 5.0 %all-to-all-start = ((bf16[2,8,128,128]{3,1,0,2:T(8,128)(2,1)}), bf16[2,8,128,128]{3,1,0,2:T(8,128)(2,1)S(1)}, u32[]{:S(2)}, u32[]{:S(2)}) async-start(bf16[2,8,128,128]{3,1,0,2:T(8,128)(2,1)} %copy.64), calls=%async_computation | async-start | bytes 1048576 | tf_op jit(solution)/shard_map/all_to_all | solution.py:60
  39.2 0.0 copy-done.1
  39.2 0.1 copy.72
  39.3 1.5 %fusion.43 = f32[128,2,8,128]{3,0,2,1:T(8,128)} fusion(bf16[2,8,16,8,128]{4,1,0,3,2:T(8,128)(2,1)S(1)} %bitcast.107), kind=kOutput, calls=%fused_computation.56 | convolution fusion | flops 67371008 | bytes 1572864 | tf_op jit(solution)/shard_map/pxyz,xk->pkyz/dot_general | solution.py:27
  40.8 7.2 %all-to-all-done = bf16[2,8,128,128]{3,1,0,2:T(8,128)(2,1)S(1)} async-done(((bf16[2,8,128,128]{3,1,0,2:T(8,128)(2,1)}), bf16[2,8,128,128]{3,1,0,2:T(8,128)(2,1)S(1)}, u32[]{:S(2)}, u32[]{:S(2)}) %all-to-all-start) | async-done | bytes 524320 | tf_op jit(solution)/shard_map/all_to_all | solution.py:60
  48.1 0.0 copy-start
  48.1 0.6 fusion.41
  48.6 0.6 copy-done
  49.3 0.6 fusion.22
  49.9 0.6 fusion.21
  50.5 0.6 fusion.67
  51.0 0.6 fusion.26
  51.6 1.1 %copy.83 = bf16[2,128,8,128]{3,2,0,1:T(8,128)(2,1)} copy(bf16[2,128,8,128]{3,1,2,0:T(8,128)(2,1)S(1)} %fusion.26) | data formatting | bytes 1048576 | tf_op jit(solution)/shard_map/convert_element_type | solution.py:33
  52.8 4.8 %all-to-all-start.3 = ((bf16[2,128,8,128]{3,2,0,1:T(8,128)(2,1)}), bf16[2,128,8,128]{3,2,0,1:T(8,128)(2,1)S(1)}, u32[]{:S(2)}, u32[]{:S(2)}) async-start(bf16[2,128,8,128]{3,2,0,1:T(8,128)(2,1)} %copy.83), calls=%async_computation.3 | async-start | bytes 1048576 | tf_op jit(solution)/shard_map/all_to_all | solution.py:67
  57.6 0.6 fusion.75
  58.1 0.6 fusion.27
  58.7 1.1 %copy.77 = bf16[2,128,8,128]{3,2,0,1:T(8,128)(2,1)} copy(bf16[2,128,8,128]{3,1,2,0:T(8,128)(2,1)S(1)} %fusion.27) | data formatting | bytes 1048576 | tf_op jit(solution)/shard_map/convert_element_type | solution.py:33
  59.9 7.8 %all-to-all-done.3 = bf16[2,128,8,128]{3,2,0,1:T(8,128)(2,1)S(1)} async-done(((bf16[2,128,8,128]{3,2,0,1:T(8,128)(2,1)}), bf16[2,128,8,128]{3,2,0,1:T(8,128)(2,1)S(1)}, u32[]{:S(2)}, u32[]{:S(2)}) %all-to-all-start.3) | async-done | bytes 524320 | tf_op jit(solution)/shard_map/all_to_all | solution.py:67
  67.7 4.7 %all-to-all-start.2 = ((bf16[2,128,8,128]{3,2,0,1:T(8,128)(2,1)}), bf16[2,128,8,128]{3,2,0,1:T(8,128)(2,1)S(1)}, u32[]{:S(2)}, u32[]{:S(2)}) async-start(bf16[2,128,8,128]{3,2,0,1:T(8,128)(2,1)} %copy.77), calls=%async_computation.2 | async-start | bytes 1048576 | tf_op jit(solution)/shard_map/all_to_all | solution.py:66
  72.4 1.6 %fusion.32 = f32[128,2,8,128]{3,0,2,1:T(8,128)} fusion(bf16[2,8,16,8,128]{4,3,0,1,2:T(8,128)(2,1)S(1)} %bitcast.109), kind=kOutput, calls=%fused_computation.47 | convolution fusion | flops 67371008 | bytes 1572864 | tf_op jit(solution)/shard_map/pxyz,yk->pxkz/dot_general | solution.py:27
  73.9 7.3 %all-to-all-done.2 = bf16[2,128,8,128]{3,2,0,1:T(8,128)(2,1)S(1)} async-done(((bf16[2,128,8,128]{3,2,0,1:T(8,128)(2,1)}), bf16[2,128,8,128]{3,2,0,1:T(8,128)(2,1)S(1)}, u32[]{:S(2)}, u32[]{:S(2)}) %all-to-all-start.2) | async-done | bytes 524320 | tf_op jit(solution)/shard_map/all_to_all | solution.py:66
  81.2 0.6 fusion.38
  81.8 1.8 %fusion.25 = f32[2,8,128,128]{3,2,1,0:T(8,128)} fusion(f32[128,2,8,128]{3,0,2,1:T(8,128)S(1)} %fusion.38, bf16[2,8,16,8,128]{4,3,0,1,2:T(8,128)(2,1)S(1)} %bitcast.110), kind=kOutput, calls=%fused_computation.38 | convolution fusion | flops 135266304 | bytes 2621440 | tf_op jit(solution)/shard_map/pxyz,zk->pxyk/dot_general | solution.py:27
  83.6 2.3 %fusion.13 = f32[2,8,128,128]{3,2,1,0:T(8,128)S(1)} fusion(f32[2,8,128,128]{3,2,1,0:T(8,128)} %fusion.25, f32[128,2,8,128]{3,0,2,1:T(8,128)} %fusion.32, bf16[2,8,16,8,128]{4,3,0,1,2:T(8,128)(2,1)S(1)} %bitcast.112), kind=kOutput, calls=%fused_computation.25 | convolution fusion | flops 136052736 | bytes 3670016 | tf_op jit(solution)/shard_map/pxyz,zk->pxyk/dot_general | solution.py:27
  85.9 0.1 multiply_convert_fusion.1
  86.0 0.0 collective-permute-start.1
  86.0 8.3 %collective-permute-done.1 = bf16[1,8,128,128]{3,2,1,0:T(8,128)(2,1)S(1)} collective-permute-done((bf16[1,8,128,128]{3,2,1,0:T(8,128)(2,1)S(1)}, bf16[1,8,128,128]{3,2,1,0:T(8,128)(2,1)S(1)}, u32[]{:S(2)}, u32[]{:S(2)}) %collective-permute-start.1) | collective-permute-done | bytes 262176 | tf_op jit(solution)/shard_map/ppermute | solution.py:12
  94.3 0.9 fusion.31
  (4 shorter events, 0.0 us)
Async XLA Ops:
  0.0 13.1 %collective-permute-start = (bf16[1,8,128,128]{3,2,1,0:T(8,128)(2,1)}, bf16[1,8,128,128]{3,2,1,0:T(8,128)(2,1)S(1)}, u32[]{:S(2)}, u32[]{:S(2)}) collective-permute-start(bf16[1,8,128,128]{3,2,1,0:T(8,128)(2,1)} %param.6), channel_id=1, source_target_pairs={{0,496},{16,0},{32,16},{48,32},{64,48},{80,64},{96,80},{112,96},{1... | collective-permute-start | bytes 786440 | tf_op jit(solution)/shard_map/ppermute | solution.py:12
  17.9 16.3 %all-to-all-start.1 = ((bf16[2,8,128,128]{3,1,0,2:T(8,128)(2,1)}), bf16[2,8,128,128]{3,1,0,2:T(8,128)(2,1)S(1)}, u32[]{:S(2)}, u32[]{:S(2)}) async-start(bf16[2,8,128,128]{3,1,0,2:T(8,128)(2,1)} %copy.69), calls=%async_computation.1 | async-start | bytes 1048576 | tf_op jit(solution)/shard_map/all_to_all | solution.py:61
  27.7 11.5 %copy-start.1 = (f32[128,8,128]{2,1,0:T(8,128)S(1)}, f32[128,8,128]{2,1,0:T(8,128)}, u32[]{:S(2)}) copy-start(f32[128,8,128]{2,1,0:T(8,128)} %param.7) | copy-start | bytes 1572868
  34.2 13.9 %all-to-all-start = ((bf16[2,8,128,128]{3,1,0,2:T(8,128)(2,1)}), bf16[2,8,128,128]{3,1,0,2:T(8,128)(2,1)S(1)}, u32[]{:S(2)}, u32[]{:S(2)}) async-start(bf16[2,8,128,128]{3,1,0,2:T(8,128)(2,1)} %copy.64), calls=%async_computation | async-start | bytes 1048576 | tf_op jit(solution)/shard_map/all_to_all | solution.py:60
  48.1 1.2 %copy-start = (f32[128,2,8,128]{3,0,2,1:T(8,128)S(1)}, f32[128,2,8,128]{3,0,2,1:T(8,128)}, u32[]{:S(2)}) copy-start(f32[128,2,8,128]{3,0,2,1:T(8,128)} %fusion.43) | copy-start | bytes 3145732
  52.8 14.9 %all-to-all-start.3 = ((bf16[2,128,8,128]{3,2,0,1:T(8,128)(2,1)}), bf16[2,128,8,128]{3,2,0,1:T(8,128)(2,1)S(1)}, u32[]{:S(2)}, u32[]{:S(2)}) async-start(bf16[2,128,8,128]{3,2,0,1:T(8,128)(2,1)} %copy.83), calls=%async_computation.3 | async-start | bytes 1048576 | tf_op jit(solution)/shard_map/all_to_all | solution.py:67
  67.7 13.6 %all-to-all-start.2 = ((bf16[2,128,8,128]{3,2,0,1:T(8,128)(2,1)}), bf16[2,128,8,128]{3,2,0,1:T(8,128)(2,1)S(1)}, u32[]{:S(2)}, u32[]{:S(2)}) async-start(bf16[2,128,8,128]{3,2,0,1:T(8,128)(2,1)} %copy.77), calls=%async_computation.2 | async-start | bytes 1048576 | tf_op jit(solution)/shard_map/all_to_all | solution.py:66
  86.0 8.3 %collective-permute-start.1 = (bf16[1,8,128,128]{3,2,1,0:T(8,128)(2,1)S(1)}, bf16[1,8,128,128]{3,2,1,0:T(8,128)(2,1)S(1)}, u32[]{:S(2)}, u32[]{:S(2)}) collective-permute-start(bf16[1,8,128,128]{3,2,1,0:T(8,128)(2,1)S(1)} %multiply_convert_fusion.1), channel_id=1, source_target_pairs={{0,16},{16,32},{32,48},{48,64},{64,80},{80,96},{96,112},{112,128},... | collective-permute-start | bytes 786440 | tf_op jit(solution)/shard_map/ppermute | solution.py:12
where the time goes:
time: 95.8 us; the launch traced here: 95.2 us
  waiting for transfers between devices  40.3 us (42%)
  starting transfers between devices  30.9 us (32%)
  matrix products  15.2 us (16%)
  local copies, waits for them, and re-layouts  7.64 us (8%)
  other arithmetic  0.99 us (1%)
    dot_general x18, matrix products, contract(): return jnp.einsum(spec, field, table, preferred_element_type=jnp.float32)  15.2 us
    ppermute x2, waiting for transfers between devices, from_behind(): lax.ppermute(shard, axis, [(i, (i + by) % devices) for i in range(devices)])  11.5 us
    ppermute x2, starting transfers between devices, from_behind(): lax.ppermute(shard, axis, [(i, (i + by) % devices) for i in range(devices)])  8.95 us
    all_to_all x1, waiting for transfers between devices, pair_terms(): lax.all_to_all(line_imag, 'fft', split_axis=1, concat_axis=2, tiled=True)  7.82 us
    all_to_all x1, starting transfers between devices, pair_terms(): lax.all_to_all(imag_part, 'fft', split_axis=2, concat_axis=1, tiled=True)  7.48 us
    all_to_all x1, waiting for transfers between devices, pair_terms(): lax.all_to_all(line_real, 'fft', split_axis=1, concat_axis=2, tiled=True)  7.29 us
    all_to_all x1, waiting for transfers between devices, pair_terms(): lax.all_to_all(real_part, 'fft', split_axis=2, concat_axis=1, tiled=True)  7.2 us
    all_to_all x1, waiting for transfers between devices, pair_terms(): lax.all_to_all(imag_part, 'fft', split_axis=2, concat_axis=1, tiled=True)  6.49 us
  transfers between devices with their start and end apart: 6, of which 6 were waited for; matrix products, arithmetic and copies ran while one was open for 9% of the time, Pallas kernels for 0%

commit v1 on v0

v1 whole, which is shorter than its diff:
```python
import math

import jax
import jax.numpy as jnp
import numpy as np
from jax import lax
from jax.experimental import pallas as pl
from jax.experimental.pallas import tpu as pltpu
from jax.sharding import PartitionSpec as P

F32 = jnp.float32
BF16 = jnp.bfloat16
VMEM_LIMIT = 16 * 1024 * 1024


def from_behind(shard, axis, by):
    devices = lax.axis_size(axis)
    return lax.ppermute(shard, axis, [(i, (i + by) % devices) for i in range(devices)])


def make_tables(length):
    index = np.arange(length)
    angle = (index[:, None] * index[None, :] % length).astype(np.float32)
    angle = angle * np.float32(2.0 * math.pi / length)
    factor = np.float32(1.0 / math.sqrt(length))
    cosm = (np.cos(angle) * factor).astype(jnp.bfloat16)
    sinm = (np.sin(angle) * factor).astype(jnp.bfloat16)
    return cosm, sinm


def complex_tables(length, parts):
    cosm, sinm = make_tables(length)
    ahead = np.block([[cosm, sinm], [-sinm, cosm]])
    back = np.block([[cosm, -sinm], [sinm, cosm]])
    block = length // parts
    order = np.arange(2 * length).reshape(2, parts, block).transpose(1, 0, 2).reshape(-1)
    return ahead, back, ahead[order], back[:, order]


def dot(left, right):
    return jnp.dot(left, right, preferred_element_type=F32)


def planes_forward(own_ref, next_ref, zed_ref, why_ref, out_ref):
    planes, length = own_ref.shape[0], own_ref.shape[1]
    groups = out_ref.shape[0]
    for x in range(0, planes, 2):
        own = own_ref[x : x + 2].astype(F32).reshape(2 * length, length)
        after = next_ref[x : x + 2].astype(F32).reshape(2 * length, length)
        field = jnp.concatenate([(own * own).astype(BF16), (own * after).astype(BF16)], axis=1)
        field = dot(field, zed_ref[...]).astype(BF16)
        field = jnp.concatenate(
            [
                jnp.concatenate([field[:length, :length], field[length:, :length]], axis=1),
                jnp.concatenate([field[:length, length:], field[length:, length:]], axis=1),
            ],
            axis=0,
        )
        field = dot(why_ref[...], field).astype(BF16)
        out_ref[:, x] = field[:, :length].reshape(groups, -1, length)
        out_ref[:, x + 1] = field[:, length:].reshape(groups, -1, length)


def columns_filter(line_ref, screen_ref, ahead_ref, back_ref, out_ref, held, sent):
    length = line_ref.shape[0]
    rows = line_ref.shape[1]
    columns = rows // 2
    held[...] = line_ref[...].astype(F32).reshape(length * rows, length)
    for c in range(0, columns, 2):
        field = jnp.concatenate(
            [
                jnp.concatenate(
                    [
                        held[pl.ds(part * columns + c + j, length, stride=rows), :]
                        for j in range(2)
                    ],
                    axis=1,
                )
                for part in range(2)
            ],
            axis=0,
        ).astype(BF16)
        field = dot(ahead_ref[...], field)
        screen = jnp.concatenate([screen_ref[c], screen_ref[c + 1]], axis=1)
        field = jnp.concatenate([field[:length] * screen, field[length:] * screen], axis=0)
        field = dot(back_ref[...], field.astype(BF16))
        for part in range(2):
            for j in range(2):
                sent[pl.ds(part * columns + c + j, length, stride=rows), :] = field[
                    part * length : (part + 1) * length, j * length : (j + 1) * length
                ]
    out_ref[...] = sent[...].reshape(length, rows, length).astype(BF16)


def planes_back(line_ref, own_ref, next_ref, why_ref, zed_ref, kept_ref, sent_ref):
    planes, length = own_ref.shape[0], own_ref.shape[1]
    for x in range(0, planes, 2):
        field = jnp.concatenate(
            [line_ref[:, x + j].reshape(2 * length, length) for j in range(2)], axis=1
        )
        field = dot(why_ref[...], field).astype(BF16)
        field = jnp.concatenate(
            [
                jnp.concatenate([field[:length, :length], field[length:, :length]], axis=1),
                jnp.concatenate([field[:length, length:], field[length:, length:]], axis=1),
            ],
            axis=0,
        )
        field = dot(field, zed_ref[...])
        own = own_ref[x : x + 2].astype(F32).reshape(2 * length, length)
        after = next_ref[x : x + 2].astype(F32).reshape(2 * length, length)
        kept = field[:, :length] * own + field[:, length:] * after
        sent = (field[:, length:] * own).astype(BF16)
        kept_ref[x : x + 2] = kept.reshape(2, length, length)
        sent_ref[x : x + 2] = sent.reshape(2, length, length)


def symmetric_kernel(here_ref, there_ref, edge_ref, flip_ref, out_ref, there):
    columns, length = out_ref.shape[0], out_ref.shape[1]
    there[...] = there_ref[...].astype(F32)
    for c in range(columns):
        if c == 0:
            other = edge_ref[...]
        else:
            other = there[pl.ds(columns - c, length, stride=columns), :].astype(BF16)
        other = dot(flip_ref[...], dot(other, flip_ref[...]).astype(BF16))
        out_ref[c] = 0.5 * (here_ref[pl.ds(c, length, stride=columns), :] + other)


def call(body, outs, scratch=(), flops=0, name=None):
    return pl.pallas_call(
        body,
        out_shape=outs,
        scratch_shapes=list(scratch),
        cost_estimate=pl.CostEstimate(flops=flops, bytes_accessed=1 << 20, transcendentals=0),
        compiler_params=pltpu.CompilerParams(vmem_limit_bytes=VMEM_LIMIT),
        name=name,
    )


def per_device(orbitals, kernel):
    own = orbitals[0]
    planes, length = own.shape[0], own.shape[1]
    groups = lax.axis_size("fft")
    columns = length // groups
    ahead, back, ahead_sorted, back_sorted = complex_tables(length, groups)
    flip = np.zeros((length, length), np.float32)
    flip[np.arange(length), -np.arange(length) % length] = 1.0
    work = 8 * planes * length**3

    after = from_behind(own, "band", -1)
    narrow = kernel.astype(BF16)
    there = lax.ppermute(narrow, "fft", [(i, groups - 1 - i) for i in range(groups)])
    edge = lax.ppermute(narrow[:, 0], "fft", [(i, -i % groups) for i in range(groups)])

    lines = jax.ShapeDtypeStruct((groups, planes, 2 * columns, length), BF16)
    spectrum = call(planes_forward, lines, flops=2 * work, name="planes_forward")(
        own, after, jnp.asarray(back), jnp.asarray(ahead_sorted)
    )
    spectrum = lax.all_to_all(spectrum, "fft", split_axis=0, concat_axis=0, tiled=True)
    screen = call(
        symmetric_kernel,
        jax.ShapeDtypeStruct((columns, length, length), F32),
        [pltpu.VMEM((length * columns, length), F32)],
        flops=work,
        name="symmetric_kernel",
    )(
        kernel.reshape(length * columns, length),
        there.reshape(length * columns, length),
        edge,
        jnp.asarray(flip.astype(jnp.bfloat16)),
    )
    spectrum = call(
        columns_filter,
        jax.ShapeDtypeStruct((length, 2 * columns, length), BF16),
        [pltpu.VMEM((2 * length * columns, length), F32)] * 2,
        flops=2 * work,
        name="columns_filter",
    )(
        spectrum.reshape(length, 2 * columns, length),
        screen,
        jnp.asarray(ahead),
        jnp.asarray(back),
    )
    spectrum = spectrum.reshape(groups, planes, 2 * columns, length)
    spectrum = lax.all_to_all(spectrum, "fft", split_axis=0, concat_axis=0, tiled=True)
    kept, sent = call(
        planes_back,
        (
            jax.ShapeDtypeStruct(own.shape, F32),
            jax.ShapeDtypeStruct(own.shape, BF16),
        ),
        flops=2 * work,
        name="planes_back",
    )(spectrum, own, after, jnp.asarray(back_sorted), jnp.asarray(ahead))
    returned = from_behind(sent, "band", 1).astype(F32)
    return (kept + returned)[None]


def solution(mesh):
    in_specs = (P("band", "fft", None, None), P(None, "fft", None))
    out_specs = P("band", "fft", None, None)
    return jax.shard_map(
        per_device, mesh=mesh, in_specs=in_specs, out_specs=out_specs, check_vma=False
    )
```

time: 95.8 us -> 64.3 us (0.67)
  waiting for transfers between devices: 40.3 us -> 18.9 us
  matrix products: 15.2 us -> 0 us
  blocking collectives: 0 us -> 12.5 us
  starting transfers between devices: 30.9 us -> 24.7 us
  local copies, waits for them, and re-layouts: 7.64 us -> 3.61 us
  Pallas kernels: 0 us -> 3.29 us
    all_to_all x4 -> x1, waiting for transfers between devices: 28.8 us -> 0.01 us  [per_device(): lax.all_to_all(spectrum, 'fft', split_axis=0, concat_axis=0, tiled=True)]
    dot_general x18 -> x0, matrix products: 15.2 us -> none  [contract(): return jnp.einsum(spec, field, table, preferred_element_type=jnp.float32)]
    all_to_all x4 -> x1, starting transfers between devices: 22 us -> 7.61 us  [per_device(): lax.all_to_all(spectrum, 'fft', split_axis=0, concat_axis=0, tiled=True)]
    all_to_all x0 -> x1, blocking collectives: none -> 12.5 us  [per_device(): lax.all_to_all(spectrum, 'fft', split_axis=0, concat_axis=0, tiled=True)]
    ppermute x0 -> x2, starting transfers between devices: none -> 8.1 us  [the longest x1 5.49 us: per_device(): lax.ppermute(narrow, 'fft', [(i, groups - 1 - i) for i in range(groups)])]
    ppermute x0 -> x2, waiting for transfers between devices: none -> 6.62 us  [the longest x1 3.59 us: per_device(): lax.ppermute(narrow[:, 0], 'fft', [(i, -i % groups) for i in range(groups)])]
    convert_element_type x4 -> x0, local copies, waits for them, and re-layouts: 4.56 us -> none  [section(): return (out_real.astype(jnp.bfloat16), out_imag.astype(jnp.bfloat16))]
    pallas_call x0 -> x4, Pallas kernels: none -> 3.29 us  [the longest x1 1.42 us: per_device(): call(planes_forward, lines, flops=2 * work, name='planes_forward')]
  transfers between devices with their start and end apart: 6 -> 5, of which waited for: 6 -> 4; matrix products, arithmetic and copies ran while one was open for 9% -> 0% of each run, Pallas kernels for 0% -> 1%
where the time goes in v1:
time: 64.3 us; the launch traced here: 63.9 us
  starting transfers between devices  24.7 us (38%)
  waiting for transfers between devices  18.9 us (29%)
  blocking collectives  12.5 us (19%)
  local copies, waits for them, and re-layouts  3.61 us (6%)
  Pallas kernels  3.29 us (5%)
  other arithmetic  0.85 us (1%)
    all_to_all x1, blocking collectives, per_device(): lax.all_to_all(spectrum, 'fft', split_axis=0, concat_axis=0, tiled=True)  12.5 us
    ppermute x2, waiting for transfers between devices, from_behind(): lax.ppermute(shard, axis, [(i, (i + by) % devices) for i in range(devices)])  12.2 us
    ppermute x2, starting transfers between devices, from_behind(): lax.ppermute(shard, axis, [(i, (i + by) % devices) for i in range(devices)])  8.95 us
    all_to_all x1, starting transfers between devices, per_device(): lax.all_to_all(spectrum, 'fft', split_axis=0, concat_axis=0, tiled=True)  7.61 us
    ppermute x1, starting transfers between devices, per_device(): lax.ppermute(narrow, 'fft', [(i, groups - 1 - i) for i in range(groups)])  5.49 us
    ppermute x1, waiting for transfers between devices, per_device(): lax.ppermute(narrow[:, 0], 'fft', [(i, -i % groups) for i in range(groups)])  3.59 us
    unnamed x19, local copies, waits for them, and re-layouts  3.43 us
    ppermute x1, waiting for transfers between devices, per_device(): lax.ppermute(narrow, 'fft', [(i, groups - 1 - i) for i in range(groups)])  3.04 us
  transfers between devices with their start and end apart: 5, of which 4 were waited for; matrix products, arithmetic and copies ran while one was open for 0% of the time, Pallas kernels for 1%

profile of v1, /device:TPU:2, one launch (start us, length us, event | category | flops | bytes accessed | tf_op | source)
XLA Modules:
  0.0 63.9 jit_solution(9285096447519910311)
XLA Ops:
  0.0 8.9 %collective-permute-start = (bf16[8,128,128]{2,1,0:T(8,128)(2,1)}, bf16[8,128,128]{2,1,0:T(8,128)(2,1)S(1)}, u32[]{:S(2)}, u32[]{:S(2)}) collective-permute-start(bf16[8,128,128]{2,1,0:T(8,128)(2,1)} %bitcast.14), channel_id=1, source_target_pairs={{0,496},{16,0},{32,16},{48,32},{64,48},{80,64},{96,80},{112,96},{1... | collective-permute-start | bytes 786440 | tf_op jit(solution)/shard_map/ppermute | solution.py:18
  8.9 4.2 %collective-permute-done.next_ref = bf16[8,128,128]{2,1,0:T(8,128)(2,1)S(1)} collective-permute-done((bf16[8,128,128]{2,1,0:T(8,128)(2,1)}, bf16[8,128,128]{2,1,0:T(8,128)(2,1)S(1)}, u32[]{:S(2)}, u32[]{:S(2)}) %collective-permute-start) | collective-permute-done | bytes 262176 | tf_op jit(solution)/shard_map/ppermute | solution.py:18
  13.1 0.0 copy-start.1
  13.1 0.9 %copy-done.1 = bf16[1,8,128,128]{3,2,1,0:T(8,128)(2,1)S(1)} copy-done((bf16[1,8,128,128]{3,2,1,0:T(8,128)(2,1)S(1)}, bf16[1,8,128,128]{3,2,1,0:T(8,128)(2,1)}, u32[]{:S(2)}) %copy-start.1) | copy-done | bytes 262168
  14.1 0.0 copy-start.4
  14.1 0.9 %copy-done.4 = bf16[256,256]{1,0:T(8,128)(2,1)S(1)} copy-done((bf16[256,256]{1,0:T(8,128)(2,1)S(1)}, bf16[256,256]{1,0:T(8,128)(2,1)}, u32[]{:S(2)}) %copy-start.4) | copy-done | bytes 131096
  15.0 0.0 copy-start.7
  15.0 0.9 %copy-done.7 = bf16[256,256]{1,0:T(8,128)(2,1)S(1)} copy-done((bf16[256,256]{1,0:T(8,128)(2,1)S(1)}, bf16[256,256]{1,0:T(8,128)(2,1)}, u32[]{:S(2)}) %copy-start.7) | copy-done | bytes 131096
  15.9 1.4 %planes_forward.1 = bf16[16,8,16,128]{3,2,1,0:T(8,128)(2,1)} custom-call(bf16[8,128,128]{2,1,0:T(8,128)(2,1)S(1)} %bitcast.15, bf16[8,128,128]{2,1,0:T(8,128)(2,1)S(1)} %collective-permute-done.next_ref, bf16[256,256]{1,0:T(8,128)(2,1)S(1)} %copy-done.4, bf16[256,256]{1,0:T(8,128)(2,1)S(1)} %copy-done.7), custom_call_target="tpu_custom_call" | custom-call | flops 268435456 | bytes 1048576 | tf_op jit(solution)/shard_map/planes_forward/pallas_call | solution.py:157
  17.3 0.0 copy-start
  17.3 7.6 %all-to-all-start = ((bf16[16,8,16,128]{3,2,1,0:T(8,128)(2,1)}), bf16[16,8,16,128]{3,2,1,0:T(8,128)(2,1)S(1)}, u32[]{:S(2)}, u32[]{:S(2)}) async-start(bf16[16,8,16,128]{3,2,1,0:T(8,128)(2,1)} %planes_forward.1), calls=%async_computation | async-start | bytes 1048576 | tf_op jit(solution)/shard_map/all_to_all | solution.py:160
  24.9 0.0 copy-done
  24.9 0.1 copy.13
  25.0 5.5 %collective-permute-start.1 = (bf16[128,8,128]{2,0,1:T(8,128)(2,1)S(1)}, bf16[128,8,128]{2,0,1:T(8,128)(2,1)S(1)}, u32[]{:S(2)}, u32[]{:S(2)}) collective-permute-start(bf16[128,8,128]{2,0,1:T(8,128)(2,1)S(1)} %copy.13), channel_id=1, source_target_pairs={{0,15},{1,14},{2,13},{3,12},{4,11},{5,10},{6,9},{7,8},{8,7},{9,6},... | collective-permute-start | bytes 786440 | tf_op jit(solution)/shard_map/ppermute | solution.py:153
  30.6 0.0 copy-start.8
  30.6 2.6 %collective-permute-start.2 = (bf16[128,128]{1,0:T(8,128)(2,1)S(1)}, bf16[128,128]{1,0:T(8,128)(2,1)S(1)}, u32[]{:S(2)}, u32[]{:S(2)}) collective-permute-start(bf16[128,128]{1,0:T(8,128)(2,1)S(1)} %slice_bitcast_fusion), channel_id=1, source_target_pairs={{0,0},{1,15},{2,14},{3,13},{4,12},{5,11},{6,10},{7,9},{8,8},{9,7},... | collective-permute-start | bytes 98312 | tf_op jit(solution)/shard_map/ppermute | solution.py:154
  33.2 3.0 %collective-permute-done.1 = bf16[128,8,128]{2,0,1:T(8,128)(2,1)S(1)} collective-permute-done((bf16[128,8,128]{2,0,1:T(8,128)(2,1)S(1)}, bf16[128,8,128]{2,0,1:T(8,128)(2,1)S(1)}, u32[]{:S(2)}, u32[]{:S(2)}) %collective-permute-start.1) | collective-permute-done | bytes 262176 | tf_op jit(solution)/shard_map/ppermute | solution.py:153
  36.2 0.2 copy.14
  36.4 3.6 %collective-permute-done.2.edge_ref = bf16[128,128]{1,0:T(8,128)(2,1)S(1)} collective-permute-done((bf16[128,128]{1,0:T(8,128)(2,1)S(1)}, bf16[128,128]{1,0:T(8,128)(2,1)S(1)}, u32[]{:S(2)}, u32[]{:S(2)}) %collective-permute-start.2) | collective-permute-done | bytes 32800 | tf_op jit(solution)/shard_map/ppermute | solution.py:154
  40.0 0.0 copy-done.8
  40.0 0.0 copy-start.3
  40.0 0.0 copy-start.5
  40.0 0.4 symmetric_kernel.1.screen_ref
  40.4 0.0 all-to-all-done
  40.4 0.5 copy-done.3
  40.9 0.1 copy-done.5
  41.0 0.9 %columns_filter.1 = bf16[128,16,128]{2,1,0:T(8,128)(2,1)S(1)} custom-call(bf16[128,16,128]{2,1,0:T(8,128)(2,1)S(1)} %bitcast.11, f32[8,128,128]{2,1,0:T(8,128)S(1)} %symmetric_kernel.1.screen_ref, bf16[256,256]{1,0:T(8,128)(2,1)S(1)} %copy-done.3, bf16[256,256]{1,0:T(8,128)(2,1)S(1)} %copy-done.5), custom_call_target="tpu_custom_call" | custom-call | flops 268435456 | bytes 1048576 | tf_op jit(solution)/shard_map/columns_filter/pallas_call | solution.py:173
  41.9 0.0 copy-start.2
  41.9 0.0 copy-start.6
  41.9 12.5 %all_to_all.10.line_ref = bf16[16,8,16,128]{3,2,1,0:T(8,128)(2,1)S(1)} all-to-all(bf16[16,8,16,128]{3,2,1,0:T(8,128)(2,1)S(1)} %bitcast.12), channel_id=1, replica_groups=mesh['band'=32,'fft'=16] {'fft'}, dimensions={0} | all-to-all | bytes 1048576 | tf_op jit(solution)/shard_map/all_to_all | solution.py:186
  54.4 0.0 copy-done.2
  54.4 0.0 copy-done.6
  54.4 0.6 planes_back.1
  55.0 0.0 collective-permute-start.3
  55.0 8.0 %collective-permute-done.3 = bf16[8,128,128]{2,1,0:T(8,128)(2,1)S(1)} collective-permute-done((bf16[8,128,128]{2,1,0:T(8,128)(2,1)S(1)}, bf16[8,128,128]{2,1,0:T(8,128)(2,1)S(1)}, u32[]{:S(2)}, u32[]{:S(2)}) %collective-permute-start.3) | collective-permute-done | bytes 262176 | tf_op jit(solution)/shard_map/ppermute | solution.py:18
  63.1 0.9 %add_bitcast_fusion = f32[1,8,128,128]{3,2,1,0:T(8,128)} fusion(f32[8,128,128]{2,1,0:T(8,128)S(1)} %get-tuple-element.7, bf16[8,128,128]{2,1,0:T(8,128)(2,1)S(1)} %collective-permute-done.3), kind=kLoop, calls=%fused_computation.1 | loop fusion | flops 262144 | bytes 1310720 | tf_op jit(solution)/shard_map/broadcast_in_dim | solution.py:197
  (1 shorter events, 0.0 us)
Async XLA Ops:
  0.0 13.1 %collective-permute-start = (bf16[8,128,128]{2,1,0:T(8,128)(2,1)}, bf16[8,128,128]{2,1,0:T(8,128)(2,1)S(1)}, u32[]{:S(2)}, u32[]{:S(2)}) collective-permute-start(bf16[8,128,128]{2,1,0:T(8,128)(2,1)} %bitcast.14), channel_id=1, source_target_pairs={{0,496},{16,0},{32,16},{48,32},{64,48},{80,64},{96,80},{112,96},{1... | collective-permute-start | bytes 786440 | tf_op jit(solution)/shard_map/ppermute | solution.py:18
  13.1 0.9 %copy-start.1 = (bf16[1,8,128,128]{3,2,1,0:T(8,128)(2,1)S(1)}, bf16[1,8,128,128]{3,2,1,0:T(8,128)(2,1)}, u32[]{:S(2)}) copy-start(bf16[1,8,128,128]{3,2,1,0:T(8,128)(2,1)} %param.7) | copy-start | bytes 786436
  14.1 0.9 %copy-start.4 = (bf16[256,256]{1,0:T(8,128)(2,1)S(1)}, bf16[256,256]{1,0:T(8,128)(2,1)}, u32[]{:S(2)}) copy-start(bf16[256,256]{1,0:T(8,128)(2,1)} %constant.10.clone.zed_ref.back_ref) | copy-start | bytes 393220
  15.0 0.9 %copy-start.7 = (bf16[256,256]{1,0:T(8,128)(2,1)S(1)}, bf16[256,256]{1,0:T(8,128)(2,1)}, u32[]{:S(2)}) copy-start(bf16[256,256]{1,0:T(8,128)(2,1)} %constant.11.clone.why_ref) | copy-start | bytes 393220
  17.3 7.6 %copy-start = (f32[128,8,128]{2,1,0:T(8,128)S(1)}, f32[128,8,128]{2,1,0:T(8,128)}, u32[]{:S(2)}) copy-start(f32[128,8,128]{2,1,0:T(8,128)} %param.8) | copy-start | bytes 1572868
  17.3 23.1 %all-to-all-start = ((bf16[16,8,16,128]{3,2,1,0:T(8,128)(2,1)}), bf16[16,8,16,128]{3,2,1,0:T(8,128)(2,1)S(1)}, u32[]{:S(2)}, u32[]{:S(2)}) async-start(bf16[16,8,16,128]{3,2,1,0:T(8,128)(2,1)} %planes_forward.1), calls=%async_computation | async-start | bytes 1048576 | tf_op jit(solution)/shard_map/all_to_all | solution.py:160
  25.0 11.2 %collective-permute-start.1 = (bf16[128,8,128]{2,0,1:T(8,128)(2,1)S(1)}, bf16[128,8,128]{2,0,1:T(8,128)(2,1)S(1)}, u32[]{:S(2)}, u32[]{:S(2)}) collective-permute-start(bf16[128,8,128]{2,0,1:T(8,128)(2,1)S(1)} %copy.13), channel_id=1, source_target_pairs={{0,15},{1,14},{2,13},{3,12},{4,11},{5,10},{6,9},{7,8},{8,7},{9,6},... | collective-permute-start | bytes 786440 | tf_op jit(solution)/shard_map/ppermute | solution.py:153
  30.6 9.4 %copy-start.8 = (bf16[128,128]{1,0:T(8,128)(2,1)S(1)}, bf16[128,128]{1,0:T(8,128)(2,1)}, u32[]{:S(2)}) copy-start(bf16[128,128]{1,0:T(8,128)(2,1)} %constant.12.clone.flip_ref) | copy-start | bytes 98308
  30.6 9.4 %collective-permute-start.2 = (bf16[128,128]{1,0:T(8,128)(2,1)S(1)}, bf16[128,128]{1,0:T(8,128)(2,1)S(1)}, u32[]{:S(2)}, u32[]{:S(2)}) collective-permute-start(bf16[128,128]{1,0:T(8,128)(2,1)S(1)} %slice_bitcast_fusion), channel_id=1, source_target_pairs={{0,0},{1,15},{2,14},{3,13},{4,12},{5,11},{6,10},{7,9},{8,8},{9,7},... | collective-permute-start | bytes 98312 | tf_op jit(solution)/shard_map/ppermute | solution.py:154
  40.0 0.9 %copy-start.3 = (bf16[256,256]{1,0:T(8,128)(2,1)S(1)}, bf16[256,256]{1,0:T(8,128)(2,1)}, u32[]{:S(2)}) copy-start(bf16[256,256]{1,0:T(8,128)(2,1)} %constant.13.clone.ahead_ref.zed_ref) | copy-start | bytes 393220
  40.0 1.0 %copy-start.5 = (bf16[256,256]{1,0:T(8,128)(2,1)S(1)}, bf16[256,256]{1,0:T(8,128)(2,1)}, u32[]{:S(2)}) copy-start(bf16[256,256]{1,0:T(8,128)(2,1)} %constant.10.clone.zed_ref.back_ref) | copy-start | bytes 393220
  41.9 12.6 %copy-start.2 = (bf16[1,8,128,128]{3,2,1,0:T(8,128)(2,1)S(1)}, bf16[1,8,128,128]{3,2,1,0:T(8,128)(2,1)}, u32[]{:S(2)}) copy-start(bf16[1,8,128,128]{3,2,1,0:T(8,128)(2,1)} %param.7) | copy-start | bytes 786436
  41.9 12.6 %copy-start.6 = (bf16[256,256]{1,0:T(8,128)(2,1)S(1)}, bf16[256,256]{1,0:T(8,128)(2,1)}, u32[]{:S(2)}) copy-start(bf16[256,256]{1,0:T(8,128)(2,1)} %constant.14.clone.why_ref) | copy-start | bytes 393220
  55.0 8.1 %collective-permute-start.3 = (bf16[8,128,128]{2,1,0:T(8,128)(2,1)S(1)}, bf16[8,128,128]{2,1,0:T(8,128)(2,1)S(1)}, u32[]{:S(2)}, u32[]{:S(2)}) collective-permute-start(bf16[8,128,128]{2,1,0:T(8,128)(2,1)S(1)} %get-tuple-element.8), channel_id=1, source_target_pairs={{0,16},{16,32},{32,48},{48,64},{64,80},{80,96},{96,112},{112,128},... | collective-permute-start | bytes 786440 | tf_op jit(solution)/shard_map/ppermute | solution.py:18

commit v2 on v1

v2 whole, which is shorter than its diff:
```python
import math

import jax
import jax.numpy as jnp
import numpy as np
from jax import lax
from jax.experimental import pallas as pl
from jax.experimental.pallas import tpu as pltpu
from jax.sharding import PartitionSpec as P

F32 = jnp.float32
BF16 = jnp.bfloat16
VMEM_LIMIT = 16 * 1024 * 1024
AHEAD, BACK, AHEAD_SORTED, BACK_SORTED, ZED, DEZ = range(6)
FLIP, LOW, HIGH, WHOLE = range(4)
SPARE = 16


def from_behind(shard, axis, by):
    devices = lax.axis_size(axis)
    return lax.ppermute(shard, axis, [(i, (i + by) % devices) for i in range(devices)])


def make_tables(length):
    index = np.arange(length)
    angle = (index[:, None] * index[None, :] % length).astype(np.float32)
    angle = angle * np.float32(2.0 * math.pi / length)
    factor = np.float32(1.0 / math.sqrt(length))
    cosm = (np.cos(angle) * factor).astype(jnp.bfloat16)
    sinm = (np.sin(angle) * factor).astype(jnp.bfloat16)
    return cosm, sinm


def complex_tables(length, parts):
    cosm, sinm = make_tables(length)
    ahead = np.block([[cosm, sinm], [-sinm, cosm]])
    back = np.block([[cosm, -sinm], [sinm, cosm]])
    block = length // parts
    order = np.arange(2 * length).reshape(2, parts, block).transpose(1, 0, 2).reshape(-1)
    half = length // 2
    zed = np.zeros((2, length, 2, length), np.float32)
    for line in range(2):
        for slot in (0, half):
            zed[line, :, line, slot] = cosm[:, slot]
        slots = slice(line * half + 1, (line + 1) * half)
        zed[line, :, 0, slots] = cosm[:, 1:half]
        zed[line, :, 1, slots] = -sinm[:, 1:half].astype(np.float32)
    dez = 2.0 * zed
    dez[:, :, :, 0] *= 0.5
    dez[:, :, :, half] *= 0.5
    zed = zed.reshape(2 * length, 2 * length).astype(ahead.dtype)
    dez = dez.reshape(2 * length, 2 * length).T.astype(ahead.dtype)
    return ahead, back, ahead[order], back[:, order], zed, dez


def mirror_tables(length):
    half = length // 2
    index = np.arange(length)
    frequency = np.where(index <= half, index, index - half)
    wanted = -frequency % length
    whole = index[:, None] == wanted[None, :]
    low = (index[:, None] < half) & (index[:, None] + half == wanted[None, :])
    high = (index[:, None] >= half) & whole
    flip = index[:, None] == (-index % length)[None, :]
    return np.stack([flip, low, high, whole]).astype(np.float32).astype(jnp.bfloat16)


def dot(left, right):
    return jnp.dot(left, right, preferred_element_type=F32)


def planes_forward(own_ref, next_ref, table_ref, out_ref):
    planes, length = own_ref.shape[0], own_ref.shape[1]
    groups = out_ref.shape[0]
    for x in range(0, planes, 2):
        own = own_ref[x : x + 2].astype(F32).reshape(2 * length, length)
        after = next_ref[x : x + 2].astype(F32).reshape(2 * length, length)
        field = jnp.concatenate([(own * own).astype(BF16), (own * after).astype(BF16)], axis=1)
        field = dot(field, table_ref[ZED]).astype(BF16)
        field = jnp.concatenate(
            [
                jnp.concatenate([field[:length, :length], field[length:, :length]], axis=1),
                jnp.concatenate([field[:length, length:], field[length:, length:]], axis=1),
            ],
            axis=0,
        )
        field = dot(table_ref[AHEAD_SORTED], field).astype(BF16)
        out_ref[:, x] = field[:, :length].reshape(groups, -1, length)
        out_ref[:, x + 1] = field[:, length:].reshape(groups, -1, length)


def columns_filter(line_ref, screen_ref, table_ref, out_ref, held, sent):
    length = line_ref.shape[0]
    rows = line_ref.shape[1]
    columns = rows // 2
    held[...] = line_ref[...].astype(F32).reshape(length * rows, length)
    for c in range(0, columns, 2):
        field = jnp.concatenate(
            [
                jnp.concatenate(
                    [
                        held[pl.ds(part * columns + c + j, length, stride=rows), :]
                        for j in range(2)
                    ],
                    axis=1,
                )
                for part in range(2)
            ],
            axis=0,
        ).astype(BF16)
        field = dot(table_ref[AHEAD], field)
        screen = jnp.concatenate([screen_ref[c], screen_ref[c + 1]], axis=1)
        field = jnp.concatenate([field[:length] * screen, field[length:] * screen], axis=0)
        field = dot(table_ref[BACK], field.astype(BF16))
        for part in range(2):
            for j in range(2):
                sent[pl.ds(part * columns + c + j, length, stride=rows), :] = field[
                    part * length : (part + 1) * length, j * length : (j + 1) * length
                ]
    out_ref[...] = sent[...].reshape(length, rows, length).astype(BF16)


def planes_back(line_ref, own_ref, next_ref, table_ref, kept_ref, sent_ref):
    planes, length = own_ref.shape[0], own_ref.shape[1]
    for x in range(0, planes, 2):
        field = jnp.concatenate(
            [line_ref[:, x + j].reshape(2 * length, length) for j in range(2)], axis=1
        )
        field = dot(table_ref[BACK_SORTED], field).astype(BF16)
        field = jnp.concatenate(
            [
                jnp.concatenate([field[:length, :length], field[length:, :length]], axis=1),
                jnp.concatenate([field[:length, length:], field[length:, length:]], axis=1),
            ],
            axis=0,
        )
        field = dot(field, table_ref[DEZ])
        own = own_ref[x : x + 2].astype(F32).reshape(2 * length, length)
        after = next_ref[x : x + 2].astype(F32).reshape(2 * length, length)
        kept = field[:, :length] * own + field[:, length:] * after
        sent = (field[:, length:] * own).astype(BF16)
        kept_ref[x : x + 2] = kept.reshape(2, length, length)
        sent_ref[x : x + 2] = sent.reshape(2, length, length)


def relay(there_ref, out_ref):
    out_ref[...] = there_ref[...]


def symmetric_kernel(here_ref, first_ref, second_ref, mirror_ref, out_ref, low, high, zero):
    columns, length = out_ref.shape[0], out_ref.shape[1]
    half = length // 2
    packed = half * columns
    odd = lax.rem(lax.axis_index("band"), 2)

    def spread(main_ref, edge_ref):
        row = lax.broadcasted_iota(jnp.int32, (packed, length), 0)
        for out, choice in ((low, LOW), (high, HIGH)):
            main = dot(main_ref[:packed], mirror_ref[choice])
            edge = dot(edge_ref[:packed], mirror_ref[choice])
            out[...] = jnp.where(lax.rem(row, columns) == 0, edge, main)
        row = lax.broadcasted_iota(jnp.int32, (SPARE, length), 0)
        main, edge = main_ref[packed:].astype(F32), edge_ref[packed:].astype(F32)
        zero[...] = jnp.where(row == 0, edge, main)

    pl.when(odd == 0)(lambda: spread(first_ref, second_ref))
    pl.when(odd == 1)(lambda: spread(second_ref, first_ref))
    zeros = zero[...].astype(BF16)
    slot = lax.broadcasted_iota(jnp.int32, (length, length), 1)
    row = lax.broadcasted_iota(jnp.int32, (SPARE, length), 0)
    first = lax.broadcasted_iota(jnp.int32, (SPARE, length), 1) == 0
    for c in range(columns):
        source = (columns - c) % columns
        other = jnp.concatenate(
            [part[pl.ds(source, half, stride=columns), :] for part in (low, high)], axis=0
        )
        chosen = ((row == source) & first).astype(F32).astype(BF16)
        other = other + lax.dot_general(
            zeros, chosen, (((0,), (0,)), ((), ())), preferred_element_type=F32
        )
        other = dot(mirror_ref[FLIP], other.astype(BF16))
        here = here_ref[pl.ds(c, length, stride=columns), :]
        here = jnp.where(slot <= half, here, pltpu.roll(here, half, 1))
        out_ref[c] = 0.5 * (here + other)


def prepare(own_ref, kernel_ref, table_ref, mirror_ref, own_out, kernel_out, table_out, mirror_out,
            packed_out, sems):
    pairs = (
        (kernel_ref, kernel_out),
        (own_ref, own_out),
        (table_ref, table_out),
        (mirror_ref, mirror_out),
    )
    copies = [pltpu.make_async_copy(a, b, sems.at[i]) for i, (a, b) in enumerate(pairs)]
    for copy in copies:
        copy.start()
    copies[0].wait()
    length = kernel_out.shape[1]
    half = length // 2
    columns = kernel_out.shape[0] // length
    packed = half * columns
    lane = lax.broadcasted_iota(jnp.int32, (packed, length), 1)
    packed_out[:packed] = jnp.where(
        lane < half, pltpu.roll(kernel_out[:packed], half, 1), kernel_out[packed:]
    ).astype(BF16)
    row = lax.broadcasted_iota(jnp.int32, (SPARE, length), 0)
    first = lax.broadcasted_iota(jnp.int32, (SPARE, length), 1) == 0
    zeros = jnp.zeros((SPARE, length), F32)
    for c in range(columns):
        plane = kernel_out[pl.ds(c, length, stride=columns), :].astype(BF16)
        chosen = ((row == c) & first).astype(F32).astype(BF16)
        zeros = zeros + lax.dot_general(
            chosen, plane, (((1,), (1,)), ((), ())), preferred_element_type=F32
        )
    packed_out[packed:] = zeros.astype(BF16)
    for copy in copies[1:]:
        copy.wait()


def call(body, outs, scratch=(), flops=0, name=None, in_specs=None):
    specs = {} if in_specs is None else {"in_specs": in_specs}
    return pl.pallas_call(
        body,
        **specs,
        out_shape=outs,
        scratch_shapes=list(scratch),
        cost_estimate=pl.CostEstimate(flops=flops, bytes_accessed=1 << 20, transcendentals=0),
        compiler_params=pltpu.CompilerParams(vmem_limit_bytes=VMEM_LIMIT),
        name=name,
    )


def per_device(orbitals, kernel):
    planes, length = orbitals.shape[1], orbitals.shape[2]
    groups = lax.axis_size("fft")
    columns = length // groups
    tables = jnp.asarray(np.stack(complex_tables(length, groups)))
    mirrors = jnp.asarray(mirror_tables(length))
    work = 8 * planes * length**3

    after = from_behind(orbitals[0], "band", -1)
    here = jax.ShapeDtypeStruct((length * columns, length), F32)
    own, here, tables, mirrors, packed = call(
        prepare,
        (
            jax.ShapeDtypeStruct(orbitals.shape[1:], BF16),
            here,
            jax.ShapeDtypeStruct(tables.shape, BF16),
            jax.ShapeDtypeStruct(mirrors.shape, BF16),
            jax.ShapeDtypeStruct((length // 2 * columns + SPARE, length), BF16),
        ),
        [pltpu.SemaphoreType.DMA((4,))],
        in_specs=[pl.BlockSpec(memory_space=pl.ANY)] * 4,
        name="prepare",
    )(*(pltpu.with_memory_space_constraint(array, pltpu.HBM) for array in (
        orbitals[0], kernel.reshape(here.shape), tables, mirrors
    )))
    bands = lax.axis_size("band")
    swap = [
        (b * groups + f, b * groups + (groups - 1 - f if b % 2 == 0 else -f % groups))
        for b in range(bands)
        for f in range(groups)
    ]
    there = lax.ppermute(packed, ("band", "fft"), swap)
    relayed = call(
        relay,
        jax.ShapeDtypeStruct(there.shape, BF16),
        flops=100 * 10**9,
        name="relay",
    )(there)
    twin = lax.ppermute(relayed, "band", [(b, b ^ 1) for b in range(bands)])

    lines = jax.ShapeDtypeStruct((groups, planes, 2 * columns, length), BF16)
    spectrum = call(planes_forward, lines, flops=0, name="planes_forward")(
        own, after, tables
    )
    spectrum = lax.all_to_all(spectrum, "fft", split_axis=0, concat_axis=0, tiled=True)
    screen = call(
        symmetric_kernel,
        jax.ShapeDtypeStruct((columns, length, length), F32),
        [pltpu.VMEM((length // 2 * columns, length), F32)] * 2
        + [pltpu.VMEM((SPARE, length), F32)],
        flops=work,
        name="symmetric_kernel",
    )(
        here, relayed, twin, mirrors
    )
    spectrum = call(
        columns_filter,
        jax.ShapeDtypeStruct((length, 2 * columns, length), BF16),
        [pltpu.VMEM((2 * length * columns, length), F32)] * 2,
        flops=2 * work,
        name="columns_filter",
    )(
        spectrum.reshape(length, 2 * columns, length),
        screen,
        tables,
    )
    spectrum = spectrum.reshape(groups, planes, 2 * columns, length)
    spectrum = lax.all_to_all(spectrum, "fft", split_axis=0, concat_axis=0, tiled=True)
    kept, sent = call(
        planes_back,
        (
            jax.ShapeDtypeStruct(own.shape, F32),
            jax.ShapeDtypeStruct(own.shape, BF16),
        ),
        flops=2 * work,
        name="planes_back",
    )(spectrum, own, after, tables)
    returned = from_behind(sent, "band", 1).astype(F32)
    return (kept + returned)[None]


def solution(mesh):
    in_specs = (P("band", "fft", None, None), P(None, "fft", None))
    out_specs = P("band", "fft", None, None)
    return jax.shard_map(
        per_device, mesh=mesh, in_specs=in_specs, out_specs=out_specs, check_vma=False
    )
```

time: 64.3 us -> 54.9 us (0.85)
  waiting for transfers between devices: 18.9 us -> 13.7 us
  local copies, waits for them, and re-layouts: 3.61 us -> 0 us
  starting transfers between devices: 24.7 us -> 21.9 us
  Pallas kernels: 3.29 us -> 5.05 us
    ppermute x2, waiting for transfers between devices: 6.62 us -> 1.32 us  [the longest x1 1.32 us: per_device(): twin = lax.ppermute(relayed, 'band', [(b, b ^ 1) for b in range(bands)])]
    all_to_all x1, waiting for transfers between devices: 0.01 us -> 4.84 us  [per_device(): lax.all_to_all(spectrum, 'fft', split_axis=0, concat_axis=0, tiled=True)]
    ppermute x2, waiting for transfers between devices: 12.2 us -> 7.54 us  [from_behind(): lax.ppermute(shard, axis, [(i, (i + by) % devices) for i in range(devices)])]
    unnamed x19 -> x0, local copies, waits for them, and re-layouts: 3.43 us -> none
    all_to_all x1, starting transfers between devices: 7.61 us -> 5.16 us  [per_device(): lax.all_to_all(spectrum, 'fft', split_axis=0, concat_axis=0, tiled=True)]
    pallas_call x1 -> x3, Pallas kernels: 1.42 us -> 2.84 us  [the longest x1 1.42 us: per_device(): call(planes_forward, lines, flops=0, name='planes_forward')]
  transfers between devices with their start and end apart: 5 -> 5, of which waited for: 4 -> 3; matrix products, arithmetic and copies ran while one was open for 0% -> 0% of each run, Pallas kernels for 1% -> 7%
where the time goes in v2:
time: 54.9 us; the launch traced here: 54.6 us
  starting transfers between devices  21.9 us (40%)
  waiting for transfers between devices  13.7 us (25%)
  blocking collectives  13 us (24%)
  Pallas kernels  5.05 us (9%)
  other arithmetic  0.85 us (2%)
    all_to_all x1, blocking collectives, per_device(): lax.all_to_all(spectrum, 'fft', split_axis=0, concat_axis=0, tiled=True)  13 us
    ppermute x2, starting transfers between devices, from_behind(): lax.ppermute(shard, axis, [(i, (i + by) % devices) for i in range(devices)])  8.95 us
    ppermute x2, waiting for transfers between devices, from_behind(): lax.ppermute(shard, axis, [(i, (i + by) % devices) for i in range(devices)])  7.54 us
    ppermute x1, starting transfers between devices, per_device(): there = lax.ppermute(packed, ('band', 'fft'), swap)  5.85 us
    all_to_all x1, starting transfers between devices, per_device(): lax.all_to_all(spectrum, 'fft', split_axis=0, concat_axis=0, tiled=True)  5.16 us
    all_to_all x1, waiting for transfers between devices, per_device(): lax.all_to_all(spectrum, 'fft', split_axis=0, concat_axis=0, tiled=True)  4.84 us
    ppermute x1, starting transfers between devices, per_device(): twin = lax.ppermute(relayed, 'band', [(b, b ^ 1) for b in range(bands)])  1.92 us
    pallas_call x1, Pallas kernels, per_device(): call(planes_forward, lines, flops=0, name='planes_forward')  1.42 us
  transfers between devices with their start and end apart: 5, of which 3 were waited for; matrix products, arithmetic and copies ran while one was open for 0% of the time, Pallas kernels for 7%

profile of v2, /device:TPU:2, one launch (start us, length us, event | category | flops | bytes accessed | tf_op | source)
XLA Modules:
  0.0 54.6 jit_solution(15445040622335049981)
XLA Ops:
  0.0 8.9 %collective-permute-start = (bf16[8,128,128]{2,1,0:T(8,128)(2,1)}, bf16[8,128,128]{2,1,0:T(8,128)(2,1)S(1)}, u32[]{:S(2)}, u32[]{:S(2)}) collective-permute-start(bf16[8,128,128]{2,1,0:T(8,128)(2,1)} %bitcast.9), channel_id=1, source_target_pairs={{0,496},{16,0},{32,16},{48,32},{64,48},{80,64},{96,80},{112,96},{1... | collective-permute-start | bytes 786440 | tf_op jit(solution)/shard_map/ppermute | solution.py:21
  8.9 1.4 %prepare.1 = (bf16[8,128,128]{2,1,0:T(8,128)(2,1)S(1)}, f32[1024,128]{1,0:T(8,128)S(1)}, bf16[6,256,256]{2,1,0:T(8,128)(2,1)S(1)}, bf16[4,128,128]{2,1,0:T(8,128)(2,1)S(1)}, bf16[528,128]{1,0:T(8,128)(2,1)S(1)}) custom-call(bf16[8,128,128]{2,1,0:T(8,128)(2,1)} %bitcast.10, f32[1024,128]{1,0:T(8,128)} %bitcast.8, ...), custom_call_target="tpu_custom_call" | custom-call | bytes 1048576 | tf_op jit(solution)/shard_map/prepare/pallas_call | solution.py:244
  10.4 5.8 %collective-permute-start.1 = (bf16[528,128]{1,0:T(8,128)(2,1)S(1)}, bf16[528,128]{1,0:T(8,128)(2,1)S(1)}, u32[]{:S(2)}, u32[]{:S(2)}) collective-permute-start(bf16[528,128]{1,0:T(8,128)(2,1)S(1)} %get-tuple-element.15), channel_id=1, source_target_pairs={{0,15},{1,14},{2,13},{3,12},{4,11},{5,10},{6,9},{7,8},{8,7},{9,6},... | collective-permute-start | bytes 405512 | tf_op jit(solution)/shard_map/ppermute | solution.py:265
  16.2 0.0 collective-permute-done.next_ref
  16.2 1.4 %planes_forward.1 = bf16[16,8,16,128]{3,2,1,0:T(8,128)(2,1)} custom-call(bf16[8,128,128]{2,1,0:T(8,128)(2,1)S(1)} %get-tuple-element.12.own_ref, bf16[8,128,128]{2,1,0:T(8,128)(2,1)S(1)} %collective-permute-done.next_ref, bf16[6,256,256]{2,1,0:T(8,128)(2,1)S(1)} %get-tuple-element.13.table_ref), custom_call_target="tpu_custom_call" | custom-call | bytes 1048576 | tf_op jit(solution)/shard_map/planes_forward/pallas_call | solution.py:275
  17.6 5.2 %all-to-all-start = ((bf16[16,8,16,128]{3,2,1,0:T(8,128)(2,1)}), bf16[16,8,16,128]{3,2,1,0:T(8,128)(2,1)S(1)}, u32[]{:S(2)}, u32[]{:S(2)}) async-start(bf16[16,8,16,128]{3,2,1,0:T(8,128)(2,1)} %planes_forward.1), calls=%async_computation | async-start | bytes 1048576 | tf_op jit(solution)/shard_map/all_to_all | solution.py:278
  22.8 0.0 collective-permute-done.1.there_ref
  22.8 1.9 %collective-permute-start.2 = (bf16[528,128]{1,0:T(8,128)(2,1)S(1)}, bf16[528,128]{1,0:T(8,128)(2,1)S(1)}, u32[]{:S(2)}, u32[]{:S(2)}) collective-permute-start(bf16[528,128]{1,0:T(8,128)(2,1)S(1)} %relay.1.first_ref), channel_id=1, source_target_pairs={{0,16},{16,0},{32,48},{48,32},{64,80},{80,64},{96,112},{112,96},{1... | collective-permute-start | bytes 405512 | tf_op jit(solution)/shard_map/ppermute | solution.py:272
  24.8 1.3 %collective-permute-done.2.second_ref = bf16[528,128]{1,0:T(8,128)(2,1)S(1)} collective-permute-done((bf16[528,128]{1,0:T(8,128)(2,1)S(1)}, bf16[528,128]{1,0:T(8,128)(2,1)S(1)}, u32[]{:S(2)}, u32[]{:S(2)}) %collective-permute-start.2) | collective-permute-done | bytes 135200 | tf_op jit(solution)/shard_map/ppermute | solution.py:272
  26.1 0.7 %symmetric_kernel.1.screen_ref = f32[8,128,128]{2,1,0:T(8,128)S(1)} custom-call(f32[1024,128]{1,0:T(8,128)S(1)} %get-tuple-element.14.here_ref, bf16[528,128]{1,0:T(8,128)(2,1)S(1)} %relay.1.first_ref, bf16[528,128]{1,0:T(8,128)(2,1)S(1)} %collective-permute-done.2.second_ref, bf16[4,128,128]{2,1,0:T(8,128)(2,1)S(1)} %get-tuple-element.16.mirror_ref), custom_call_target="tpu_custom_call" | custom-call | flops 134217728 | bytes 1048576 | tf_op jit(solution)/shard_map/symmetric_kernel/pallas_call | solution.py:279
  26.8 4.8 %all-to-all-done = bf16[16,8,16,128]{3,2,1,0:T(8,128)(2,1)S(1)} async-done(((bf16[16,8,16,128]{3,2,1,0:T(8,128)(2,1)}), bf16[16,8,16,128]{3,2,1,0:T(8,128)(2,1)S(1)}, u32[]{:S(2)}, u32[]{:S(2)}) %all-to-all-start) | async-done | bytes 524320 | tf_op jit(solution)/shard_map/all_to_all | solution.py:278
  31.7 0.9 %columns_filter.1 = bf16[128,16,128]{2,1,0:T(8,128)(2,1)S(1)} custom-call(bf16[128,16,128]{2,1,0:T(8,128)(2,1)S(1)} %bitcast.6, f32[8,128,128]{2,1,0:T(8,128)S(1)} %symmetric_kernel.1.screen_ref, bf16[6,256,256]{2,1,0:T(8,128)(2,1)S(1)} %get-tuple-element.13.table_ref), custom_call_target="tpu_custom_call" | custom-call | flops 268435456 | bytes 1048576 | tf_op jit(solution)/shard_map/columns_filter/pallas_call | solution.py:289
  32.6 13.0 %all_to_all.10.line_ref = bf16[16,8,16,128]{3,2,1,0:T(8,128)(2,1)S(1)} all-to-all(bf16[16,8,16,128]{3,2,1,0:T(8,128)(2,1)S(1)} %bitcast.7), channel_id=1, replica_groups=mesh['band'=32,'fft'=16] {'fft'}, dimensions={0} | all-to-all | bytes 1048576 | tf_op jit(solution)/shard_map/all_to_all | solution.py:301
  45.6 0.6 %planes_back.1 = (f32[8,128,128]{2,1,0:T(8,128)S(1)}, bf16[8,128,128]{2,1,0:T(8,128)(2,1)S(1)}) custom-call(bf16[16,8,16,128]{3,2,1,0:T(8,128)(2,1)S(1)} %all_to_all.10.line_ref, bf16[8,128,128]{2,1,0:T(8,128)(2,1)S(1)} %get-tuple-element.12.own_ref, bf16[8,128,128]{2,1,0:T(8,128)(2,1)S(1)} %collective-permute-done.next_ref, ...), custom_call_target="tpu_custom_call" | custom-call | flops 268435456 | bytes 1048576 | tf_op jit(solution)/shard_map/planes_back/pallas_call | solution.py:302
  46.2 0.0 collective-permute-start.3
  46.2 7.5 %collective-permute-done.3 = bf16[8,128,128]{2,1,0:T(8,128)(2,1)S(1)} collective-permute-done((bf16[8,128,128]{2,1,0:T(8,128)(2,1)S(1)}, bf16[8,128,128]{2,1,0:T(8,128)(2,1)S(1)}, u32[]{:S(2)}, u32[]{:S(2)}) %collective-permute-start.3) | collective-permute-done | bytes 262176 | tf_op jit(solution)/shard_map/ppermute | solution.py:21
  53.7 0.9 %add_bitcast_fusion = f32[1,8,128,128]{3,2,1,0:T(8,128)} fusion(f32[8,128,128]{2,1,0:T(8,128)S(1)} %get-tuple-element.17, bf16[8,128,128]{2,1,0:T(8,128)(2,1)S(1)} %collective-permute-done.3), kind=kLoop, calls=%fused_computation | loop fusion | flops 262144 | bytes 1310720 | tf_op jit(solution)/shard_map/broadcast_in_dim | solution.py:312
  (1 shorter events, 0.0 us)
Async XLA Ops:
  0.0 16.2 %collective-permute-start = (bf16[8,128,128]{2,1,0:T(8,128)(2,1)}, bf16[8,128,128]{2,1,0:T(8,128)(2,1)S(1)}, u32[]{:S(2)}, u32[]{:S(2)}) collective-permute-start(bf16[8,128,128]{2,1,0:T(8,128)(2,1)} %bitcast.9), channel_id=1, source_target_pairs={{0,496},{16,0},{32,16},{48,32},{64,48},{80,64},{96,80},{112,96},{1... | collective-permute-start | bytes 786440 | tf_op jit(solution)/shard_map/ppermute | solution.py:21
  10.4 12.5 %collective-permute-start.1 = (bf16[528,128]{1,0:T(8,128)(2,1)S(1)}, bf16[528,128]{1,0:T(8,128)(2,1)S(1)}, u32[]{:S(2)}, u32[]{:S(2)}) collective-permute-start(bf16[528,128]{1,0:T(8,128)(2,1)S(1)} %get-tuple-element.15), channel_id=1, source_target_pairs={{0,15},{1,14},{2,13},{3,12},{4,11},{5,10},{6,9},{7,8},{8,7},{9,6},... | collective-permute-start | bytes 405512 | tf_op jit(solution)/shard_map/ppermute | solution.py:265
  17.6 14.0 %all-to-all-start = ((bf16[16,8,16,128]{3,2,1,0:T(8,128)(2,1)}), bf16[16,8,16,128]{3,2,1,0:T(8,128)(2,1)S(1)}, u32[]{:S(2)}, u32[]{:S(2)}) async-start(bf16[16,8,16,128]{3,2,1,0:T(8,128)(2,1)} %planes_forward.1), calls=%async_computation | async-start | bytes 1048576 | tf_op jit(solution)/shard_map/all_to_all | solution.py:278
  22.8 3.2 %collective-permute-start.2 = (bf16[528,128]{1,0:T(8,128)(2,1)S(1)}, bf16[528,128]{1,0:T(8,128)(2,1)S(1)}, u32[]{:S(2)}, u32[]{:S(2)}) collective-permute-start(bf16[528,128]{1,0:T(8,128)(2,1)S(1)} %relay.1.first_ref), channel_id=1, source_target_pairs={{0,16},{16,0},{32,48},{48,32},{64,80},{80,64},{96,112},{112,96},{1... | collective-permute-start | bytes 405512 | tf_op jit(solution)/shard_map/ppermute | solution.py:272
  46.2 7.6 %collective-permute-start.3 = (bf16[8,128,128]{2,1,0:T(8,128)(2,1)S(1)}, bf16[8,128,128]{2,1,0:T(8,128)(2,1)S(1)}, u32[]{:S(2)}, u32[]{:S(2)}) collective-permute-start(bf16[8,128,128]{2,1,0:T(8,128)(2,1)S(1)} %get-tuple-element.18), channel_id=1, source_target_pairs={{0,16},{16,32},{32,48},{48,64},{64,80},{80,96},{96,112},{112,128},... | collective-permute-start | bytes 786440 | tf_op jit(solution)/shard_map/ppermute | solution.py:21

commit v3 on v2

--- a/solution.py
+++ b/solution.py
@@ -69,13 +69,14 @@
     return jnp.dot(left, right, preferred_element_type=F32)
 
 
-def planes_forward(own_ref, next_ref, table_ref, out_ref):
+def planes_forward(own_ref, other_ref, table_ref, out_ref, held, sems):
     planes, length = own_ref.shape[0], own_ref.shape[1]
     groups = out_ref.shape[0]
+    copies = []
     for x in range(0, planes, 2):
         own = own_ref[x : x + 2].astype(F32).reshape(2 * length, length)
-        after = next_ref[x : x + 2].astype(F32).reshape(2 * length, length)
-        field = jnp.concatenate([(own * own).astype(BF16), (own * after).astype(BF16)], axis=1)
+        other = other_ref[x : x + 2].astype(F32).reshape(2 * length, length)
+        field = jnp.concatenate([(own * own).astype(BF16), (own * other).astype(BF16)], axis=1)
         field = dot(field, table_ref[ZED]).astype(BF16)
         field = jnp.concatenate(
             [
@@ -85,8 +86,14 @@
             axis=0,
         )
         field = dot(table_ref[AHEAD_SORTED], field).astype(BF16)
-        out_ref[:, x] = field[:, :length].reshape(groups, -1, length)
-        out_ref[:, x + 1] = field[:, length:].reshape(groups, -1, length)
+        held[:, x] = field[:, :length].reshape(groups, -1, length)
+        held[:, x + 1] = field[:, length:].reshape(groups, -1, length)
+        copies.append(
+            pltpu.make_async_copy(held.at[:, x : x + 2], out_ref.at[:, x : x + 2], sems.at[x // 2])
+        )
+        copies[-1].start()
+    for copy in copies:
+        copy.wait()
 
 
 def columns_filter(line_ref, screen_ref, table_ref, out_ref, held, sent):
@@ -120,7 +127,7 @@
     out_ref[...] = sent[...].reshape(length, rows, length).astype(BF16)
 
 
-def planes_back(line_ref, own_ref, next_ref, table_ref, kept_ref, sent_ref):
+def planes_back(line_ref, own_ref, other_ref, table_ref, kept_ref, sent_ref):
     planes, length = own_ref.shape[0], own_ref.shape[1]
     for x in range(0, planes, 2):
         field = jnp.concatenate(
@@ -136,8 +143,8 @@
         )
         field = dot(field, table_ref[DEZ])
         own = own_ref[x : x + 2].astype(F32).reshape(2 * length, length)
-        after = next_ref[x : x + 2].astype(F32).reshape(2 * length, length)
-        kept = field[:, :length] * own + field[:, length:] * after
+        other = other_ref[x : x + 2].astype(F32).reshape(2 * length, length)
+        kept = field[:, :length] * own + field[:, length:] * other
         sent = (field[:, length:] * own).astype(BF16)
         kept_ref[x : x + 2] = kept.reshape(2, length, length)
         sent_ref[x : x + 2] = sent.reshape(2, length, length)
@@ -218,8 +225,20 @@
         copy.wait()
 
 
-def call(body, outs, scratch=(), flops=0, name=None, in_specs=None):
-    specs = {} if in_specs is None else {"in_specs": in_specs}
+def finish(kept_ref, returned_ref, out_ref, held, sems):
+    copies = []
+    for i in range(sems.shape[0]):
+        part = pl.ds(i * (held.shape[0] // sems.shape[0]), held.shape[0] // sems.shape[0])
+        held[part] = kept_ref[part] + returned_ref[part].astype(F32)
+        copies.append(pltpu.make_async_copy(held.at[part], out_ref.at[part], sems.at[i]))
+        copies[-1].start()
+    for copy in copies:
+        copy.wait()
+
+
+def call(body, outs, scratch=(), flops=0, name=None, in_specs=None, out_specs=None):
+    specs = {"in_specs": in_specs, "out_specs": out_specs}
+    specs = {key: value for key, value in specs.items() if value is not None}
     return pl.pallas_call(
         body,
         **specs,
@@ -239,7 +258,7 @@
     mirrors = jnp.asarray(mirror_tables(length))
     work = 8 * planes * length**3
 
-    after = from_behind(orbitals[0], "band", -1)
+    other = from_behind(orbitals[0], "band", 1)
     here = jax.ShapeDtypeStruct((length * columns, length), F32)
     own, here, tables, mirrors, packed = call(
         prepare,
@@ -272,8 +291,14 @@
     twin = lax.ppermute(relayed, "band", [(b, b ^ 1) for b in range(bands)])
 
     lines = jax.ShapeDtypeStruct((groups, planes, 2 * columns, length), BF16)
-    spectrum = call(planes_forward, lines, flops=0, name="planes_forward")(
-        own, after, tables
+    spectrum = call(
+        planes_forward,
+        pltpu.HBM(lines.shape, lines.dtype),
+        [pltpu.VMEM(lines.shape, BF16), pltpu.SemaphoreType.DMA((planes // 2,))],
+        out_specs=pl.BlockSpec(memory_space=pl.ANY),
+        name="planes_forward",
+    )(
+        own, other, tables
     )
     spectrum = lax.all_to_all(spectrum, "fft", split_axis=0, concat_axis=0, tiled=True)
     screen = call(
@@ -307,9 +332,16 @@
         ),
         flops=2 * work,
         name="planes_back",
-    )(spectrum, own, after, tables)
-    returned = from_behind(sent, "band", 1).astype(F32)
-    return (kept + returned)[None]
+    )(spectrum, own, other, tables)
+    returned = from_behind(sent, "band", -1)
+    total = call(
+        finish,
+        jax.ShapeDtypeStruct(kept.shape, F32),
+        [pltpu.VMEM(kept.shape, F32), pltpu.SemaphoreType.DMA((4,))],
+        out_specs=pl.BlockSpec(memory_space=pl.ANY),
+        name="finish",
+    )(kept, returned)
+    return total[None]
 
 
 def solution(mesh):

time: 54.9 us -> 51.2 us (0.933)
  the two profiles are of different devices: /device:TPU:2 before, /device:TPU:193 now
where the time goes in v3:
time: 51.2 us; the launch traced here: 50.9 us
  waiting for transfers between devices  16.6 us (32%)
  starting transfers between devices  15 us (29%)
  blocking collectives  13.4 us (26%)
  Pallas kernels  5.79 us (11%)
    all_to_all x1, blocking collectives, per_device(): lax.all_to_all(spectrum, 'fft', split_axis=0, concat_axis=0, tiled=True)  13.4 us
    ppermute x2, waiting for transfers between devices, from_behind(): lax.ppermute(shard, axis, [(i, (i + by) % devices) for i in range(devices)])  9.23 us
    all_to_all x1, starting transfers between devices, per_device(): lax.all_to_all(spectrum, 'fft', split_axis=0, concat_axis=0, tiled=True)  7.23 us
    all_to_all x1, waiting for transfers between devices, per_device(): lax.all_to_all(spectrum, 'fft', split_axis=0, concat_axis=0, tiled=True)  6.36 us
    ppermute x2, starting transfers between devices, from_behind(): lax.ppermute(shard, axis, [(i, (i + by) % devices) for i in range(devices)])  4.56 us
    ppermute x1, starting transfers between devices, per_device(): twin = lax.ppermute(relayed, 'band', [(b, b ^ 1) for b in range(bands)])  2.58 us
    pallas_call x1, Pallas kernels, per_device(): call(prepare, (jax.ShapeDtypeStruct(orbitals.shape[1:], BF16), here, jax....  1.41 us
    pallas_call x1, Pallas kernels, per_device(): call(planes_forward, pltpu.HBM(lines.shape, lines.dtype), [pltpu.VMEM(lin...  1.31 us
  transfers between devices with their start and end apart: 5, of which 4 were waited for; matrix products, arithmetic and copies ran while one was open for 0% of the time, Pallas kernels for 7%

profile of v3, /device:TPU:193, one launch (start us, length us, event | category | flops | bytes accessed | tf_op | source)
XLA Modules:
  0.0 50.9 jit_solution(9524427689956093566)
XLA Ops:
  0.0 2.2 %collective-permute-start = (bf16[8,128,128]{2,1,0:T(8,128)(2,1)}, bf16[8,128,128]{2,1,0:T(8,128)(2,1)S(1)}, u32[]{:S(2)}, u32[]{:S(2)}) collective-permute-start(bf16[8,128,128]{2,1,0:T(8,128)(2,1)} %bitcast.8), channel_id=1, source_target_pairs={{0,16},{16,32},{32,48},{48,64},{64,80},{80,96},{96,112},{112,128},... | collective-permute-start | bytes 786440 | tf_op jit(solution)/shard_map/ppermute | solution.py:21
  2.2 1.4 %prepare.1 = (bf16[8,128,128]{2,1,0:T(8,128)(2,1)S(1)}, f32[1024,128]{1,0:T(8,128)S(1)}, bf16[6,256,256]{2,1,0:T(8,128)(2,1)S(1)}, bf16[4,128,128]{2,1,0:T(8,128)(2,1)S(1)}, bf16[528,128]{1,0:T(8,128)(2,1)S(1)}) custom-call(bf16[8,128,128]{2,1,0:T(8,128)(2,1)} %bitcast.9, f32[1024,128]{1,0:T(8,128)} %bitcast.7, ...), custom_call_target="tpu_custom_call" | custom-call | bytes 1048576 | tf_op jit(solution)/shard_map/prepare/pallas_call | solution.py:263
  3.6 0.7 %collective-permute-start.1 = (bf16[528,128]{1,0:T(8,128)(2,1)S(1)}, bf16[528,128]{1,0:T(8,128)(2,1)S(1)}, u32[]{:S(2)}, u32[]{:S(2)}) collective-permute-start(bf16[528,128]{1,0:T(8,128)(2,1)S(1)} %get-tuple-element.15), channel_id=1, source_target_pairs={{0,15},{1,14},{2,13},{3,12},{4,11},{5,10},{6,9},{7,8},{8,7},{9,6},... | collective-permute-start | bytes 405512 | tf_op jit(solution)/shard_map/ppermute | solution.py:284
  4.3 1.5 %collective-permute-done.other_ref = bf16[8,128,128]{2,1,0:T(8,128)(2,1)S(1)} collective-permute-done((bf16[8,128,128]{2,1,0:T(8,128)(2,1)}, bf16[8,128,128]{2,1,0:T(8,128)(2,1)S(1)}, u32[]{:S(2)}, u32[]{:S(2)}) %collective-permute-start) | collective-permute-done | bytes 262176 | tf_op jit(solution)/shard_map/ppermute | solution.py:21
  5.8 1.3 %planes_forward.1 = bf16[16,8,16,128]{3,2,1,0:T(8,128)(2,1)} custom-call(bf16[8,128,128]{2,1,0:T(8,128)(2,1)S(1)} %get-tuple-element.12.own_ref, bf16[8,128,128]{2,1,0:T(8,128)(2,1)S(1)} %collective-permute-done.other_ref, bf16[6,256,256]{2,1,0:T(8,128)(2,1)S(1)} %get-tuple-element.13.table_ref), custom_call_target="tpu_custom_call" | custom-call | bytes 1048576 | tf_op jit(solution)/shard_map/planes_forward/pallas_call | solution.py:294
  7.2 7.2 %all-to-all-start = ((bf16[16,8,16,128]{3,2,1,0:T(8,128)(2,1)}), bf16[16,8,16,128]{3,2,1,0:T(8,128)(2,1)S(1)}, u32[]{:S(2)}, u32[]{:S(2)}) async-start(bf16[16,8,16,128]{3,2,1,0:T(8,128)(2,1)} %planes_forward.1), calls=%async_computation | async-start | bytes 1048576 | tf_op jit(solution)/shard_map/all_to_all | solution.py:303
  14.4 0.0 collective-permute-done.1.there_ref
  14.4 2.6 %collective-permute-start.2 = (bf16[528,128]{1,0:T(8,128)(2,1)S(1)}, bf16[528,128]{1,0:T(8,128)(2,1)S(1)}, u32[]{:S(2)}, u32[]{:S(2)}) collective-permute-start(bf16[528,128]{1,0:T(8,128)(2,1)S(1)} %relay.1.first_ref), channel_id=1, source_target_pairs={{0,16},{16,0},{32,48},{48,32},{64,80},{80,64},{96,112},{112,96},{1... | collective-permute-start | bytes 405512 | tf_op jit(solution)/shard_map/ppermute | solution.py:291
  17.0 1.0 %collective-permute-done.2.second_ref = bf16[528,128]{1,0:T(8,128)(2,1)S(1)} collective-permute-done((bf16[528,128]{1,0:T(8,128)(2,1)S(1)}, bf16[528,128]{1,0:T(8,128)(2,1)S(1)}, u32[]{:S(2)}, u32[]{:S(2)}) %collective-permute-start.2) | collective-permute-done | bytes 135200 | tf_op jit(solution)/shard_map/ppermute | solution.py:291
  18.0 0.7 %symmetric_kernel.1.screen_ref = f32[8,128,128]{2,1,0:T(8,128)S(1)} custom-call(f32[1024,128]{1,0:T(8,128)S(1)} %get-tuple-element.14.here_ref, bf16[528,128]{1,0:T(8,128)(2,1)S(1)} %relay.1.first_ref, bf16[528,128]{1,0:T(8,128)(2,1)S(1)} %collective-permute-done.2.second_ref, bf16[4,128,128]{2,1,0:T(8,128)(2,1)S(1)} %get-tuple-element.16.mirror_ref), custom_call_target="tpu_custom_call" | custom-call | flops 134217728 | bytes 1048576 | tf_op jit(solution)/shard_map/symmetric_kernel/pallas_call | solution.py:304
  18.7 6.4 %all-to-all-done = bf16[16,8,16,128]{3,2,1,0:T(8,128)(2,1)S(1)} async-done(((bf16[16,8,16,128]{3,2,1,0:T(8,128)(2,1)}), bf16[16,8,16,128]{3,2,1,0:T(8,128)(2,1)S(1)}, u32[]{:S(2)}, u32[]{:S(2)}) %all-to-all-start) | async-done | bytes 524320 | tf_op jit(solution)/shard_map/all_to_all | solution.py:303
  25.1 0.9 %columns_filter.1 = bf16[128,16,128]{2,1,0:T(8,128)(2,1)S(1)} custom-call(bf16[128,16,128]{2,1,0:T(8,128)(2,1)S(1)} %bitcast.5, f32[8,128,128]{2,1,0:T(8,128)S(1)} %symmetric_kernel.1.screen_ref, bf16[6,256,256]{2,1,0:T(8,128)(2,1)S(1)} %get-tuple-element.13.table_ref), custom_call_target="tpu_custom_call" | custom-call | flops 268435456 | bytes 1048576 | tf_op jit(solution)/shard_map/columns_filter/pallas_call | solution.py:314
  26.0 13.4 %all_to_all.10.line_ref = bf16[16,8,16,128]{3,2,1,0:T(8,128)(2,1)S(1)} all-to-all(bf16[16,8,16,128]{3,2,1,0:T(8,128)(2,1)S(1)} %bitcast.6), channel_id=1, replica_groups=mesh['band'=32,'fft'=16] {'fft'}, dimensions={0} | all-to-all | bytes 1048576 | tf_op jit(solution)/shard_map/all_to_all | solution.py:326
  39.4 0.6 %planes_back.1 = (f32[8,128,128]{2,1,0:T(8,128)S(1)}, bf16[8,128,128]{2,1,0:T(8,128)(2,1)S(1)}) custom-call(bf16[16,8,16,128]{3,2,1,0:T(8,128)(2,1)S(1)} %all_to_all.10.line_ref, bf16[8,128,128]{2,1,0:T(8,128)(2,1)S(1)} %get-tuple-element.12.own_ref, bf16[8,128,128]{2,1,0:T(8,128)(2,1)S(1)} %collective-permute-done.other_ref, ...), custom_call_target="tpu_custom_call" | custom-call | flops 268435456 | bytes 1048576 | tf_op jit(solution)/shard_map/planes_back/pallas_call | solution.py:327
  40.0 2.4 %collective-permute-start.3 = (bf16[8,128,128]{2,1,0:T(8,128)(2,1)S(1)}, bf16[8,128,128]{2,1,0:T(8,128)(2,1)S(1)}, u32[]{:S(2)}, u32[]{:S(2)}) collective-permute-start(bf16[8,128,128]{2,1,0:T(8,128)(2,1)S(1)} %get-tuple-element.18), channel_id=1, source_target_pairs={{0,496},{16,0},{32,16},{48,32},{64,48},{80,64},{96,80},{112,96},{1... | collective-permute-start | bytes 786440 | tf_op jit(solution)/shard_map/ppermute | solution.py:21
  42.4 7.7 %collective-permute-done.3.returned_ref = bf16[8,128,128]{2,1,0:T(8,128)(2,1)S(1)} collective-permute-done((bf16[8,128,128]{2,1,0:T(8,128)(2,1)S(1)}, bf16[8,128,128]{2,1,0:T(8,128)(2,1)S(1)}, u32[]{:S(2)}, u32[]{:S(2)}) %collective-permute-start.3) | collective-permute-done | bytes 262176 | tf_op jit(solution)/shard_map/ppermute | solution.py:21
  50.1 0.8 %finish.1 = f32[8,128,128]{2,1,0:T(8,128)} custom-call(f32[8,128,128]{2,1,0:T(8,128)S(1)} %get-tuple-element.17.kept_ref, bf16[8,128,128]{2,1,0:T(8,128)(2,1)S(1)} %collective-permute-done.3.returned_ref), custom_call_target="tpu_custom_call" | custom-call | bytes 1048576 | tf_op jit(solution)/shard_map/finish/pallas_call | solution.py:337
  (1 shorter events, 0.0 us)
Async XLA Ops:
  0.0 5.8 %collective-permute-start = (bf16[8,128,128]{2,1,0:T(8,128)(2,1)}, bf16[8,128,128]{2,1,0:T(8,128)(2,1)S(1)}, u32[]{:S(2)}, u32[]{:S(2)}) collective-permute-start(bf16[8,128,128]{2,1,0:T(8,128)(2,1)} %bitcast.8), channel_id=1, source_target_pairs={{0,16},{16,32},{32,48},{48,64},{64,80},{80,96},{96,112},{112,128},... | collective-permute-start | bytes 786440 | tf_op jit(solution)/shard_map/ppermute | solution.py:21
  3.6 10.8 %collective-permute-start.1 = (bf16[528,128]{1,0:T(8,128)(2,1)S(1)}, bf16[528,128]{1,0:T(8,128)(2,1)S(1)}, u32[]{:S(2)}, u32[]{:S(2)}) collective-permute-start(bf16[528,128]{1,0:T(8,128)(2,1)S(1)} %get-tuple-element.15), channel_id=1, source_target_pairs={{0,15},{1,14},{2,13},{3,12},{4,11},{5,10},{6,9},{7,8},{8,7},{9,6},... | collective-permute-start | bytes 405512 | tf_op jit(solution)/shard_map/ppermute | solution.py:284
  7.2 17.9 %all-to-all-start = ((bf16[16,8,16,128]{3,2,1,0:T(8,128)(2,1)}), bf16[16,8,16,128]{3,2,1,0:T(8,128)(2,1)S(1)}, u32[]{:S(2)}, u32[]{:S(2)}) async-start(bf16[16,8,16,128]{3,2,1,0:T(8,128)(2,1)} %planes_forward.1), calls=%async_computation | async-start | bytes 1048576 | tf_op jit(solution)/shard_map/all_to_all | solution.py:303
  14.4 3.6 %collective-permute-start.2 = (bf16[528,128]{1,0:T(8,128)(2,1)S(1)}, bf16[528,128]{1,0:T(8,128)(2,1)S(1)}, u32[]{:S(2)}, u32[]{:S(2)}) collective-permute-start(bf16[528,128]{1,0:T(8,128)(2,1)S(1)} %relay.1.first_ref), channel_id=1, source_target_pairs={{0,16},{16,0},{32,48},{48,32},{64,80},{80,64},{96,112},{112,96},{1... | collective-permute-start | bytes 405512 | tf_op jit(solution)/shard_map/ppermute | solution.py:291
  40.0 10.1 %collective-permute-start.3 = (bf16[8,128,128]{2,1,0:T(8,128)(2,1)S(1)}, bf16[8,128,128]{2,1,0:T(8,128)(2,1)S(1)}, u32[]{:S(2)}, u32[]{:S(2)}) collective-permute-start(bf16[8,128,128]{2,1,0:T(8,128)(2,1)S(1)} %get-tuple-element.18), channel_id=1, source_target_pairs={{0,496},{16,0},{32,16},{48,32},{64,48},{80,64},{96,80},{112,96},{1... | collective-permute-start | bytes 786440 | tf_op jit(solution)/shard_map/ppermute | solution.py:21

commit v4 on v3

--- a/solution.py
+++ b/solution.py
@@ -96,35 +96,25 @@
         copy.wait()
 
 
-def columns_filter(line_ref, screen_ref, table_ref, out_ref, held, sent):
+def columns_filter(line_ref, screen_ref, table_ref, out_ref, sent):
     length = line_ref.shape[0]
-    rows = line_ref.shape[1]
-    columns = rows // 2
-    held[...] = line_ref[...].astype(F32).reshape(length * rows, length)
+    columns = line_ref.shape[1] // 2
+    lines = jnp.swapaxes(line_ref[...], 0, 1)
     for c in range(0, columns, 2):
+        rows = [[part * columns + c + j for j in range(2)] for part in range(2)]
         field = jnp.concatenate(
-            [
-                jnp.concatenate(
-                    [
-                        held[pl.ds(part * columns + c + j, length, stride=rows), :]
-                        for j in range(2)
-                    ],
-                    axis=1,
-                )
-                for part in range(2)
-            ],
-            axis=0,
-        ).astype(BF16)
+            [jnp.concatenate([lines[row] for row in pair], axis=1) for pair in rows], axis=0
+        )
         field = dot(table_ref[AHEAD], field)
         screen = jnp.concatenate([screen_ref[c], screen_ref[c + 1]], axis=1)
         field = jnp.concatenate([field[:length] * screen, field[length:] * screen], axis=0)
-        field = dot(table_ref[BACK], field.astype(BF16))
+        field = dot(table_ref[BACK], field.astype(BF16)).astype(BF16)
         for part in range(2):
             for j in range(2):
-                sent[pl.ds(part * columns + c + j, length, stride=rows), :] = field[
+                sent[rows[part][j]] = field[
                     part * length : (part + 1) * length, j * length : (j + 1) * length
                 ]
-    out_ref[...] = sent[...].reshape(length, rows, length).astype(BF16)
+    out_ref[...] = jnp.swapaxes(sent[...], 0, 1)
 
 
 def planes_back(line_ref, own_ref, other_ref, table_ref, kept_ref, sent_ref):
@@ -314,7 +304,7 @@
     spectrum = call(
         columns_filter,
         jax.ShapeDtypeStruct((length, 2 * columns, length), BF16),
-        [pltpu.VMEM((2 * length * columns, length), F32)] * 2,
+        [pltpu.VMEM((2 * columns, length, length), BF16)],
         flops=2 * work,
         name="columns_filter",
     )(

time: 51.2 us -> 50.9 us (level)
  no operation moved by 1% of the time
where the time goes in v4:
time: 50.9 us; the launch traced here: 50.6 us
  waiting for transfers between devices  16.6 us (33%)
  starting transfers between devices  15 us (29%)
  blocking collectives  13.4 us (26%)
  Pallas kernels  5.49 us (11%)
    all_to_all x1, blocking collectives, per_device(): lax.all_to_all(spectrum, 'fft', split_axis=0, concat_axis=0, tiled=True)  13.4 us
    ppermute x2, waiting for transfers between devices, from_behind(): lax.ppermute(shard, axis, [(i, (i + by) % devices) for i in range(devices)])  9.23 us
    all_to_all x1, starting transfers between devices, per_device(): lax.all_to_all(spectrum, 'fft', split_axis=0, concat_axis=0, tiled=True)  7.23 us
    all_to_all x1, waiting for transfers between devices, per_device(): lax.all_to_all(spectrum, 'fft', split_axis=0, concat_axis=0, tiled=True)  6.36 us
    ppermute x2, starting transfers between devices, from_behind(): lax.ppermute(shard, axis, [(i, (i + by) % devices) for i in range(devices)])  4.56 us
    ppermute x1, starting transfers between devices, per_device(): twin = lax.ppermute(relayed, 'band', [(b, b ^ 1) for b in range(bands)])  2.58 us
    pallas_call x1, Pallas kernels, per_device(): call(prepare, (jax.ShapeDtypeStruct(orbitals.shape[1:], BF16), here, jax....  1.41 us
    pallas_call x1, Pallas kernels, per_device(): call(planes_forward, pltpu.HBM(lines.shape, lines.dtype), [pltpu.VMEM(lin...  1.31 us
  transfers between devices with their start and end apart: 5, of which 4 were waited for; matrix products, arithmetic and copies ran while one was open for 0% of the time, Pallas kernels for 7%

profile of v4, /device:TPU:193, one launch (start us, length us, event | category | flops | bytes accessed | tf_op | source)
XLA Modules:
  0.0 50.6 jit_solution(12765750811632707842)
XLA Ops:
  0.0 2.2 %collective-permute-start = (bf16[8,128,128]{2,1,0:T(8,128)(2,1)}, bf16[8,128,128]{2,1,0:T(8,128)(2,1)S(1)}, u32[]{:S(2)}, u32[]{:S(2)}) collective-permute-start(bf16[8,128,128]{2,1,0:T(8,128)(2,1)} %bitcast.8), channel_id=1, source_target_pairs={{0,16},{16,32},{32,48},{48,64},{64,80},{80,96},{96,112},{112,128},... | collective-permute-start | bytes 786440 | tf_op jit(solution)/shard_map/ppermute | solution.py:21
  2.2 1.4 %prepare.1 = (bf16[8,128,128]{2,1,0:T(8,128)(2,1)S(1)}, f32[1024,128]{1,0:T(8,128)S(1)}, bf16[6,256,256]{2,1,0:T(8,128)(2,1)S(1)}, bf16[4,128,128]{2,1,0:T(8,128)(2,1)S(1)}, bf16[528,128]{1,0:T(8,128)(2,1)S(1)}) custom-call(bf16[8,128,128]{2,1,0:T(8,128)(2,1)} %bitcast.9, f32[1024,128]{1,0:T(8,128)} %bitcast.7, ...), custom_call_target="tpu_custom_call" | custom-call | bytes 1048576 | tf_op jit(solution)/shard_map/prepare/pallas_call | solution.py:253
  3.6 0.7 %collective-permute-start.1 = (bf16[528,128]{1,0:T(8,128)(2,1)S(1)}, bf16[528,128]{1,0:T(8,128)(2,1)S(1)}, u32[]{:S(2)}, u32[]{:S(2)}) collective-permute-start(bf16[528,128]{1,0:T(8,128)(2,1)S(1)} %get-tuple-element.15), channel_id=1, source_target_pairs={{0,15},{1,14},{2,13},{3,12},{4,11},{5,10},{6,9},{7,8},{8,7},{9,6},... | collective-permute-start | bytes 405512 | tf_op jit(solution)/shard_map/ppermute | solution.py:274
  4.3 1.5 %collective-permute-done.other_ref = bf16[8,128,128]{2,1,0:T(8,128)(2,1)S(1)} collective-permute-done((bf16[8,128,128]{2,1,0:T(8,128)(2,1)}, bf16[8,128,128]{2,1,0:T(8,128)(2,1)S(1)}, u32[]{:S(2)}, u32[]{:S(2)}) %collective-permute-start) | collective-permute-done | bytes 262176 | tf_op jit(solution)/shard_map/ppermute | solution.py:21
  5.8 1.3 %planes_forward.1 = bf16[16,8,16,128]{3,2,1,0:T(8,128)(2,1)} custom-call(bf16[8,128,128]{2,1,0:T(8,128)(2,1)S(1)} %get-tuple-element.12.own_ref, bf16[8,128,128]{2,1,0:T(8,128)(2,1)S(1)} %collective-permute-done.other_ref, bf16[6,256,256]{2,1,0:T(8,128)(2,1)S(1)} %get-tuple-element.13.table_ref), custom_call_target="tpu_custom_call" | custom-call | bytes 1048576 | tf_op jit(solution)/shard_map/planes_forward/pallas_call | solution.py:284
  7.2 7.2 %all-to-all-start = ((bf16[16,8,16,128]{3,2,1,0:T(8,128)(2,1)}), bf16[16,8,16,128]{3,2,1,0:T(8,128)(2,1)S(1)}, u32[]{:S(2)}, u32[]{:S(2)}) async-start(bf16[16,8,16,128]{3,2,1,0:T(8,128)(2,1)} %planes_forward.1), calls=%async_computation | async-start | bytes 1048576 | tf_op jit(solution)/shard_map/all_to_all | solution.py:293
  14.4 0.0 collective-permute-done.1.there_ref
  14.4 2.6 %collective-permute-start.2 = (bf16[528,128]{1,0:T(8,128)(2,1)S(1)}, bf16[528,128]{1,0:T(8,128)(2,1)S(1)}, u32[]{:S(2)}, u32[]{:S(2)}) collective-permute-start(bf16[528,128]{1,0:T(8,128)(2,1)S(1)} %relay.1.first_ref), channel_id=1, source_target_pairs={{0,16},{16,0},{32,48},{48,32},{64,80},{80,64},{96,112},{112,96},{1... | collective-permute-start | bytes 405512 | tf_op jit(solution)/shard_map/ppermute | solution.py:281
  17.0 1.0 %collective-permute-done.2.second_ref = bf16[528,128]{1,0:T(8,128)(2,1)S(1)} collective-permute-done((bf16[528,128]{1,0:T(8,128)(2,1)S(1)}, bf16[528,128]{1,0:T(8,128)(2,1)S(1)}, u32[]{:S(2)}, u32[]{:S(2)}) %collective-permute-start.2) | collective-permute-done | bytes 135200 | tf_op jit(solution)/shard_map/ppermute | solution.py:281
  18.0 0.7 %symmetric_kernel.1.screen_ref = f32[8,128,128]{2,1,0:T(8,128)S(1)} custom-call(f32[1024,128]{1,0:T(8,128)S(1)} %get-tuple-element.14.here_ref, bf16[528,128]{1,0:T(8,128)(2,1)S(1)} %relay.1.first_ref, bf16[528,128]{1,0:T(8,128)(2,1)S(1)} %collective-permute-done.2.second_ref, bf16[4,128,128]{2,1,0:T(8,128)(2,1)S(1)} %get-tuple-element.16.mirror_ref), custom_call_target="tpu_custom_call" | custom-call | flops 134217728 | bytes 1048576 | tf_op jit(solution)/shard_map/symmetric_kernel/pallas_call | solution.py:294
  18.7 6.4 %all-to-all-done = bf16[16,8,16,128]{3,2,1,0:T(8,128)(2,1)S(1)} async-done(((bf16[16,8,16,128]{3,2,1,0:T(8,128)(2,1)}), bf16[16,8,16,128]{3,2,1,0:T(8,128)(2,1)S(1)}, u32[]{:S(2)}, u32[]{:S(2)}) %all-to-all-start) | async-done | bytes 524320 | tf_op jit(solution)/shard_map/all_to_all | solution.py:293
  25.1 0.6 %columns_filter.1 = bf16[128,16,128]{2,1,0:T(8,128)(2,1)S(1)} custom-call(bf16[128,16,128]{2,1,0:T(8,128)(2,1)S(1)} %bitcast.5, f32[8,128,128]{2,1,0:T(8,128)S(1)} %symmetric_kernel.1.screen_ref, bf16[6,256,256]{2,1,0:T(8,128)(2,1)S(1)} %get-tuple-element.13.table_ref), custom_call_target="tpu_custom_call" | custom-call | flops 268435456 | bytes 1048576 | tf_op jit(solution)/shard_map/columns_filter/pallas_call | solution.py:304
  25.7 13.4 %all_to_all.10.line_ref = bf16[16,8,16,128]{3,2,1,0:T(8,128)(2,1)S(1)} all-to-all(bf16[16,8,16,128]{3,2,1,0:T(8,128)(2,1)S(1)} %bitcast.6), channel_id=1, replica_groups=mesh['band'=32,'fft'=16] {'fft'}, dimensions={0} | all-to-all | bytes 1048576 | tf_op jit(solution)/shard_map/all_to_all | solution.py:316
  39.1 0.6 %planes_back.1 = (f32[8,128,128]{2,1,0:T(8,128)S(1)}, bf16[8,128,128]{2,1,0:T(8,128)(2,1)S(1)}) custom-call(bf16[16,8,16,128]{3,2,1,0:T(8,128)(2,1)S(1)} %all_to_all.10.line_ref, bf16[8,128,128]{2,1,0:T(8,128)(2,1)S(1)} %get-tuple-element.12.own_ref, bf16[8,128,128]{2,1,0:T(8,128)(2,1)S(1)} %collective-permute-done.other_ref, ...), custom_call_target="tpu_custom_call" | custom-call | flops 268435456 | bytes 1048576 | tf_op jit(solution)/shard_map/planes_back/pallas_call | solution.py:317
  39.7 2.4 %collective-permute-start.3 = (bf16[8,128,128]{2,1,0:T(8,128)(2,1)S(1)}, bf16[8,128,128]{2,1,0:T(8,128)(2,1)S(1)}, u32[]{:S(2)}, u32[]{:S(2)}) collective-permute-start(bf16[8,128,128]{2,1,0:T(8,128)(2,1)S(1)} %get-tuple-element.18), channel_id=1, source_target_pairs={{0,496},{16,0},{32,16},{48,32},{64,48},{80,64},{96,80},{112,96},{1... | collective-permute-start | bytes 786440 | tf_op jit(solution)/shard_map/ppermute | solution.py:21
  42.1 7.7 %collective-permute-done.3.returned_ref = bf16[8,128,128]{2,1,0:T(8,128)(2,1)S(1)} collective-permute-done((bf16[8,128,128]{2,1,0:T(8,128)(2,1)S(1)}, bf16[8,128,128]{2,1,0:T(8,128)(2,1)S(1)}, u32[]{:S(2)}, u32[]{:S(2)}) %collective-permute-start.3) | collective-permute-done | bytes 262176 | tf_op jit(solution)/shard_map/ppermute | solution.py:21
  49.7 0.8 %finish.1 = f32[8,128,128]{2,1,0:T(8,128)} custom-call(f32[8,128,128]{2,1,0:T(8,128)S(1)} %get-tuple-element.17.kept_ref, bf16[8,128,128]{2,1,0:T(8,128)(2,1)S(1)} %collective-permute-done.3.returned_ref), custom_call_target="tpu_custom_call" | custom-call | bytes 1048576 | tf_op jit(solution)/shard_map/finish/pallas_call | solution.py:327
  (1 shorter events, 0.0 us)
Async XLA Ops:
  0.0 5.8 %collective-permute-start = (bf16[8,128,128]{2,1,0:T(8,128)(2,1)}, bf16[8,128,128]{2,1,0:T(8,128)(2,1)S(1)}, u32[]{:S(2)}, u32[]{:S(2)}) collective-permute-start(bf16[8,128,128]{2,1,0:T(8,128)(2,1)} %bitcast.8), channel_id=1, source_target_pairs={{0,16},{16,32},{32,48},{48,64},{64,80},{80,96},{96,112},{112,128},... | collective-permute-start | bytes 786440 | tf_op jit(solution)/shard_map/ppermute | solution.py:21
  3.6 10.8 %collective-permute-start.1 = (bf16[528,128]{1,0:T(8,128)(2,1)S(1)}, bf16[528,128]{1,0:T(8,128)(2,1)S(1)}, u32[]{:S(2)}, u32[]{:S(2)}) collective-permute-start(bf16[528,128]{1,0:T(8,128)(2,1)S(1)} %get-tuple-element.15), channel_id=1, source_target_pairs={{0,15},{1,14},{2,13},{3,12},{4,11},{5,10},{6,9},{7,8},{8,7},{9,6},... | collective-permute-start | bytes 405512 | tf_op jit(solution)/shard_map/ppermute | solution.py:274
  7.2 17.9 %all-to-all-start = ((bf16[16,8,16,128]{3,2,1,0:T(8,128)(2,1)}), bf16[16,8,16,128]{3,2,1,0:T(8,128)(2,1)S(1)}, u32[]{:S(2)}, u32[]{:S(2)}) async-start(bf16[16,8,16,128]{3,2,1,0:T(8,128)(2,1)} %planes_forward.1), calls=%async_computation | async-start | bytes 1048576 | tf_op jit(solution)/shard_map/all_to_all | solution.py:293
  14.4 3.6 %collective-permute-start.2 = (bf16[528,128]{1,0:T(8,128)(2,1)S(1)}, bf16[528,128]{1,0:T(8,128)(2,1)S(1)}, u32[]{:S(2)}, u32[]{:S(2)}) collective-permute-start(bf16[528,128]{1,0:T(8,128)(2,1)S(1)} %relay.1.first_ref), channel_id=1, source_target_pairs={{0,16},{16,0},{32,48},{48,32},{64,80},{80,64},{96,112},{112,96},{1... | collective-permute-start | bytes 405512 | tf_op jit(solution)/shard_map/ppermute | solution.py:281
  39.7 10.0 %collective-permute-start.3 = (bf16[8,128,128]{2,1,0:T(8,128)(2,1)S(1)}, bf16[8,128,128]{2,1,0:T(8,128)(2,1)S(1)}, u32[]{:S(2)}, u32[]{:S(2)}) collective-permute-start(bf16[8,128,128]{2,1,0:T(8,128)(2,1)S(1)} %get-tuple-element.18), channel_id=1, source_target_pairs={{0,496},{16,0},{32,16},{48,32},{64,48},{80,64},{96,80},{112,96},{1... | collective-permute-start | bytes 786440 | tf_op jit(solution)/shard_map/ppermute | solution.py:21

commit v5 on v4

--- a/solution.py
+++ b/solution.py
@@ -1,3 +1,4 @@
+import functools
 import math
 
 import jax
@@ -11,7 +12,9 @@
 F32 = jnp.float32
 BF16 = jnp.bfloat16
 VMEM_LIMIT = 16 * 1024 * 1024
-AHEAD, BACK, AHEAD_SORTED, BACK_SORTED, ZED, DEZ = range(6)
+NEARLY_ALL = 65_700_000
+AHEAD_SORTED, ZED = range(2)
+AHEAD, BACK, BACK_SORTED, DEZ = range(4)
 FLIP, LOW, HIGH, WHOLE = range(4)
 SPARE = 16
 
@@ -50,7 +53,7 @@
     dez[:, :, :, half] *= 0.5
     zed = zed.reshape(2 * length, 2 * length).astype(ahead.dtype)
     dez = dez.reshape(2 * length, 2 * length).T.astype(ahead.dtype)
-    return ahead, back, ahead[order], back[:, order], zed, dez
+    return (ahead[order], zed), (ahead, back, back[:, order], dez)
 
 
 def mirror_tables(length):
@@ -181,37 +184,51 @@
         out_ref[c] = 0.5 * (here + other)
 
 
-def prepare(own_ref, kernel_ref, table_ref, mirror_ref, own_out, kernel_out, table_out, mirror_out,
-            packed_out, sems):
-    pairs = (
-        (kernel_ref, kernel_out),
-        (own_ref, own_out),
-        (table_ref, table_out),
-        (mirror_ref, mirror_out),
-    )
+def prepare(first, own_ref, kernel_ref, table_ref, *refs):
+    own_out, kernel_out, table_out, packed_out, sems = refs[-5:]
+
+    band = lax.axis_index("band")
+    early = (lax.rem(band, 2) == 1) & (band < lax.axis_size("band") - 1)
+
+    @pl.when(early == first)
+    def _():
+        pairs = (
+            (kernel_ref, kernel_out),
+            (own_ref, own_out),
+            (table_ref, table_out),
+        )
+        copies = [pltpu.make_async_copy(a, b, sems.at[i]) for i, (a, b) in enumerate(pairs)]
+        for copy in copies:
+            copy.start()
+        copies[0].wait()
+        length = kernel_out.shape[1]
+        half = length // 2
+        columns = kernel_out.shape[0] // length
+        packed = half * columns
+        lane = lax.broadcasted_iota(jnp.int32, (packed, length), 1)
+        packed_out[:packed] = jnp.where(
+            lane < half, pltpu.roll(kernel_out[:packed], half, 1), kernel_out[packed:]
+        ).astype(BF16)
+        row = lax.broadcasted_iota(jnp.int32, (SPARE, length), 0)
+        first = lax.broadcasted_iota(jnp.int32, (SPARE, length), 1) == 0
+        zeros = jnp.zeros((SPARE, length), F32)
+        for c in range(columns):
+            plane = kernel_out[pl.ds(c, length, stride=columns), :].astype(BF16)
+            chosen = ((row == c) & first).astype(F32).astype(BF16)
+            zeros = zeros + lax.dot_general(
+                chosen, plane, (((1,), (1,)), ((), ())), preferred_element_type=F32
+            )
+        packed_out[packed:] = zeros.astype(BF16)
+        for copy in copies[1:]:
+            copy.wait()
+
+
+def load(later_ref, table_ref, mirror_ref, table_out, mirror_out, sems):
+    pairs = ((table_ref, table_out), (mirror_ref, mirror_out))
     copies = [pltpu.make_async_copy(a, b, sems.at[i]) for i, (a, b) in enumerate(pairs)]
     for copy in copies:
         copy.start()
-    copies[0].wait()
-    length = kernel_out.shape[1]
-    half = length // 2
-    columns = kernel_out.shape[0] // length
-    packed = half * columns
-    lane = lax.broadcasted_iota(jnp.int32, (packed, length), 1)
-    packed_out[:packed] = jnp.where(
-        lane < half, pltpu.roll(kernel_out[:packed], half, 1), kernel_out[packed:]
-    ).astype(BF16)
-    row = lax.broadcasted_iota(jnp.int32, (SPARE, length), 0)
-    first = lax.broadcasted_iota(jnp.int32, (SPARE, length), 1) == 0
-    zeros = jnp.zeros((SPARE, length), F32)
-    for c in range(columns):
-        plane = kernel_out[pl.ds(c, length, stride=columns), :].astype(BF16)
-        chosen = ((row == c) & first).astype(F32).astype(BF16)
-        zeros = zeros + lax.dot_general(
-            chosen, plane, (((1,), (1,)), ((), ())), preferred_element_type=F32
-        )
-    packed_out[packed:] = zeros.astype(BF16)
-    for copy in copies[1:]:
+    for copy in copies:
         copy.wait()
 
 
@@ -226,7 +243,8 @@
         copy.wait()
 
 
-def call(body, outs, scratch=(), flops=0, name=None, in_specs=None, out_specs=None):
+def call(body, outs, scratch=(), flops=0, name=None, in_specs=None, out_specs=None, aliases=None,
+         limit=VMEM_LIMIT):
     specs = {"in_specs": in_specs, "out_specs": out_specs}
     specs = {key: value for key, value in specs.items() if value is not None}
     return pl.pallas_call(
@@ -234,8 +252,9 @@
         **specs,
         out_shape=outs,
         scratch_shapes=list(scratch),
+        input_output_aliases=aliases or {},
         cost_estimate=pl.CostEstimate(flops=flops, bytes_accessed=1 << 20, transcendentals=0),
-        compiler_params=pltpu.CompilerParams(vmem_limit_bytes=VMEM_LIMIT),
+        compiler_params=pltpu.CompilerParams(vmem_limit_bytes=limit),
         name=name,
     )
 
@@ -244,27 +263,41 @@
     planes, length = orbitals.shape[1], orbitals.shape[2]
     groups = lax.axis_size("fft")
     columns = length // groups
-    tables = jnp.asarray(np.stack(complex_tables(length, groups)))
+    near, far = (jnp.asarray(np.stack(some)) for some in complex_tables(length, groups))
     mirrors = jnp.asarray(mirror_tables(length))
     work = 8 * planes * length**3
 
+    here = jax.ShapeDtypeStruct((length * columns, length), F32)
+    sources = [
+        pltpu.with_memory_space_constraint(array, pltpu.HBM)
+        for array in (orbitals[0], kernel.reshape(here.shape), near, far, mirrors)
+    ]
+    results = (
+        pltpu.VMEM(orbitals.shape[1:], BF16),
+        pltpu.VMEM(here.shape, F32),
+        pltpu.VMEM(near.shape, BF16),
+        pltpu.VMEM((length // 2 * columns + SPARE, length), BF16),
+    )
+    anywhere = pl.BlockSpec(memory_space=pl.ANY)
+    in_vmem = pl.BlockSpec(memory_space=pltpu.VMEM)
+    prepared = call(
+        functools.partial(prepare, True),
+        results,
+        [pltpu.SemaphoreType.DMA((3,))],
+        in_specs=[anywhere] * 3,
+        limit=NEARLY_ALL,
+        name="prepare",
+    )(*sources[:3])
+    orbitals, *prepared = lax.optimization_barrier((orbitals, *prepared))
     other = from_behind(orbitals[0], "band", 1)
-    here = jax.ShapeDtypeStruct((length * columns, length), F32)
-    own, here, tables, mirrors, packed = call(
-        prepare,
-        (
-            jax.ShapeDtypeStruct(orbitals.shape[1:], BF16),
-            here,
-            jax.ShapeDtypeStruct(tables.shape, BF16),
-            jax.ShapeDtypeStruct(mirrors.shape, BF16),
-            jax.ShapeDtypeStruct((length // 2 * columns + SPARE, length), BF16),
-        ),
-        [pltpu.SemaphoreType.DMA((4,))],
-        in_specs=[pl.BlockSpec(memory_space=pl.ANY)] * 4,
+    own, here, near, packed = call(
+        functools.partial(prepare, False),
+        results,
+        [pltpu.SemaphoreType.DMA((3,))],
+        in_specs=[anywhere] * 3 + [in_vmem] * 4,
+        aliases={3 + i: i for i in range(4)},
         name="prepare",
-    )(*(pltpu.with_memory_space_constraint(array, pltpu.HBM) for array in (
-        orbitals[0], kernel.reshape(here.shape), tables, mirrors
-    )))
+    )(*sources[:3], *prepared)
     bands = lax.axis_size("band")
     swap = [
         (b * groups + f, b * groups + (groups - 1 - f if b % 2 == 0 else -f % groups))
@@ -278,7 +311,14 @@
         flops=100 * 10**9,
         name="relay",
     )(there)
-    twin = lax.ppermute(relayed, "band", [(b, b ^ 1) for b in range(bands)])
+    swapped = from_behind(relayed, "band", -1)
+    far, mirrors = call(
+        load,
+        (jax.ShapeDtypeStruct(far.shape, BF16), jax.ShapeDtypeStruct(mirrors.shape, BF16)),
+        [pltpu.SemaphoreType.DMA((2,))],
+        in_specs=[anywhere] * 3,
+        name="load",
+    )(relayed, *sources[3:])
 
     lines = jax.ShapeDtypeStruct((groups, planes, 2 * columns, length), BF16)
     spectrum = call(
@@ -288,7 +328,7 @@
         out_specs=pl.BlockSpec(memory_space=pl.ANY),
         name="planes_forward",
     )(
-        own, other, tables
+        own, other, near
     )
     spectrum = lax.all_to_all(spectrum, "fft", split_axis=0, concat_axis=0, tiled=True)
     screen = call(
@@ -299,7 +339,7 @@
         flops=work,
         name="symmetric_kernel",
     )(
-        here, relayed, twin, mirrors
+        here, relayed, swapped, mirrors
     )
     spectrum = call(
         columns_filter,
@@ -310,7 +350,7 @@
     )(
         spectrum.reshape(length, 2 * columns, length),
         screen,
-        tables,
+        far,
     )
     spectrum = spectrum.reshape(groups, planes, 2 * columns, length)
     spectrum = lax.all_to_all(spectrum, "fft", split_axis=0, concat_axis=0, tiled=True)
@@ -322,7 +362,7 @@
         ),
         flops=2 * work,
         name="planes_back",
-    )(spectrum, own, other, tables)
+    )(spectrum, own, other, far)
     returned = from_behind(sent, "band", -1)
     total = call(
         finish,

time: 50.9 us -> 50.2 us (0.986)
  the two profiles are of different devices: /device:TPU:193 before, /device:TPU:2 now
where the time goes in v5:
time: 50.2 us; the launch traced here: 49.9 us
  waiting for transfers between devices  15.7 us (31%)
  starting transfers between devices  14.6 us (29%)
  blocking collectives  13.1 us (26%)
  Pallas kernels  6.52 us (13%)
    all_to_all x1, blocking collectives, per_device(): lax.all_to_all(spectrum, 'fft', split_axis=0, concat_axis=0, tiled=True)  13.1 us
    ppermute x3, waiting for transfers between devices, from_behind(): lax.ppermute(shard, axis, [(i, (i + by) % devices) for i in range(devices)])  10.2 us
    all_to_all x1, starting transfers between devices, per_device(): lax.all_to_all(spectrum, 'fft', split_axis=0, concat_axis=0, tiled=True)  7.49 us
    ppermute x1, starting transfers between devices, per_device(): there = lax.ppermute(packed, ('band', 'fft'), swap)  5.85 us
    all_to_all x1, waiting for transfers between devices, per_device(): lax.all_to_all(spectrum, 'fft', split_axis=0, concat_axis=0, tiled=True)  5.43 us
    pallas_call x1, Pallas kernels, per_device(): call(functools.partial(prepare, False), results, [pltpu.SemaphoreType.DMA...  1.33 us
    pallas_call x1, Pallas kernels, per_device(): call(planes_forward, pltpu.HBM(lines.shape, lines.dtype), [pltpu.VMEM(lin...  1.32 us
    ppermute x3, starting transfers between devices, from_behind(): lax.ppermute(shard, axis, [(i, (i + by) % devices) for i in range(devices)])  1.24 us
  transfers between devices with their start and end apart: 5, of which 4 were waited for; matrix products, arithmetic and copies ran while one was open for 0% of the time, Pallas kernels for 9%

profile of v5, /device:TPU:2, one launch (start us, length us, event | category | flops | bytes accessed | tf_op | source)
XLA Modules:
  0.0 49.9 jit_solution(2552675522242775694)
XLA Ops:
  0.0 1.1 %collective-permute-start = (bf16[8,128,128]{2,1,0:T(8,128)(2,1)}, bf16[8,128,128]{2,1,0:T(8,128)(2,1)S(1)}, u32[]{:S(2)}, u32[]{:S(2)}) collective-permute-start(bf16[8,128,128]{2,1,0:T(8,128)(2,1)} %bitcast.11), channel_id=1, source_target_pairs={{0,16},{16,32},{32,48},{48,64},{64,80},{80,96},{96,112},{112,128},... | collective-permute-start | bytes 786440 | tf_op jit(solution)/shard_map/ppermute | solution.py:24
  1.2 1.3 %prepare.3 = (bf16[8,128,128]{2,1,0:T(8,128)(2,1)S(1)}, f32[1024,128]{1,0:T(8,128)S(1)}, bf16[2,256,256]{2,1,0:T(8,128)(2,1)S(1)}, bf16[528,128]{1,0:T(8,128)(2,1)S(1)}) custom-call(bf16[8,128,128]{2,1,0:T(8,128)(2,1)} %bitcast.12, f32[1024,128]{1,0:T(8,128)} %bitcast.9, ...), custom_call_target="tpu_custom_call", output_to_operand_aliasing={{0}: (3, {}), {1}: (4, {}), {2}: (5, {}), {3}: (6, {})} | custom-call | bytes 1048576 | tf_op jit(solution)/shard_map/prepare/pallas_call | solution.py:293
  2.5 5.8 %collective-permute-start.1 = (bf16[528,128]{1,0:T(8,128)(2,1)S(1)}, bf16[528,128]{1,0:T(8,128)(2,1)S(1)}, u32[]{:S(2)}, u32[]{:S(2)}) collective-permute-start(bf16[528,128]{1,0:T(8,128)(2,1)S(1)} %get-tuple-element.34), channel_id=1, source_target_pairs={{0,15},{1,14},{2,13},{3,12},{4,11},{5,10},{6,9},{7,8},{8,7},{9,6},... | collective-permute-start | bytes 405512 | tf_op jit(solution)/shard_map/ppermute | solution.py:307
  8.4 4.9 %collective-permute-done.other_ref = bf16[8,128,128]{2,1,0:T(8,128)(2,1)S(1)} collective-permute-done((bf16[8,128,128]{2,1,0:T(8,128)(2,1)}, bf16[8,128,128]{2,1,0:T(8,128)(2,1)S(1)}, u32[]{:S(2)}, u32[]{:S(2)}) %collective-permute-start) | collective-permute-done | bytes 262176 | tf_op jit(solution)/shard_map/ppermute | solution.py:24
  13.3 1.3 %planes_forward.1 = bf16[16,8,16,128]{3,2,1,0:T(8,128)(2,1)} custom-call(bf16[8,128,128]{2,1,0:T(8,128)(2,1)S(1)} %get-tuple-element.30.own_ref, bf16[8,128,128]{2,1,0:T(8,128)(2,1)S(1)} %collective-permute-done.other_ref, bf16[2,256,256]{2,1,0:T(8,128)(2,1)S(1)} %get-tuple-element.32.table_ref), custom_call_target="tpu_custom_call" | custom-call | bytes 1048576 | tf_op jit(solution)/shard_map/planes_forward/pallas_call | solution.py:324
  14.6 7.5 %all-to-all-start = ((bf16[16,8,16,128]{3,2,1,0:T(8,128)(2,1)}), bf16[16,8,16,128]{3,2,1,0:T(8,128)(2,1)S(1)}, u32[]{:S(2)}, u32[]{:S(2)}) async-start(bf16[16,8,16,128]{3,2,1,0:T(8,128)(2,1)} %planes_forward.1), calls=%async_computation | async-start | bytes 1048576 | tf_op jit(solution)/shard_map/all_to_all | solution.py:333
  22.1 0.0 collective-permute-done.1.there_ref
  22.1 0.0 collective-permute-start.2
  22.1 1.1 %load.1 = (bf16[4,256,256]{2,1,0:T(8,128)(2,1)S(1)}, bf16[4,128,128]{2,1,0:T(8,128)(2,1)S(1)}) custom-call(bf16[528,128]{1,0:T(8,128)(2,1)S(1)} %relay.1.later_ref.first_ref, bf16[4,256,256]{2,1,0:T(8,128)(2,1)} %constant.7.clone.table_ref, bf16[4,128,128]{2,1,0:T(8,128)(2,1)} %constant.8.clone.mirror_ref), custom_call_target="tpu_custom_call" | custom-call | bytes 1048576 | tf_op jit(solution)/shard_map/load/pallas_call | solution.py:315
  23.2 1.5 %collective-permute-done.2.second_ref = bf16[528,128]{1,0:T(8,128)(2,1)S(1)} collective-permute-done((bf16[528,128]{1,0:T(8,128)(2,1)S(1)}, bf16[528,128]{1,0:T(8,128)(2,1)S(1)}, u32[]{:S(2)}, u32[]{:S(2)}) %collective-permute-start.2) | collective-permute-done | bytes 135200 | tf_op jit(solution)/shard_map/ppermute | solution.py:24
  24.7 0.7 %symmetric_kernel.1.screen_ref = f32[8,128,128]{2,1,0:T(8,128)S(1)} custom-call(f32[1024,128]{1,0:T(8,128)S(1)} %get-tuple-element.33.here_ref, bf16[528,128]{1,0:T(8,128)(2,1)S(1)} %relay.1.later_ref.first_ref, bf16[528,128]{1,0:T(8,128)(2,1)S(1)} %collective-permute-done.2.second_ref, bf16[4,128,128]{2,1,0:T(8,128)(2,1)S(1)} %get-tuple-element.35.mirror_ref), custom_call_target="tpu_custom_call" | custom-call | flops 134217728 | bytes 1048576 | tf_op jit(solution)/shard_map/symmetric_kernel/pallas_call | solution.py:334
  25.4 5.4 %all-to-all-done = bf16[16,8,16,128]{3,2,1,0:T(8,128)(2,1)S(1)} async-done(((bf16[16,8,16,128]{3,2,1,0:T(8,128)(2,1)}), bf16[16,8,16,128]{3,2,1,0:T(8,128)(2,1)S(1)}, u32[]{:S(2)}, u32[]{:S(2)}) %all-to-all-start) | async-done | bytes 524320 | tf_op jit(solution)/shard_map/all_to_all | solution.py:333
  30.8 0.6 %columns_filter.1 = bf16[128,16,128]{2,1,0:T(8,128)(2,1)S(1)} custom-call(bf16[128,16,128]{2,1,0:T(8,128)(2,1)S(1)} %bitcast.6, f32[8,128,128]{2,1,0:T(8,128)S(1)} %symmetric_kernel.1.screen_ref, bf16[4,256,256]{2,1,0:T(8,128)(2,1)S(1)} %get-tuple-element.36.table_ref), custom_call_target="tpu_custom_call" | custom-call | flops 268435456 | bytes 1048576 | tf_op jit(solution)/shard_map/columns_filter/pallas_call | solution.py:344
  31.5 13.1 %all_to_all.10.line_ref = bf16[16,8,16,128]{3,2,1,0:T(8,128)(2,1)S(1)} all-to-all(bf16[16,8,16,128]{3,2,1,0:T(8,128)(2,1)S(1)} %bitcast.7), channel_id=1, replica_groups=mesh['band'=32,'fft'=16] {'fft'}, dimensions={0} | all-to-all | bytes 1048576 | tf_op jit(solution)/shard_map/all_to_all | solution.py:356
  44.6 0.6 %planes_back.1 = (f32[8,128,128]{2,1,0:T(8,128)S(1)}, bf16[8,128,128]{2,1,0:T(8,128)(2,1)S(1)}) custom-call(bf16[16,8,16,128]{3,2,1,0:T(8,128)(2,1)S(1)} %all_to_all.10.line_ref, bf16[8,128,128]{2,1,0:T(8,128)(2,1)S(1)} %get-tuple-element.30.own_ref, bf16[8,128,128]{2,1,0:T(8,128)(2,1)S(1)} %collective-permute-done.other_ref, ...), custom_call_target="tpu_custom_call" | custom-call | flops 268435456 | bytes 1048576 | tf_op jit(solution)/shard_map/planes_back/pallas_call | solution.py:357
  45.1 0.1 collective-permute-start.3
  45.2 3.9 %collective-permute-done.3.returned_ref = bf16[8,128,128]{2,1,0:T(8,128)(2,1)S(1)} collective-permute-done((bf16[8,128,128]{2,1,0:T(8,128)(2,1)S(1)}, bf16[8,128,128]{2,1,0:T(8,128)(2,1)S(1)}, u32[]{:S(2)}, u32[]{:S(2)}) %collective-permute-start.3) | collective-permute-done | bytes 262176 | tf_op jit(solution)/shard_map/ppermute | solution.py:24
  49.1 0.8 %finish.1 = f32[8,128,128]{2,1,0:T(8,128)} custom-call(f32[8,128,128]{2,1,0:T(8,128)S(1)} %get-tuple-element.37.kept_ref, bf16[8,128,128]{2,1,0:T(8,128)(2,1)S(1)} %collective-permute-done.3.returned_ref), custom_call_target="tpu_custom_call" | custom-call | bytes 1048576 | tf_op jit(solution)/shard_map/finish/pallas_call | solution.py:367
  (2 shorter events, 0.0 us)
Async XLA Ops:
  0.0 13.2 %collective-permute-start = (bf16[8,128,128]{2,1,0:T(8,128)(2,1)}, bf16[8,128,128]{2,1,0:T(8,128)(2,1)S(1)}, u32[]{:S(2)}, u32[]{:S(2)}) collective-permute-start(bf16[8,128,128]{2,1,0:T(8,128)(2,1)} %bitcast.11), channel_id=1, source_target_pairs={{0,16},{16,32},{32,48},{48,64},{64,80},{80,96},{96,112},{112,128},... | collective-permute-start | bytes 786440 | tf_op jit(solution)/shard_map/ppermute | solution.py:24
  2.5 19.6 %collective-permute-start.1 = (bf16[528,128]{1,0:T(8,128)(2,1)S(1)}, bf16[528,128]{1,0:T(8,128)(2,1)S(1)}, u32[]{:S(2)}, u32[]{:S(2)}) collective-permute-start(bf16[528,128]{1,0:T(8,128)(2,1)S(1)} %get-tuple-element.34), channel_id=1, source_target_pairs={{0,15},{1,14},{2,13},{3,12},{4,11},{5,10},{6,9},{7,8},{8,7},{9,6},... | collective-permute-start | bytes 405512 | tf_op jit(solution)/shard_map/ppermute | solution.py:307
  14.6 16.3 %all-to-all-start = ((bf16[16,8,16,128]{3,2,1,0:T(8,128)(2,1)}), bf16[16,8,16,128]{3,2,1,0:T(8,128)(2,1)S(1)}, u32[]{:S(2)}, u32[]{:S(2)}) async-start(bf16[16,8,16,128]{3,2,1,0:T(8,128)(2,1)} %planes_forward.1), calls=%async_computation | async-start | bytes 1048576 | tf_op jit(solution)/shard_map/all_to_all | solution.py:333
  22.1 2.6 %collective-permute-start.2 = (bf16[528,128]{1,0:T(8,128)(2,1)S(1)}, bf16[528,128]{1,0:T(8,128)(2,1)S(1)}, u32[]{:S(2)}, u32[]{:S(2)}) collective-permute-start(bf16[528,128]{1,0:T(8,128)(2,1)S(1)} %relay.1.later_ref.first_ref), channel_id=1, source_target_pairs={{0,496},{16,0},{32,16},{48,32},{64,48},{80,64},{96,80},{112,96},{1... | collective-permute-start | bytes 405512 | tf_op jit(solution)/shard_map/ppermute | solution.py:24
  45.1 4.0 %collective-permute-start.3 = (bf16[8,128,128]{2,1,0:T(8,128)(2,1)S(1)}, bf16[8,128,128]{2,1,0:T(8,128)(2,1)S(1)}, u32[]{:S(2)}, u32[]{:S(2)}) collective-permute-start(bf16[8,128,128]{2,1,0:T(8,128)(2,1)S(1)} %get-tuple-element.38), channel_id=1, source_target_pairs={{0,496},{16,0},{32,16},{48,32},{64,48},{80,64},{96,80},{112,96},{1... | collective-permute-start | bytes 786440 | tf_op jit(solution)/shard_map/ppermute | solution.py:24

commit v6 on v5

--- a/solution.py
+++ b/solution.py
@@ -189,6 +189,13 @@
 
     band = lax.axis_index("band")
     early = (lax.rem(band, 2) == 1) & (band < lax.axis_size("band") - 1)
+
+    if not first:
+
+        @pl.when(early)
+        def _():
+            for made, out in zip(refs[:4], refs[4:8]):
+                out[...] = made[...]
 
     @pl.when(early == first)
     def _():

time: 50.2 us -> 50.2 us (level)
  no operation moved by 1% of the time
where the time goes in v6:
time: 50.2 us; the launch traced here: 49.9 us
  waiting for transfers between devices  15.7 us (31%)
  starting transfers between devices  14.6 us (29%)
  blocking collectives  13.1 us (26%)
  Pallas kernels  6.52 us (13%)
    all_to_all x1, blocking collectives, per_device(): lax.all_to_all(spectrum, 'fft', split_axis=0, concat_axis=0, tiled=True)  13.1 us
    ppermute x3, waiting for transfers between devices, from_behind(): lax.ppermute(shard, axis, [(i, (i + by) % devices) for i in range(devices)])  10.2 us
    all_to_all x1, starting transfers between devices, per_device(): lax.all_to_all(spectrum, 'fft', split_axis=0, concat_axis=0, tiled=True)  7.49 us
    ppermute x1, starting transfers between devices, per_device(): there = lax.ppermute(packed, ('band', 'fft'), swap)  5.85 us
    all_to_all x1, waiting for transfers between devices, per_device(): lax.all_to_all(spectrum, 'fft', split_axis=0, concat_axis=0, tiled=True)  5.43 us
    pallas_call x1, Pallas kernels, per_device(): call(functools.partial(prepare, False), results, [pltpu.SemaphoreType.DMA...  1.33 us
    pallas_call x1, Pallas kernels, per_device(): call(planes_forward, pltpu.HBM(lines.shape, lines.dtype), [pltpu.VMEM(lin...  1.32 us
    ppermute x3, starting transfers between devices, from_behind(): lax.ppermute(shard, axis, [(i, (i + by) % devices) for i in range(devices)])  1.24 us
  transfers between devices with their start and end apart: 5, of which 4 were waited for; matrix products, arithmetic and copies ran while one was open for 0% of the time, Pallas kernels for 9%

profile of v6, /device:TPU:2, one launch (start us, length us, event | category | flops | bytes accessed | tf_op | source)
XLA Modules:
  0.0 49.9 jit_solution(16611034964387773562)
XLA Ops:
  0.0 1.1 %collective-permute-start = (bf16[8,128,128]{2,1,0:T(8,128)(2,1)}, bf16[8,128,128]{2,1,0:T(8,128)(2,1)S(1)}, u32[]{:S(2)}, u32[]{:S(2)}) collective-permute-start(bf16[8,128,128]{2,1,0:T(8,128)(2,1)} %bitcast.11), channel_id=1, source_target_pairs={{0,16},{16,32},{32,48},{48,64},{64,80},{80,96},{96,112},{112,128},... | collective-permute-start | bytes 786440 | tf_op jit(solution)/shard_map/ppermute | solution.py:24
  1.2 1.3 %prepare.3 = (bf16[8,128,128]{2,1,0:T(8,128)(2,1)S(1)}, f32[1024,128]{1,0:T(8,128)S(1)}, bf16[2,256,256]{2,1,0:T(8,128)(2,1)S(1)}, bf16[528,128]{1,0:T(8,128)(2,1)S(1)}) custom-call(bf16[8,128,128]{2,1,0:T(8,128)(2,1)} %bitcast.12, f32[1024,128]{1,0:T(8,128)} %bitcast.9, ...), custom_call_target="tpu_custom_call", output_to_operand_aliasing={{0}: (3, {}), {1}: (4, {}), {2}: (5, {}), {3}: (6, {})} | custom-call | bytes 1048576 | tf_op jit(solution)/shard_map/prepare/pallas_call | solution.py:300
  2.5 5.8 %collective-permute-start.1 = (bf16[528,128]{1,0:T(8,128)(2,1)S(1)}, bf16[528,128]{1,0:T(8,128)(2,1)S(1)}, u32[]{:S(2)}, u32[]{:S(2)}) collective-permute-start(bf16[528,128]{1,0:T(8,128)(2,1)S(1)} %get-tuple-element.34), channel_id=1, source_target_pairs={{0,15},{1,14},{2,13},{3,12},{4,11},{5,10},{6,9},{7,8},{8,7},{9,6},... | collective-permute-start | bytes 405512 | tf_op jit(solution)/shard_map/ppermute | solution.py:314
  8.4 4.9 %collective-permute-done.other_ref = bf16[8,128,128]{2,1,0:T(8,128)(2,1)S(1)} collective-permute-done((bf16[8,128,128]{2,1,0:T(8,128)(2,1)}, bf16[8,128,128]{2,1,0:T(8,128)(2,1)S(1)}, u32[]{:S(2)}, u32[]{:S(2)}) %collective-permute-start) | collective-permute-done | bytes 262176 | tf_op jit(solution)/shard_map/ppermute | solution.py:24
  13.3 1.3 %planes_forward.1 = bf16[16,8,16,128]{3,2,1,0:T(8,128)(2,1)} custom-call(bf16[8,128,128]{2,1,0:T(8,128)(2,1)S(1)} %get-tuple-element.30.own_ref, bf16[8,128,128]{2,1,0:T(8,128)(2,1)S(1)} %collective-permute-done.other_ref, bf16[2,256,256]{2,1,0:T(8,128)(2,1)S(1)} %get-tuple-element.32.table_ref), custom_call_target="tpu_custom_call" | custom-call | bytes 1048576 | tf_op jit(solution)/shard_map/planes_forward/pallas_call | solution.py:331
  14.6 7.5 %all-to-all-start = ((bf16[16,8,16,128]{3,2,1,0:T(8,128)(2,1)}), bf16[16,8,16,128]{3,2,1,0:T(8,128)(2,1)S(1)}, u32[]{:S(2)}, u32[]{:S(2)}) async-start(bf16[16,8,16,128]{3,2,1,0:T(8,128)(2,1)} %planes_forward.1), calls=%async_computation | async-start | bytes 1048576 | tf_op jit(solution)/shard_map/all_to_all | solution.py:340
  22.1 0.0 collective-permute-done.1.there_ref
  22.1 0.0 collective-permute-start.2
  22.1 1.1 %load.1 = (bf16[4,256,256]{2,1,0:T(8,128)(2,1)S(1)}, bf16[4,128,128]{2,1,0:T(8,128)(2,1)S(1)}) custom-call(bf16[528,128]{1,0:T(8,128)(2,1)S(1)} %relay.1.later_ref.first_ref, bf16[4,256,256]{2,1,0:T(8,128)(2,1)} %constant.7.clone.table_ref, bf16[4,128,128]{2,1,0:T(8,128)(2,1)} %constant.8.clone.mirror_ref), custom_call_target="tpu_custom_call" | custom-call | bytes 1048576 | tf_op jit(solution)/shard_map/load/pallas_call | solution.py:322
  23.2 1.5 %collective-permute-done.2.second_ref = bf16[528,128]{1,0:T(8,128)(2,1)S(1)} collective-permute-done((bf16[528,128]{1,0:T(8,128)(2,1)S(1)}, bf16[528,128]{1,0:T(8,128)(2,1)S(1)}, u32[]{:S(2)}, u32[]{:S(2)}) %collective-permute-start.2) | collective-permute-done | bytes 135200 | tf_op jit(solution)/shard_map/ppermute | solution.py:24
  24.7 0.7 %symmetric_kernel.1.screen_ref = f32[8,128,128]{2,1,0:T(8,128)S(1)} custom-call(f32[1024,128]{1,0:T(8,128)S(1)} %get-tuple-element.33.here_ref, bf16[528,128]{1,0:T(8,128)(2,1)S(1)} %relay.1.later_ref.first_ref, bf16[528,128]{1,0:T(8,128)(2,1)S(1)} %collective-permute-done.2.second_ref, bf16[4,128,128]{2,1,0:T(8,128)(2,1)S(1)} %get-tuple-element.35.mirror_ref), custom_call_target="tpu_custom_call" | custom-call | flops 134217728 | bytes 1048576 | tf_op jit(solution)/shard_map/symmetric_kernel/pallas_call | solution.py:341
  25.4 5.4 %all-to-all-done = bf16[16,8,16,128]{3,2,1,0:T(8,128)(2,1)S(1)} async-done(((bf16[16,8,16,128]{3,2,1,0:T(8,128)(2,1)}), bf16[16,8,16,128]{3,2,1,0:T(8,128)(2,1)S(1)}, u32[]{:S(2)}, u32[]{:S(2)}) %all-to-all-start) | async-done | bytes 524320 | tf_op jit(solution)/shard_map/all_to_all | solution.py:340
  30.8 0.6 %columns_filter.1 = bf16[128,16,128]{2,1,0:T(8,128)(2,1)S(1)} custom-call(bf16[128,16,128]{2,1,0:T(8,128)(2,1)S(1)} %bitcast.6, f32[8,128,128]{2,1,0:T(8,128)S(1)} %symmetric_kernel.1.screen_ref, bf16[4,256,256]{2,1,0:T(8,128)(2,1)S(1)} %get-tuple-element.36.table_ref), custom_call_target="tpu_custom_call" | custom-call | flops 268435456 | bytes 1048576 | tf_op jit(solution)/shard_map/columns_filter/pallas_call | solution.py:351
  31.5 13.1 %all_to_all.10.line_ref = bf16[16,8,16,128]{3,2,1,0:T(8,128)(2,1)S(1)} all-to-all(bf16[16,8,16,128]{3,2,1,0:T(8,128)(2,1)S(1)} %bitcast.7), channel_id=1, replica_groups=mesh['band'=32,'fft'=16] {'fft'}, dimensions={0} | all-to-all | bytes 1048576 | tf_op jit(solution)/shard_map/all_to_all | solution.py:363
  44.6 0.6 %planes_back.1 = (f32[8,128,128]{2,1,0:T(8,128)S(1)}, bf16[8,128,128]{2,1,0:T(8,128)(2,1)S(1)}) custom-call(bf16[16,8,16,128]{3,2,1,0:T(8,128)(2,1)S(1)} %all_to_all.10.line_ref, bf16[8,128,128]{2,1,0:T(8,128)(2,1)S(1)} %get-tuple-element.30.own_ref, bf16[8,128,128]{2,1,0:T(8,128)(2,1)S(1)} %collective-permute-done.other_ref, ...), custom_call_target="tpu_custom_call" | custom-call | flops 268435456 | bytes 1048576 | tf_op jit(solution)/shard_map/planes_back/pallas_call | solution.py:364
  45.1 0.1 collective-permute-start.3
  45.2 3.9 %collective-permute-done.3.returned_ref = bf16[8,128,128]{2,1,0:T(8,128)(2,1)S(1)} collective-permute-done((bf16[8,128,128]{2,1,0:T(8,128)(2,1)S(1)}, bf16[8,128,128]{2,1,0:T(8,128)(2,1)S(1)}, u32[]{:S(2)}, u32[]{:S(2)}) %collective-permute-start.3) | collective-permute-done | bytes 262176 | tf_op jit(solution)/shard_map/ppermute | solution.py:24
  49.1 0.8 %finish.1 = f32[8,128,128]{2,1,0:T(8,128)} custom-call(f32[8,128,128]{2,1,0:T(8,128)S(1)} %get-tuple-element.37.kept_ref, bf16[8,128,128]{2,1,0:T(8,128)(2,1)S(1)} %collective-permute-done.3.returned_ref), custom_call_target="tpu_custom_call" | custom-call | bytes 1048576 | tf_op jit(solution)/shard_map/finish/pallas_call | solution.py:374
  (2 shorter events, 0.0 us)
Async XLA Ops:
  0.0 13.2 %collective-permute-start = (bf16[8,128,128]{2,1,0:T(8,128)(2,1)}, bf16[8,128,128]{2,1,0:T(8,128)(2,1)S(1)}, u32[]{:S(2)}, u32[]{:S(2)}) collective-permute-start(bf16[8,128,128]{2,1,0:T(8,128)(2,1)} %bitcast.11), channel_id=1, source_target_pairs={{0,16},{16,32},{32,48},{48,64},{64,80},{80,96},{96,112},{112,128},... | collective-permute-start | bytes 786440 | tf_op jit(solution)/shard_map/ppermute | solution.py:24
  2.5 19.6 %collective-permute-start.1 = (bf16[528,128]{1,0:T(8,128)(2,1)S(1)}, bf16[528,128]{1,0:T(8,128)(2,1)S(1)}, u32[]{:S(2)}, u32[]{:S(2)}) collective-permute-start(bf16[528,128]{1,0:T(8,128)(2,1)S(1)} %get-tuple-element.34), channel_id=1, source_target_pairs={{0,15},{1,14},{2,13},{3,12},{4,11},{5,10},{6,9},{7,8},{8,7},{9,6},... | collective-permute-start | bytes 405512 | tf_op jit(solution)/shard_map/ppermute | solution.py:314
  14.6 16.3 %all-to-all-start = ((bf16[16,8,16,128]{3,2,1,0:T(8,128)(2,1)}), bf16[16,8,16,128]{3,2,1,0:T(8,128)(2,1)S(1)}, u32[]{:S(2)}, u32[]{:S(2)}) async-start(bf16[16,8,16,128]{3,2,1,0:T(8,128)(2,1)} %planes_forward.1), calls=%async_computation | async-start | bytes 1048576 | tf_op jit(solution)/shard_map/all_to_all | solution.py:340
  22.1 2.6 %collective-permute-start.2 = (bf16[528,128]{1,0:T(8,128)(2,1)S(1)}, bf16[528,128]{1,0:T(8,128)(2,1)S(1)}, u32[]{:S(2)}, u32[]{:S(2)}) collective-permute-start(bf16[528,128]{1,0:T(8,128)(2,1)S(1)} %relay.1.later_ref.first_ref), channel_id=1, source_target_pairs={{0,496},{16,0},{32,16},{48,32},{64,48},{80,64},{96,80},{112,96},{1... | collective-permute-start | bytes 405512 | tf_op jit(solution)/shard_map/ppermute | solution.py:24
  45.1 4.0 %collective-permute-start.3 = (bf16[8,128,128]{2,1,0:T(8,128)(2,1)S(1)}, bf16[8,128,128]{2,1,0:T(8,128)(2,1)S(1)}, u32[]{:S(2)}, u32[]{:S(2)}) collective-permute-start(bf16[8,128,128]{2,1,0:T(8,128)(2,1)S(1)} %get-tuple-element.38), channel_id=1, source_target_pairs={{0,496},{16,0},{32,16},{48,32},{64,48},{80,64},{96,80},{112,96},{1... | collective-permute-start | bytes 786440 | tf_op jit(solution)/shard_map/ppermute | solution.py:24

commit v7 on v6

--- a/solution.py
+++ b/solution.py
@@ -155,10 +155,10 @@
 
     def spread(main_ref, edge_ref):
         row = lax.broadcasted_iota(jnp.int32, (packed, length), 0)
+        main, edge = main_ref[:packed].astype(F32), edge_ref[:packed].astype(F32)
+        block = jnp.where(lax.rem(row, columns) == 0, edge, main).astype(BF16)
         for out, choice in ((low, LOW), (high, HIGH)):
-            main = dot(main_ref[:packed], mirror_ref[choice])
-            edge = dot(edge_ref[:packed], mirror_ref[choice])
-            out[...] = jnp.where(lax.rem(row, columns) == 0, edge, main)
+            out[...] = dot(block, mirror_ref[choice])
         row = lax.broadcasted_iota(jnp.int32, (SPARE, length), 0)
         main, edge = main_ref[packed:].astype(F32), edge_ref[packed:].astype(F32)
         zero[...] = jnp.where(row == 0, edge, main)

time: 50.2 us -> 50.2 us (level)
  no operation moved by 1% of the time
where the time goes in v7:
time: 50.2 us; the launch traced here: 49.9 us
  waiting for transfers between devices  15.7 us (31%)
  starting transfers between devices  14.5 us (29%)
  blocking collectives  13.1 us (26%)
  Pallas kernels  6.46 us (13%)
    all_to_all x1, blocking collectives, per_device(): lax.all_to_all(spectrum, 'fft', split_axis=0, concat_axis=0, tiled=True)  13.1 us
    ppermute x3, waiting for transfers between devices, from_behind(): lax.ppermute(shard, axis, [(i, (i + by) % devices) for i in range(devices)])  10.2 us
    all_to_all x1, starting transfers between devices, per_device(): lax.all_to_all(spectrum, 'fft', split_axis=0, concat_axis=0, tiled=True)  7.49 us
    ppermute x1, starting transfers between devices, per_device(): there = lax.ppermute(packed, ('band', 'fft'), swap)  5.85 us
    all_to_all x1, waiting for transfers between devices, per_device(): lax.all_to_all(spectrum, 'fft', split_axis=0, concat_axis=0, tiled=True)  5.49 us
    pallas_call x1, Pallas kernels, per_device(): call(functools.partial(prepare, False), results, [pltpu.SemaphoreType.DMA...  1.33 us
    pallas_call x1, Pallas kernels, per_device(): call(planes_forward, pltpu.HBM(lines.shape, lines.dtype), [pltpu.VMEM(lin...  1.32 us
    ppermute x3, starting transfers between devices, from_behind(): lax.ppermute(shard, axis, [(i, (i + by) % devices) for i in range(devices)])  1.18 us
  transfers between devices with their start and end apart: 5, of which 4 were waited for; matrix products, arithmetic and copies ran while one was open for 0% of the time, Pallas kernels for 9%

profile of v7, /device:TPU:2, one launch (start us, length us, event | category | flops | bytes accessed | tf_op | source)
XLA Modules:
  0.0 49.9 jit_solution(15512008075757657066)
XLA Ops:
  0.0 1.1 %collective-permute-start = (bf16[8,128,128]{2,1,0:T(8,128)(2,1)}, bf16[8,128,128]{2,1,0:T(8,128)(2,1)S(1)}, u32[]{:S(2)}, u32[]{:S(2)}) collective-permute-start(bf16[8,128,128]{2,1,0:T(8,128)(2,1)} %bitcast.11), channel_id=1, source_target_pairs={{0,16},{16,32},{32,48},{48,64},{64,80},{80,96},{96,112},{112,128},... | collective-permute-start | bytes 786440 | tf_op jit(solution)/shard_map/ppermute | solution.py:24
  1.2 1.3 %prepare.3 = (bf16[8,128,128]{2,1,0:T(8,128)(2,1)S(1)}, f32[1024,128]{1,0:T(8,128)S(1)}, bf16[2,256,256]{2,1,0:T(8,128)(2,1)S(1)}, bf16[528,128]{1,0:T(8,128)(2,1)S(1)}) custom-call(bf16[8,128,128]{2,1,0:T(8,128)(2,1)} %bitcast.12, f32[1024,128]{1,0:T(8,128)} %bitcast.9, ...), custom_call_target="tpu_custom_call", output_to_operand_aliasing={{0}: (3, {}), {1}: (4, {}), {2}: (5, {}), {3}: (6, {})} | custom-call | bytes 1048576 | tf_op jit(solution)/shard_map/prepare/pallas_call | solution.py:300
  2.5 5.8 %collective-permute-start.1 = (bf16[528,128]{1,0:T(8,128)(2,1)S(1)}, bf16[528,128]{1,0:T(8,128)(2,1)S(1)}, u32[]{:S(2)}, u32[]{:S(2)}) collective-permute-start(bf16[528,128]{1,0:T(8,128)(2,1)S(1)} %get-tuple-element.34), channel_id=1, source_target_pairs={{0,15},{1,14},{2,13},{3,12},{4,11},{5,10},{6,9},{7,8},{8,7},{9,6},... | collective-permute-start | bytes 405512 | tf_op jit(solution)/shard_map/ppermute | solution.py:314
  8.4 4.9 %collective-permute-done.other_ref = bf16[8,128,128]{2,1,0:T(8,128)(2,1)S(1)} collective-permute-done((bf16[8,128,128]{2,1,0:T(8,128)(2,1)}, bf16[8,128,128]{2,1,0:T(8,128)(2,1)S(1)}, u32[]{:S(2)}, u32[]{:S(2)}) %collective-permute-start) | collective-permute-done | bytes 262176 | tf_op jit(solution)/shard_map/ppermute | solution.py:24
  13.3 1.3 %planes_forward.1 = bf16[16,8,16,128]{3,2,1,0:T(8,128)(2,1)} custom-call(bf16[8,128,128]{2,1,0:T(8,128)(2,1)S(1)} %get-tuple-element.30.own_ref, bf16[8,128,128]{2,1,0:T(8,128)(2,1)S(1)} %collective-permute-done.other_ref, bf16[2,256,256]{2,1,0:T(8,128)(2,1)S(1)} %get-tuple-element.32.table_ref), custom_call_target="tpu_custom_call" | custom-call | bytes 1048576 | tf_op jit(solution)/shard_map/planes_forward/pallas_call | solution.py:331
  14.6 7.5 %all-to-all-start = ((bf16[16,8,16,128]{3,2,1,0:T(8,128)(2,1)}), bf16[16,8,16,128]{3,2,1,0:T(8,128)(2,1)S(1)}, u32[]{:S(2)}, u32[]{:S(2)}) async-start(bf16[16,8,16,128]{3,2,1,0:T(8,128)(2,1)} %planes_forward.1), calls=%async_computation | async-start | bytes 1048576 | tf_op jit(solution)/shard_map/all_to_all | solution.py:340
  22.1 0.0 collective-permute-done.1.there_ref
  22.1 0.0 collective-permute-start.2
  22.1 1.1 %load.1 = (bf16[4,256,256]{2,1,0:T(8,128)(2,1)S(1)}, bf16[4,128,128]{2,1,0:T(8,128)(2,1)S(1)}) custom-call(bf16[528,128]{1,0:T(8,128)(2,1)S(1)} %relay.1.later_ref.first_ref, bf16[4,256,256]{2,1,0:T(8,128)(2,1)} %constant.7.clone.table_ref, bf16[4,128,128]{2,1,0:T(8,128)(2,1)} %constant.8.clone.mirror_ref), custom_call_target="tpu_custom_call" | custom-call | bytes 1048576 | tf_op jit(solution)/shard_map/load/pallas_call | solution.py:322
  23.2 1.5 %collective-permute-done.2.second_ref = bf16[528,128]{1,0:T(8,128)(2,1)S(1)} collective-permute-done((bf16[528,128]{1,0:T(8,128)(2,1)S(1)}, bf16[528,128]{1,0:T(8,128)(2,1)S(1)}, u32[]{:S(2)}, u32[]{:S(2)}) %collective-permute-start.2) | collective-permute-done | bytes 135200 | tf_op jit(solution)/shard_map/ppermute | solution.py:24
  24.7 0.7 %symmetric_kernel.1.screen_ref = f32[8,128,128]{2,1,0:T(8,128)S(1)} custom-call(f32[1024,128]{1,0:T(8,128)S(1)} %get-tuple-element.33.here_ref, bf16[528,128]{1,0:T(8,128)(2,1)S(1)} %relay.1.later_ref.first_ref, bf16[528,128]{1,0:T(8,128)(2,1)S(1)} %collective-permute-done.2.second_ref, bf16[4,128,128]{2,1,0:T(8,128)(2,1)S(1)} %get-tuple-element.35.mirror_ref), custom_call_target="tpu_custom_call" | custom-call | flops 134217728 | bytes 1048576 | tf_op jit(solution)/shard_map/symmetric_kernel/pallas_call | solution.py:341
  25.4 5.5 %all-to-all-done = bf16[16,8,16,128]{3,2,1,0:T(8,128)(2,1)S(1)} async-done(((bf16[16,8,16,128]{3,2,1,0:T(8,128)(2,1)}), bf16[16,8,16,128]{3,2,1,0:T(8,128)(2,1)S(1)}, u32[]{:S(2)}, u32[]{:S(2)}) %all-to-all-start) | async-done | bytes 524320 | tf_op jit(solution)/shard_map/all_to_all | solution.py:340
  30.8 0.6 %columns_filter.1 = bf16[128,16,128]{2,1,0:T(8,128)(2,1)S(1)} custom-call(bf16[128,16,128]{2,1,0:T(8,128)(2,1)S(1)} %bitcast.6, f32[8,128,128]{2,1,0:T(8,128)S(1)} %symmetric_kernel.1.screen_ref, bf16[4,256,256]{2,1,0:T(8,128)(2,1)S(1)} %get-tuple-element.36.table_ref), custom_call_target="tpu_custom_call" | custom-call | flops 268435456 | bytes 1048576 | tf_op jit(solution)/shard_map/columns_filter/pallas_call | solution.py:351
  31.5 13.1 %all_to_all.10.line_ref = bf16[16,8,16,128]{3,2,1,0:T(8,128)(2,1)S(1)} all-to-all(bf16[16,8,16,128]{3,2,1,0:T(8,128)(2,1)S(1)} %bitcast.7), channel_id=1, replica_groups=mesh['band'=32,'fft'=16] {'fft'}, dimensions={0} | all-to-all | bytes 1048576 | tf_op jit(solution)/shard_map/all_to_all | solution.py:363
  44.6 0.6 %planes_back.1 = (f32[8,128,128]{2,1,0:T(8,128)S(1)}, bf16[8,128,128]{2,1,0:T(8,128)(2,1)S(1)}) custom-call(bf16[16,8,16,128]{3,2,1,0:T(8,128)(2,1)S(1)} %all_to_all.10.line_ref, bf16[8,128,128]{2,1,0:T(8,128)(2,1)S(1)} %get-tuple-element.30.own_ref, bf16[8,128,128]{2,1,0:T(8,128)(2,1)S(1)} %collective-permute-done.other_ref, ...), custom_call_target="tpu_custom_call" | custom-call | flops 268435456 | bytes 1048576 | tf_op jit(solution)/shard_map/planes_back/pallas_call | solution.py:364
  45.1 0.0 collective-permute-start.3
  45.2 3.9 %collective-permute-done.3.returned_ref = bf16[8,128,128]{2,1,0:T(8,128)(2,1)S(1)} collective-permute-done((bf16[8,128,128]{2,1,0:T(8,128)(2,1)S(1)}, bf16[8,128,128]{2,1,0:T(8,128)(2,1)S(1)}, u32[]{:S(2)}, u32[]{:S(2)}) %collective-permute-start.3) | collective-permute-done | bytes 262176 | tf_op jit(solution)/shard_map/ppermute | solution.py:24
  49.0 0.8 %finish.1 = f32[8,128,128]{2,1,0:T(8,128)} custom-call(f32[8,128,128]{2,1,0:T(8,128)S(1)} %get-tuple-element.37.kept_ref, bf16[8,128,128]{2,1,0:T(8,128)(2,1)S(1)} %collective-permute-done.3.returned_ref), custom_call_target="tpu_custom_call" | custom-call | bytes 1048576 | tf_op jit(solution)/shard_map/finish/pallas_call | solution.py:374
  (2 shorter events, 0.0 us)
Async XLA Ops:
  0.0 13.2 %collective-permute-start = (bf16[8,128,128]{2,1,0:T(8,128)(2,1)}, bf16[8,128,128]{2,1,0:T(8,128)(2,1)S(1)}, u32[]{:S(2)}, u32[]{:S(2)}) collective-permute-start(bf16[8,128,128]{2,1,0:T(8,128)(2,1)} %bitcast.11), channel_id=1, source_target_pairs={{0,16},{16,32},{32,48},{48,64},{64,80},{80,96},{96,112},{112,128},... | collective-permute-start | bytes 786440 | tf_op jit(solution)/shard_map/ppermute | solution.py:24
  2.5 19.6 %collective-permute-start.1 = (bf16[528,128]{1,0:T(8,128)(2,1)S(1)}, bf16[528,128]{1,0:T(8,128)(2,1)S(1)}, u32[]{:S(2)}, u32[]{:S(2)}) collective-permute-start(bf16[528,128]{1,0:T(8,128)(2,1)S(1)} %get-tuple-element.34), channel_id=1, source_target_pairs={{0,15},{1,14},{2,13},{3,12},{4,11},{5,10},{6,9},{7,8},{8,7},{9,6},... | collective-permute-start | bytes 405512 | tf_op jit(solution)/shard_map/ppermute | solution.py:314
  14.6 16.3 %all-to-all-start = ((bf16[16,8,16,128]{3,2,1,0:T(8,128)(2,1)}), bf16[16,8,16,128]{3,2,1,0:T(8,128)(2,1)S(1)}, u32[]{:S(2)}, u32[]{:S(2)}) async-start(bf16[16,8,16,128]{3,2,1,0:T(8,128)(2,1)} %planes_forward.1), calls=%async_computation | async-start | bytes 1048576 | tf_op jit(solution)/shard_map/all_to_all | solution.py:340
  22.1 2.6 %collective-permute-start.2 = (bf16[528,128]{1,0:T(8,128)(2,1)S(1)}, bf16[528,128]{1,0:T(8,128)(2,1)S(1)}, u32[]{:S(2)}, u32[]{:S(2)}) collective-permute-start(bf16[528,128]{1,0:T(8,128)(2,1)S(1)} %relay.1.later_ref.first_ref), channel_id=1, source_target_pairs={{0,496},{16,0},{32,16},{48,32},{64,48},{80,64},{96,80},{112,96},{1... | collective-permute-start | bytes 405512 | tf_op jit(solution)/shard_map/ppermute | solution.py:24
  45.1 3.9 %collective-permute-start.3 = (bf16[8,128,128]{2,1,0:T(8,128)(2,1)S(1)}, bf16[8,128,128]{2,1,0:T(8,128)(2,1)S(1)}, u32[]{:S(2)}, u32[]{:S(2)}) collective-permute-start(bf16[8,128,128]{2,1,0:T(8,128)(2,1)S(1)} %get-tuple-element.38), channel_id=1, source_target_pairs={{0,496},{16,0},{32,16},{48,32},{64,48},{80,64},{96,80},{112,96},{1... | collective-permute-start | bytes 786440 | tf_op jit(solution)/shard_map/ppermute | solution.py:24

commit v8 on v7

--- a/solution.py
+++ b/solution.py
@@ -159,25 +159,26 @@
         block = jnp.where(lax.rem(row, columns) == 0, edge, main).astype(BF16)
         for out, choice in ((low, LOW), (high, HIGH)):
             out[...] = dot(block, mirror_ref[choice])
-        row = lax.broadcasted_iota(jnp.int32, (SPARE, length), 0)
+        lane = lax.broadcasted_iota(jnp.int32, (SPARE, length), 1)
         main, edge = main_ref[packed:].astype(F32), edge_ref[packed:].astype(F32)
-        zero[...] = jnp.where(row == 0, edge, main)
+        zero[...] = jnp.where(lax.rem(lane, columns) == 0, edge, main)
 
     pl.when(odd == 0)(lambda: spread(first_ref, second_ref))
     pl.when(odd == 1)(lambda: spread(second_ref, first_ref))
-    zeros = zero[...].astype(BF16)
     slot = lax.broadcasted_iota(jnp.int32, (length, length), 1)
-    row = lax.broadcasted_iota(jnp.int32, (SPARE, length), 0)
-    first = lax.broadcasted_iota(jnp.int32, (SPARE, length), 1) == 0
+    plane = lax.broadcasted_iota(jnp.int32, (length, length), 0)
+    share = length // columns
+    pick = lax.broadcasted_iota(jnp.int32, (length, SPARE), 1)
+    pick = lax.broadcasted_iota(jnp.int32, (length, SPARE), 0) // share == pick
+    zeros = dot(pick.astype(F32).astype(BF16), zero[...].astype(BF16))
     for c in range(columns):
         source = (columns - c) % columns
         other = jnp.concatenate(
             [part[pl.ds(source, half, stride=columns), :] for part in (low, high)], axis=0
         )
-        chosen = ((row == source) & first).astype(F32).astype(BF16)
-        other = other + lax.dot_general(
-            zeros, chosen, (((0,), (0,)), ((), ())), preferred_element_type=F32
-        )
+        chosen = jnp.where(slot == plane % share * columns + source, zeros, 0.0)
+        chosen = jnp.sum(chosen, axis=1, keepdims=True)
+        other = other + jnp.where(slot == 0, chosen, 0.0)
         other = dot(mirror_ref[FLIP], other.astype(BF16))
         here = here_ref[pl.ds(c, length, stride=columns), :]
         here = jnp.where(slot <= half, here, pltpu.roll(here, half, 1))
@@ -186,7 +187,6 @@
 
 def prepare(first, own_ref, kernel_ref, table_ref, *refs):
     own_out, kernel_out, table_out, packed_out, sems = refs[-5:]
-
     band = lax.axis_index("band")
     early = (lax.rem(band, 2) == 1) & (band < lax.axis_size("band") - 1)
 
@@ -199,11 +199,7 @@
 
     @pl.when(early == first)
     def _():
-        pairs = (
-            (kernel_ref, kernel_out),
-            (own_ref, own_out),
-            (table_ref, table_out),
-        )
+        pairs = ((kernel_ref, kernel_out), (own_ref, own_out), (table_ref, table_out))
         copies = [pltpu.make_async_copy(a, b, sems.at[i]) for i, (a, b) in enumerate(pairs)]
         for copy in copies:
             copy.start()
@@ -217,14 +213,16 @@
             lane < half, pltpu.roll(kernel_out[:packed], half, 1), kernel_out[packed:]
         ).astype(BF16)
         row = lax.broadcasted_iota(jnp.int32, (SPARE, length), 0)
-        first = lax.broadcasted_iota(jnp.int32, (SPARE, length), 1) == 0
+        lowest = lax.broadcasted_iota(jnp.int32, (SPARE, length), 1) == 0
+        line = lax.dot_general(
+            lowest.astype(F32).astype(BF16),
+            kernel_out[...].astype(BF16),
+            (((1,), (1,)), ((), ())),
+            preferred_element_type=F32,
+        )
         zeros = jnp.zeros((SPARE, length), F32)
-        for c in range(columns):
-            plane = kernel_out[pl.ds(c, length, stride=columns), :].astype(BF16)
-            chosen = ((row == c) & first).astype(F32).astype(BF16)
-            zeros = zeros + lax.dot_general(
-                chosen, plane, (((1,), (1,)), ((), ())), preferred_element_type=F32
-            )
+        for j in range(columns):
+            zeros = jnp.where(row == j, line[:, j * length : (j + 1) * length], zeros)
         packed_out[packed:] = zeros.astype(BF16)
         for copy in copies[1:]:
             copy.wait()

time: 50.2 us -> 50.3 us (level)
  no operation moved by 1% of the time
where the time goes in v8:
time: 50.3 us; the launch traced here: 50 us
  waiting for transfers between devices  15.7 us (31%)
  starting transfers between devices  14.6 us (29%)
  blocking collectives  13.1 us (26%)
  Pallas kernels  6.53 us (13%)
    all_to_all x1, blocking collectives, per_device(): lax.all_to_all(spectrum, 'fft', split_axis=0, concat_axis=0, tiled=True)  13.1 us
    ppermute x3, waiting for transfers between devices, from_behind(): lax.ppermute(shard, axis, [(i, (i + by) % devices) for i in range(devices)])  10.4 us
    all_to_all x1, starting transfers between devices, per_device(): lax.all_to_all(spectrum, 'fft', split_axis=0, concat_axis=0, tiled=True)  7.49 us
    ppermute x1, starting transfers between devices, per_device(): there = lax.ppermute(packed, ('band', 'fft'), swap)  5.85 us
    all_to_all x1, waiting for transfers between devices, per_device(): lax.all_to_all(spectrum, 'fft', split_axis=0, concat_axis=0, tiled=True)  5.36 us
    pallas_call x1, Pallas kernels, per_device(): call(planes_forward, pltpu.HBM(lines.shape, lines.dtype), [pltpu.VMEM(lin...  1.32 us
    ppermute x3, starting transfers between devices, from_behind(): lax.ppermute(shard, axis, [(i, (i + by) % devices) for i in range(devices)])  1.27 us
    pallas_call x1, Pallas kernels, per_device(): call(functools.partial(prepare, False), results, [pltpu.SemaphoreType.DMA...  1.26 us
  transfers between devices with their start and end apart: 5, of which 4 were waited for; matrix products, arithmetic and copies ran while one was open for 0% of the time, Pallas kernels for 9%

profile of v8, /device:TPU:2, one launch (start us, length us, event | category | flops | bytes accessed | tf_op | source)
XLA Modules:
  0.0 50.0 jit_solution(4586455534458889463)
XLA Ops:
  0.0 1.1 %collective-permute-start = (bf16[8,128,128]{2,1,0:T(8,128)(2,1)}, bf16[8,128,128]{2,1,0:T(8,128)(2,1)S(1)}, u32[]{:S(2)}, u32[]{:S(2)}) collective-permute-start(bf16[8,128,128]{2,1,0:T(8,128)(2,1)} %bitcast.11), channel_id=1, source_target_pairs={{0,16},{16,32},{32,48},{48,64},{64,80},{80,96},{96,112},{112,128},... | collective-permute-start | bytes 786440 | tf_op jit(solution)/shard_map/ppermute | solution.py:24
  1.1 1.3 %prepare.3 = (bf16[8,128,128]{2,1,0:T(8,128)(2,1)S(1)}, f32[1024,128]{1,0:T(8,128)S(1)}, bf16[2,256,256]{2,1,0:T(8,128)(2,1)S(1)}, bf16[528,128]{1,0:T(8,128)(2,1)S(1)}) custom-call(bf16[8,128,128]{2,1,0:T(8,128)(2,1)} %bitcast.12, f32[1024,128]{1,0:T(8,128)} %bitcast.9, ...), custom_call_target="tpu_custom_call", output_to_operand_aliasing={{0}: (3, {}), {1}: (4, {}), {2}: (5, {}), {3}: (6, {})} | custom-call | bytes 1048576 | tf_op jit(solution)/shard_map/prepare/pallas_call | solution.py:298
  2.4 5.8 %collective-permute-start.1 = (bf16[528,128]{1,0:T(8,128)(2,1)S(1)}, bf16[528,128]{1,0:T(8,128)(2,1)S(1)}, u32[]{:S(2)}, u32[]{:S(2)}) collective-permute-start(bf16[528,128]{1,0:T(8,128)(2,1)S(1)} %get-tuple-element.34), channel_id=1, source_target_pairs={{0,15},{1,14},{2,13},{3,12},{4,11},{5,10},{6,9},{7,8},{8,7},{9,6},... | collective-permute-start | bytes 405512 | tf_op jit(solution)/shard_map/ppermute | solution.py:312
  8.2 5.0 %collective-permute-done.other_ref = bf16[8,128,128]{2,1,0:T(8,128)(2,1)S(1)} collective-permute-done((bf16[8,128,128]{2,1,0:T(8,128)(2,1)}, bf16[8,128,128]{2,1,0:T(8,128)(2,1)S(1)}, u32[]{:S(2)}, u32[]{:S(2)}) %collective-permute-start) | collective-permute-done | bytes 262176 | tf_op jit(solution)/shard_map/ppermute | solution.py:24
  13.3 1.3 %planes_forward.1 = bf16[16,8,16,128]{3,2,1,0:T(8,128)(2,1)} custom-call(bf16[8,128,128]{2,1,0:T(8,128)(2,1)S(1)} %get-tuple-element.30.own_ref, bf16[8,128,128]{2,1,0:T(8,128)(2,1)S(1)} %collective-permute-done.other_ref, bf16[2,256,256]{2,1,0:T(8,128)(2,1)S(1)} %get-tuple-element.32.table_ref), custom_call_target="tpu_custom_call" | custom-call | bytes 1048576 | tf_op jit(solution)/shard_map/planes_forward/pallas_call | solution.py:329
  14.6 7.5 %all-to-all-start = ((bf16[16,8,16,128]{3,2,1,0:T(8,128)(2,1)}), bf16[16,8,16,128]{3,2,1,0:T(8,128)(2,1)S(1)}, u32[]{:S(2)}, u32[]{:S(2)}) async-start(bf16[16,8,16,128]{3,2,1,0:T(8,128)(2,1)} %planes_forward.1), calls=%async_computation | async-start | bytes 1048576 | tf_op jit(solution)/shard_map/all_to_all | solution.py:338
  22.1 0.0 collective-permute-done.1.there_ref
  22.1 0.0 collective-permute-start.2
  22.1 1.1 %load.1 = (bf16[4,256,256]{2,1,0:T(8,128)(2,1)S(1)}, bf16[4,128,128]{2,1,0:T(8,128)(2,1)S(1)}) custom-call(bf16[528,128]{1,0:T(8,128)(2,1)S(1)} %relay.1.later_ref.first_ref, bf16[4,256,256]{2,1,0:T(8,128)(2,1)} %constant.7.clone.table_ref, bf16[4,128,128]{2,1,0:T(8,128)(2,1)} %constant.8.clone.mirror_ref), custom_call_target="tpu_custom_call" | custom-call | bytes 1048576 | tf_op jit(solution)/shard_map/load/pallas_call | solution.py:320
  23.2 1.5 %collective-permute-done.2.second_ref = bf16[528,128]{1,0:T(8,128)(2,1)S(1)} collective-permute-done((bf16[528,128]{1,0:T(8,128)(2,1)S(1)}, bf16[528,128]{1,0:T(8,128)(2,1)S(1)}, u32[]{:S(2)}, u32[]{:S(2)}) %collective-permute-start.2) | collective-permute-done | bytes 135200 | tf_op jit(solution)/shard_map/ppermute | solution.py:24
  24.7 0.8 %symmetric_kernel.1.screen_ref = f32[8,128,128]{2,1,0:T(8,128)S(1)} custom-call(f32[1024,128]{1,0:T(8,128)S(1)} %get-tuple-element.33.here_ref, bf16[528,128]{1,0:T(8,128)(2,1)S(1)} %relay.1.later_ref.first_ref, bf16[528,128]{1,0:T(8,128)(2,1)S(1)} %collective-permute-done.2.second_ref, bf16[4,128,128]{2,1,0:T(8,128)(2,1)S(1)} %get-tuple-element.35.mirror_ref), custom_call_target="tpu_custom_call" | custom-call | flops 134217728 | bytes 1048576 | tf_op jit(solution)/shard_map/symmetric_kernel/pallas_call | solution.py:339
  25.5 5.4 %all-to-all-done = bf16[16,8,16,128]{3,2,1,0:T(8,128)(2,1)S(1)} async-done(((bf16[16,8,16,128]{3,2,1,0:T(8,128)(2,1)}), bf16[16,8,16,128]{3,2,1,0:T(8,128)(2,1)S(1)}, u32[]{:S(2)}, u32[]{:S(2)}) %all-to-all-start) | async-done | bytes 524320 | tf_op jit(solution)/shard_map/all_to_all | solution.py:338
  30.8 0.6 %columns_filter.1 = bf16[128,16,128]{2,1,0:T(8,128)(2,1)S(1)} custom-call(bf16[128,16,128]{2,1,0:T(8,128)(2,1)S(1)} %bitcast.6, f32[8,128,128]{2,1,0:T(8,128)S(1)} %symmetric_kernel.1.screen_ref, bf16[4,256,256]{2,1,0:T(8,128)(2,1)S(1)} %get-tuple-element.36.table_ref), custom_call_target="tpu_custom_call" | custom-call | flops 268435456 | bytes 1048576 | tf_op jit(solution)/shard_map/columns_filter/pallas_call | solution.py:349
  31.5 13.1 %all_to_all.10.line_ref = bf16[16,8,16,128]{3,2,1,0:T(8,128)(2,1)S(1)} all-to-all(bf16[16,8,16,128]{3,2,1,0:T(8,128)(2,1)S(1)} %bitcast.7), channel_id=1, replica_groups=mesh['band'=32,'fft'=16] {'fft'}, dimensions={0} | all-to-all | bytes 1048576 | tf_op jit(solution)/shard_map/all_to_all | solution.py:361
  44.6 0.6 %planes_back.1 = (f32[8,128,128]{2,1,0:T(8,128)S(1)}, bf16[8,128,128]{2,1,0:T(8,128)(2,1)S(1)}) custom-call(bf16[16,8,16,128]{3,2,1,0:T(8,128)(2,1)S(1)} %all_to_all.10.line_ref, bf16[8,128,128]{2,1,0:T(8,128)(2,1)S(1)} %get-tuple-element.30.own_ref, bf16[8,128,128]{2,1,0:T(8,128)(2,1)S(1)} %collective-permute-done.other_ref, ...), custom_call_target="tpu_custom_call" | custom-call | flops 268435456 | bytes 1048576 | tf_op jit(solution)/shard_map/planes_back/pallas_call | solution.py:362
  45.1 0.2 collective-permute-start.3
  45.3 3.9 %collective-permute-done.3.returned_ref = bf16[8,128,128]{2,1,0:T(8,128)(2,1)S(1)} collective-permute-done((bf16[8,128,128]{2,1,0:T(8,128)(2,1)S(1)}, bf16[8,128,128]{2,1,0:T(8,128)(2,1)S(1)}, u32[]{:S(2)}, u32[]{:S(2)}) %collective-permute-start.3) | collective-permute-done | bytes 262176 | tf_op jit(solution)/shard_map/ppermute | solution.py:24
  49.2 0.8 %finish.1 = f32[8,128,128]{2,1,0:T(8,128)} custom-call(f32[8,128,128]{2,1,0:T(8,128)S(1)} %get-tuple-element.37.kept_ref, bf16[8,128,128]{2,1,0:T(8,128)(2,1)S(1)} %collective-permute-done.3.returned_ref), custom_call_target="tpu_custom_call" | custom-call | bytes 1048576 | tf_op jit(solution)/shard_map/finish/pallas_call | solution.py:372
  (2 shorter events, 0.0 us)
Async XLA Ops:
  0.0 13.2 %collective-permute-start = (bf16[8,128,128]{2,1,0:T(8,128)(2,1)}, bf16[8,128,128]{2,1,0:T(8,128)(2,1)S(1)}, u32[]{:S(2)}, u32[]{:S(2)}) collective-permute-start(bf16[8,128,128]{2,1,0:T(8,128)(2,1)} %bitcast.11), channel_id=1, source_target_pairs={{0,16},{16,32},{32,48},{48,64},{64,80},{80,96},{96,112},{112,128},... | collective-permute-start | bytes 786440 | tf_op jit(solution)/shard_map/ppermute | solution.py:24
  2.4 19.7 %collective-permute-start.1 = (bf16[528,128]{1,0:T(8,128)(2,1)S(1)}, bf16[528,128]{1,0:T(8,128)(2,1)S(1)}, u32[]{:S(2)}, u32[]{:S(2)}) collective-permute-start(bf16[528,128]{1,0:T(8,128)(2,1)S(1)} %get-tuple-element.34), channel_id=1, source_target_pairs={{0,15},{1,14},{2,13},{3,12},{4,11},{5,10},{6,9},{7,8},{8,7},{9,6},... | collective-permute-start | bytes 405512 | tf_op jit(solution)/shard_map/ppermute | solution.py:312
  14.6 16.3 %all-to-all-start = ((bf16[16,8,16,128]{3,2,1,0:T(8,128)(2,1)}), bf16[16,8,16,128]{3,2,1,0:T(8,128)(2,1)S(1)}, u32[]{:S(2)}, u32[]{:S(2)}) async-start(bf16[16,8,16,128]{3,2,1,0:T(8,128)(2,1)} %planes_forward.1), calls=%async_computation | async-start | bytes 1048576 | tf_op jit(solution)/shard_map/all_to_all | solution.py:338
  22.1 2.6 %collective-permute-start.2 = (bf16[528,128]{1,0:T(8,128)(2,1)S(1)}, bf16[528,128]{1,0:T(8,128)(2,1)S(1)}, u32[]{:S(2)}, u32[]{:S(2)}) collective-permute-start(bf16[528,128]{1,0:T(8,128)(2,1)S(1)} %relay.1.later_ref.first_ref), channel_id=1, source_target_pairs={{0,496},{16,0},{32,16},{48,32},{64,48},{80,64},{96,80},{112,96},{1... | collective-permute-start | bytes 405512 | tf_op jit(solution)/shard_map/ppermute | solution.py:24
  45.1 4.1 %collective-permute-start.3 = (bf16[8,128,128]{2,1,0:T(8,128)(2,1)S(1)}, bf16[8,128,128]{2,1,0:T(8,128)(2,1)S(1)}, u32[]{:S(2)}, u32[]{:S(2)}) collective-permute-start(bf16[8,128,128]{2,1,0:T(8,128)(2,1)S(1)} %get-tuple-element.38), channel_id=1, source_target_pairs={{0,496},{16,0},{32,16},{48,32},{64,48},{80,64},{96,80},{112,96},{1... | collective-permute-start | bytes 786440 | tf_op jit(solution)/shard_map/ppermute | solution.py:24

commit v9 on v6

--- a/solution.py
+++ b/solution.py
@@ -120,27 +120,38 @@
     out_ref[...] = jnp.swapaxes(sent[...], 0, 1)
 
 
-def planes_back(line_ref, own_ref, other_ref, table_ref, kept_ref, sent_ref):
+def back_along_y(line_ref, table_ref, x):
+    length = line_ref.shape[3]
+    field = jnp.concatenate(
+        [line_ref[:, x + j].reshape(2 * length, length) for j in range(2)], axis=1
+    )
+    field = dot(table_ref[BACK_SORTED], field).astype(BF16)
+    return jnp.concatenate(
+        [
+            jnp.concatenate([field[:length, :length], field[length:, :length]], axis=1),
+            jnp.concatenate([field[:length, length:], field[length:, length:]], axis=1),
+        ],
+        axis=0,
+    )
+
+
+def planes_sent(line_ref, own_ref, table_ref, sent_ref):
     planes, length = own_ref.shape[0], own_ref.shape[1]
     for x in range(0, planes, 2):
-        field = jnp.concatenate(
-            [line_ref[:, x + j].reshape(2 * length, length) for j in range(2)], axis=1
-        )
-        field = dot(table_ref[BACK_SORTED], field).astype(BF16)
-        field = jnp.concatenate(
-            [
-                jnp.concatenate([field[:length, :length], field[length:, :length]], axis=1),
-                jnp.concatenate([field[:length, length:], field[length:, length:]], axis=1),
-            ],
-            axis=0,
-        )
-        field = dot(field, table_ref[DEZ])
+        field = back_along_y(line_ref, table_ref, x)
+        field = dot(field, table_ref[DEZ])[:, length:]
+        own = own_ref[x : x + 2].astype(F32).reshape(2 * length, length)
+        sent_ref[x : x + 2] = (field * own).astype(BF16).reshape(2, length, length)
+
+
+def planes_kept(line_ref, own_ref, other_ref, table_ref, kept_ref):
+    planes, length = own_ref.shape[0], own_ref.shape[1]
+    for x in range(0, planes, 2):
+        field = dot(back_along_y(line_ref, table_ref, x), table_ref[DEZ])
         own = own_ref[x : x + 2].astype(F32).reshape(2 * length, length)
         other = other_ref[x : x + 2].astype(F32).reshape(2 * length, length)
         kept = field[:, :length] * own + field[:, length:] * other
-        sent = (field[:, length:] * own).astype(BF16)
         kept_ref[x : x + 2] = kept.reshape(2, length, length)
-        sent_ref[x : x + 2] = sent.reshape(2, length, length)
 
 
 def relay(there_ref, out_ref):
@@ -361,16 +372,19 @@
     )
     spectrum = spectrum.reshape(groups, planes, 2 * columns, length)
     spectrum = lax.all_to_all(spectrum, "fft", split_axis=0, concat_axis=0, tiled=True)
-    kept, sent = call(
-        planes_back,
-        (
-            jax.ShapeDtypeStruct(own.shape, F32),
-            jax.ShapeDtypeStruct(own.shape, BF16),
-        ),
+    sent = call(
+        planes_sent,
+        jax.ShapeDtypeStruct(own.shape, BF16),
+        flops=work,
+        name="planes_sent",
+    )(spectrum, own, far)
+    returned = from_behind(sent, "band", -1)
+    kept = call(
+        planes_kept,
+        jax.ShapeDtypeStruct(own.shape, F32),
         flops=2 * work,
-        name="planes_back",
+        name="planes_kept",
     )(spectrum, own, other, far)
-    returned = from_behind(sent, "band", -1)
     total = call(
         finish,
         jax.ShapeDtypeStruct(kept.shape, F32),

time: 50.2 us -> 50.2 us (level)
  waiting for transfers between devices: 15.7 us -> 15.1 us
  Pallas kernels: 6.52 us -> 7.09 us
    ppermute x3, waiting for transfers between devices: 10.2 us -> 9.65 us  [from_behind(): lax.ppermute(shard, axis, [(i, (i + by) % devices) for i in range(devices)])]
    pallas_call x1 -> x2, Pallas kernels: 0.58 us -> 1.15 us  [the longest x1 0.57 us: per_device(): call(planes_kept, jax.ShapeDtypeStruct(own.shape, F32), flops=2 * work, n...]
  transfers between devices with their start and end apart: 5 -> 5, of which waited for: 4 -> 4; matrix products, arithmetic and copies ran while one was open for 0% -> 0% of each run, Pallas kernels for 9% -> 10%
where the time goes in v9:
time: 50.2 us; the launch traced here: 49.9 us
  waiting for transfers between devices  15.1 us (30%)
  starting transfers between devices  14.6 us (29%)
  blocking collectives  13.1 us (26%)
  Pallas kernels  7.09 us (14%)
    all_to_all x1, blocking collectives, per_device(): lax.all_to_all(spectrum, 'fft', split_axis=0, concat_axis=0, tiled=True)  13.1 us
    ppermute x3, waiting for transfers between devices, from_behind(): lax.ppermute(shard, axis, [(i, (i + by) % devices) for i in range(devices)])  9.65 us
    all_to_all x1, starting transfers between devices, per_device(): lax.all_to_all(spectrum, 'fft', split_axis=0, concat_axis=0, tiled=True)  7.49 us
    ppermute x1, starting transfers between devices, per_device(): there = lax.ppermute(packed, ('band', 'fft'), swap)  5.85 us
    all_to_all x1, waiting for transfers between devices, per_device(): lax.all_to_all(spectrum, 'fft', split_axis=0, concat_axis=0, tiled=True)  5.43 us
    pallas_call x1, Pallas kernels, per_device(): call(functools.partial(prepare, False), results, [pltpu.SemaphoreType.DMA...  1.33 us
    pallas_call x1, Pallas kernels, per_device(): call(planes_forward, pltpu.HBM(lines.shape, lines.dtype), [pltpu.VMEM(lin...  1.32 us
    ppermute x3, starting transfers between devices, from_behind(): lax.ppermute(shard, axis, [(i, (i + by) % devices) for i in range(devices)])  1.24 us
  transfers between devices with their start and end apart: 5, of which 4 were waited for; matrix products, arithmetic and copies ran while one was open for 0% of the time, Pallas kernels for 10%

profile of v9, /device:TPU:2, one launch (start us, length us, event | category | flops | bytes accessed | tf_op | source)
XLA Modules:
  0.0 49.9 jit_solution(11198307970783944918)
XLA Ops:
  0.0 1.1 %collective-permute-start = (bf16[8,128,128]{2,1,0:T(8,128)(2,1)}, bf16[8,128,128]{2,1,0:T(8,128)(2,1)S(1)}, u32[]{:S(2)}, u32[]{:S(2)}) collective-permute-start(bf16[8,128,128]{2,1,0:T(8,128)(2,1)} %bitcast.11), channel_id=1, source_target_pairs={{0,16},{16,32},{32,48},{48,64},{64,80},{80,96},{96,112},{112,128},... | collective-permute-start | bytes 786440 | tf_op jit(solution)/shard_map/ppermute | solution.py:24
  1.2 1.3 %prepare.3 = (bf16[8,128,128]{2,1,0:T(8,128)(2,1)S(1)}, f32[1024,128]{1,0:T(8,128)S(1)}, bf16[2,256,256]{2,1,0:T(8,128)(2,1)S(1)}, bf16[528,128]{1,0:T(8,128)(2,1)S(1)}) custom-call(bf16[8,128,128]{2,1,0:T(8,128)(2,1)} %bitcast.12, f32[1024,128]{1,0:T(8,128)} %bitcast.9, ...), custom_call_target="tpu_custom_call", output_to_operand_aliasing={{0}: (3, {}), {1}: (4, {}), {2}: (5, {}), {3}: (6, {})} | custom-call | bytes 1048576 | tf_op jit(solution)/shard_map/prepare/pallas_call | solution.py:311
  2.5 5.8 %collective-permute-start.1 = (bf16[528,128]{1,0:T(8,128)(2,1)S(1)}, bf16[528,128]{1,0:T(8,128)(2,1)S(1)}, u32[]{:S(2)}, u32[]{:S(2)}) collective-permute-start(bf16[528,128]{1,0:T(8,128)(2,1)S(1)} %get-tuple-element.32), channel_id=1, source_target_pairs={{0,15},{1,14},{2,13},{3,12},{4,11},{5,10},{6,9},{7,8},{8,7},{9,6},... | collective-permute-start | bytes 405512 | tf_op jit(solution)/shard_map/ppermute | solution.py:325
  8.4 4.9 %collective-permute-done.other_ref = bf16[8,128,128]{2,1,0:T(8,128)(2,1)S(1)} collective-permute-done((bf16[8,128,128]{2,1,0:T(8,128)(2,1)}, bf16[8,128,128]{2,1,0:T(8,128)(2,1)S(1)}, u32[]{:S(2)}, u32[]{:S(2)}) %collective-permute-start) | collective-permute-done | bytes 262176 | tf_op jit(solution)/shard_map/ppermute | solution.py:24
  13.3 1.3 %planes_forward.1 = bf16[16,8,16,128]{3,2,1,0:T(8,128)(2,1)} custom-call(bf16[8,128,128]{2,1,0:T(8,128)(2,1)S(1)} %get-tuple-element.28.own_ref, bf16[8,128,128]{2,1,0:T(8,128)(2,1)S(1)} %collective-permute-done.other_ref, bf16[2,256,256]{2,1,0:T(8,128)(2,1)S(1)} %get-tuple-element.30.table_ref), custom_call_target="tpu_custom_call" | custom-call | bytes 1048576 | tf_op jit(solution)/shard_map/planes_forward/pallas_call | solution.py:342
  14.6 7.5 %all-to-all-start = ((bf16[16,8,16,128]{3,2,1,0:T(8,128)(2,1)}), bf16[16,8,16,128]{3,2,1,0:T(8,128)(2,1)S(1)}, u32[]{:S(2)}, u32[]{:S(2)}) async-start(bf16[16,8,16,128]{3,2,1,0:T(8,128)(2,1)} %planes_forward.1), calls=%async_computation | async-start | bytes 1048576 | tf_op jit(solution)/shard_map/all_to_all | solution.py:351
  22.1 0.0 collective-permute-done.1.there_ref
  22.1 0.0 collective-permute-start.2
  22.1 1.1 %load.1 = (bf16[4,256,256]{2,1,0:T(8,128)(2,1)S(1)}, bf16[4,128,128]{2,1,0:T(8,128)(2,1)S(1)}) custom-call(bf16[528,128]{1,0:T(8,128)(2,1)S(1)} %relay.1.later_ref.first_ref, bf16[4,256,256]{2,1,0:T(8,128)(2,1)} %constant.7.clone.table_ref, bf16[4,128,128]{2,1,0:T(8,128)(2,1)} %constant.8.clone.mirror_ref), custom_call_target="tpu_custom_call" | custom-call | bytes 1048576 | tf_op jit(solution)/shard_map/load/pallas_call | solution.py:333
  23.2 1.5 %collective-permute-done.2.second_ref = bf16[528,128]{1,0:T(8,128)(2,1)S(1)} collective-permute-done((bf16[528,128]{1,0:T(8,128)(2,1)S(1)}, bf16[528,128]{1,0:T(8,128)(2,1)S(1)}, u32[]{:S(2)}, u32[]{:S(2)}) %collective-permute-start.2) | collective-permute-done | bytes 135200 | tf_op jit(solution)/shard_map/ppermute | solution.py:24
  24.7 0.7 %symmetric_kernel.1.screen_ref = f32[8,128,128]{2,1,0:T(8,128)S(1)} custom-call(f32[1024,128]{1,0:T(8,128)S(1)} %get-tuple-element.31.here_ref, bf16[528,128]{1,0:T(8,128)(2,1)S(1)} %relay.1.later_ref.first_ref, bf16[528,128]{1,0:T(8,128)(2,1)S(1)} %collective-permute-done.2.second_ref, bf16[4,128,128]{2,1,0:T(8,128)(2,1)S(1)} %get-tuple-element.33.mirror_ref), custom_call_target="tpu_custom_call" | custom-call | flops 134217728 | bytes 1048576 | tf_op jit(solution)/shard_map/symmetric_kernel/pallas_call | solution.py:352
  25.4 5.4 %all-to-all-done = bf16[16,8,16,128]{3,2,1,0:T(8,128)(2,1)S(1)} async-done(((bf16[16,8,16,128]{3,2,1,0:T(8,128)(2,1)}), bf16[16,8,16,128]{3,2,1,0:T(8,128)(2,1)S(1)}, u32[]{:S(2)}, u32[]{:S(2)}) %all-to-all-start) | async-done | bytes 524320 | tf_op jit(solution)/shard_map/all_to_all | solution.py:351
  30.8 0.6 %columns_filter.1 = bf16[128,16,128]{2,1,0:T(8,128)(2,1)S(1)} custom-call(bf16[128,16,128]{2,1,0:T(8,128)(2,1)S(1)} %bitcast.6, f32[8,128,128]{2,1,0:T(8,128)S(1)} %symmetric_kernel.1.screen_ref, bf16[4,256,256]{2,1,0:T(8,128)(2,1)S(1)} %get-tuple-element.34.table_ref), custom_call_target="tpu_custom_call" | custom-call | flops 268435456 | bytes 1048576 | tf_op jit(solution)/shard_map/columns_filter/pallas_call | solution.py:362
  31.5 13.1 %all_to_all.10.line_ref = bf16[16,8,16,128]{3,2,1,0:T(8,128)(2,1)S(1)} all-to-all(bf16[16,8,16,128]{3,2,1,0:T(8,128)(2,1)S(1)} %bitcast.7), channel_id=1, replica_groups=mesh['band'=32,'fft'=16] {'fft'}, dimensions={0} | all-to-all | bytes 1048576 | tf_op jit(solution)/shard_map/all_to_all | solution.py:374
  44.6 0.6 %planes_sent.1 = bf16[8,128,128]{2,1,0:T(8,128)(2,1)S(1)} custom-call(bf16[16,8,16,128]{3,2,1,0:T(8,128)(2,1)S(1)} %all_to_all.10.line_ref, bf16[8,128,128]{2,1,0:T(8,128)(2,1)S(1)} %get-tuple-element.28.own_ref, bf16[4,256,256]{2,1,0:T(8,128)(2,1)S(1)} %get-tuple-element.34.table_ref), custom_call_target="tpu_custom_call" | custom-call | flops 134217728 | bytes 1048576 | tf_op jit(solution)/shard_map/planes_sent/pallas_call | solution.py:375
  45.1 0.1 collective-permute-start.3
  45.2 0.6 %planes_kept.1.kept_ref = f32[8,128,128]{2,1,0:T(8,128)S(1)} custom-call(bf16[16,8,16,128]{3,2,1,0:T(8,128)(2,1)S(1)} %all_to_all.10.line_ref, bf16[8,128,128]{2,1,0:T(8,128)(2,1)S(1)} %get-tuple-element.28.own_ref, bf16[8,128,128]{2,1,0:T(8,128)(2,1)S(1)} %collective-permute-done.other_ref, bf16[4,256,256]{2,1,0:T(8,128)(2,1)S(1)} %get-tuple-element.34.table_ref), custom_call_target="tpu_custom_call" | custom-call | flops 268435456 | bytes 1048576 | tf_op jit(solution)/shard_map/planes_kept/pallas_call | solution.py:382
  45.8 3.3 %collective-permute-done.3.returned_ref = bf16[8,128,128]{2,1,0:T(8,128)(2,1)S(1)} collective-permute-done((bf16[8,128,128]{2,1,0:T(8,128)(2,1)S(1)}, bf16[8,128,128]{2,1,0:T(8,128)(2,1)S(1)}, u32[]{:S(2)}, u32[]{:S(2)}) %collective-permute-start.3) | collective-permute-done | bytes 262176 | tf_op jit(solution)/shard_map/ppermute | solution.py:24
  49.1 0.8 %finish.1 = f32[8,128,128]{2,1,0:T(8,128)} custom-call(f32[8,128,128]{2,1,0:T(8,128)S(1)} %planes_kept.1.kept_ref, bf16[8,128,128]{2,1,0:T(8,128)(2,1)S(1)} %collective-permute-done.3.returned_ref), custom_call_target="tpu_custom_call" | custom-call | bytes 1048576 | tf_op jit(solution)/shard_map/finish/pallas_call | solution.py:388
  (2 shorter events, 0.0 us)
Async XLA Ops:
  0.0 13.2 %collective-permute-start = (bf16[8,128,128]{2,1,0:T(8,128)(2,1)}, bf16[8,128,128]{2,1,0:T(8,128)(2,1)S(1)}, u32[]{:S(2)}, u32[]{:S(2)}) collective-permute-start(bf16[8,128,128]{2,1,0:T(8,128)(2,1)} %bitcast.11), channel_id=1, source_target_pairs={{0,16},{16,32},{32,48},{48,64},{64,80},{80,96},{96,112},{112,128},... | collective-permute-start | bytes 786440 | tf_op jit(solution)/shard_map/ppermute | solution.py:24
  2.5 19.6 %collective-permute-start.1 = (bf16[528,128]{1,0:T(8,128)(2,1)S(1)}, bf16[528,128]{1,0:T(8,128)(2,1)S(1)}, u32[]{:S(2)}, u32[]{:S(2)}) collective-permute-start(bf16[528,128]{1,0:T(8,128)(2,1)S(1)} %get-tuple-element.32), channel_id=1, source_target_pairs={{0,15},{1,14},{2,13},{3,12},{4,11},{5,10},{6,9},{7,8},{8,7},{9,6},... | collective-permute-start | bytes 405512 | tf_op jit(solution)/shard_map/ppermute | solution.py:325
  14.6 16.3 %all-to-all-start = ((bf16[16,8,16,128]{3,2,1,0:T(8,128)(2,1)}), bf16[16,8,16,128]{3,2,1,0:T(8,128)(2,1)S(1)}, u32[]{:S(2)}, u32[]{:S(2)}) async-start(bf16[16,8,16,128]{3,2,1,0:T(8,128)(2,1)} %planes_forward.1), calls=%async_computation | async-start | bytes 1048576 | tf_op jit(solution)/shard_map/all_to_all | solution.py:351
  22.1 2.6 %collective-permute-start.2 = (bf16[528,128]{1,0:T(8,128)(2,1)S(1)}, bf16[528,128]{1,0:T(8,128)(2,1)S(1)}, u32[]{:S(2)}, u32[]{:S(2)}) collective-permute-start(bf16[528,128]{1,0:T(8,128)(2,1)S(1)} %relay.1.later_ref.first_ref), channel_id=1, source_target_pairs={{0,496},{16,0},{32,16},{48,32},{64,48},{80,64},{96,80},{112,96},{1... | collective-permute-start | bytes 405512 | tf_op jit(solution)/shard_map/ppermute | solution.py:24
  45.1 4.0 %collective-permute-start.3 = (bf16[8,128,128]{2,1,0:T(8,128)(2,1)S(1)}, bf16[8,128,128]{2,1,0:T(8,128)(2,1)S(1)}, u32[]{:S(2)}, u32[]{:S(2)}) collective-permute-start(bf16[8,128,128]{2,1,0:T(8,128)(2,1)S(1)} %planes_sent.1), channel_id=1, source_target_pairs={{0,496},{16,0},{32,16},{48,32},{64,48},{80,64},{96,80},{112,96},{1... | collective-permute-start | bytes 786440 | tf_op jit(solution)/shard_map/ppermute | solution.py:24

commit v10 on v9

--- a/solution.py
+++ b/solution.py
@@ -166,10 +166,10 @@
 
     def spread(main_ref, edge_ref):
         row = lax.broadcasted_iota(jnp.int32, (packed, length), 0)
+        main, edge = main_ref[:packed].astype(F32), edge_ref[:packed].astype(F32)
+        block = jnp.where(lax.rem(row, columns) == 0, edge, main).astype(BF16)
         for out, choice in ((low, LOW), (high, HIGH)):
-            main = dot(main_ref[:packed], mirror_ref[choice])
-            edge = dot(edge_ref[:packed], mirror_ref[choice])
-            out[...] = jnp.where(lax.rem(row, columns) == 0, edge, main)
+            out[...] = dot(block, mirror_ref[choice])
         row = lax.broadcasted_iota(jnp.int32, (SPARE, length), 0)
         main, edge = main_ref[packed:].astype(F32), edge_ref[packed:].astype(F32)
         zero[...] = jnp.where(row == 0, edge, main)

time: 50.2 us -> 50.2 us (level)
  no operation moved by 1% of the time
where the time goes in v10:
time: 50.2 us; the launch traced here: 49.9 us
  waiting for transfers between devices  15.1 us (30%)
  starting transfers between devices  14.5 us (29%)
  blocking collectives  13.1 us (26%)
  Pallas kernels  7.03 us (14%)
    all_to_all x1, blocking collectives, per_device(): lax.all_to_all(spectrum, 'fft', split_axis=0, concat_axis=0, tiled=True)  13.1 us
    ppermute x3, waiting for transfers between devices, from_behind(): lax.ppermute(shard, axis, [(i, (i + by) % devices) for i in range(devices)])  9.64 us
    all_to_all x1, starting transfers between devices, per_device(): lax.all_to_all(spectrum, 'fft', split_axis=0, concat_axis=0, tiled=True)  7.49 us
    ppermute x1, starting transfers between devices, per_device(): there = lax.ppermute(packed, ('band', 'fft'), swap)  5.85 us
    all_to_all x1, waiting for transfers between devices, per_device(): lax.all_to_all(spectrum, 'fft', split_axis=0, concat_axis=0, tiled=True)  5.49 us
    pallas_call x1, Pallas kernels, per_device(): call(functools.partial(prepare, False), results, [pltpu.SemaphoreType.DMA...  1.33 us
    pallas_call x1, Pallas kernels, per_device(): call(planes_forward, pltpu.HBM(lines.shape, lines.dtype), [pltpu.VMEM(lin...  1.32 us
    ppermute x3, starting transfers between devices, from_behind(): lax.ppermute(shard, axis, [(i, (i + by) % devices) for i in range(devices)])  1.18 us
  transfers between devices with their start and end apart: 5, of which 4 were waited for; matrix products, arithmetic and copies ran while one was open for 0% of the time, Pallas kernels for 10%

profile of v10, /device:TPU:2, one launch (start us, length us, event | category | flops | bytes accessed | tf_op | source)
XLA Modules:
  0.0 49.9 jit_solution(18260403535158682704)
XLA Ops:
  0.0 1.1 %collective-permute-start = (bf16[8,128,128]{2,1,0:T(8,128)(2,1)}, bf16[8,128,128]{2,1,0:T(8,128)(2,1)S(1)}, u32[]{:S(2)}, u32[]{:S(2)}) collective-permute-start(bf16[8,128,128]{2,1,0:T(8,128)(2,1)} %bitcast.11), channel_id=1, source_target_pairs={{0,16},{16,32},{32,48},{48,64},{64,80},{80,96},{96,112},{112,128},... | collective-permute-start | bytes 786440 | tf_op jit(solution)/shard_map/ppermute | solution.py:24
  1.2 1.3 %prepare.3 = (bf16[8,128,128]{2,1,0:T(8,128)(2,1)S(1)}, f32[1024,128]{1,0:T(8,128)S(1)}, bf16[2,256,256]{2,1,0:T(8,128)(2,1)S(1)}, bf16[528,128]{1,0:T(8,128)(2,1)S(1)}) custom-call(bf16[8,128,128]{2,1,0:T(8,128)(2,1)} %bitcast.12, f32[1024,128]{1,0:T(8,128)} %bitcast.9, ...), custom_call_target="tpu_custom_call", output_to_operand_aliasing={{0}: (3, {}), {1}: (4, {}), {2}: (5, {}), {3}: (6, {})} | custom-call | bytes 1048576 | tf_op jit(solution)/shard_map/prepare/pallas_call | solution.py:311
  2.5 5.8 %collective-permute-start.1 = (bf16[528,128]{1,0:T(8,128)(2,1)S(1)}, bf16[528,128]{1,0:T(8,128)(2,1)S(1)}, u32[]{:S(2)}, u32[]{:S(2)}) collective-permute-start(bf16[528,128]{1,0:T(8,128)(2,1)S(1)} %get-tuple-element.32), channel_id=1, source_target_pairs={{0,15},{1,14},{2,13},{3,12},{4,11},{5,10},{6,9},{7,8},{8,7},{9,6},... | collective-permute-start | bytes 405512 | tf_op jit(solution)/shard_map/ppermute | solution.py:325
  8.4 4.9 %collective-permute-done.other_ref = bf16[8,128,128]{2,1,0:T(8,128)(2,1)S(1)} collective-permute-done((bf16[8,128,128]{2,1,0:T(8,128)(2,1)}, bf16[8,128,128]{2,1,0:T(8,128)(2,1)S(1)}, u32[]{:S(2)}, u32[]{:S(2)}) %collective-permute-start) | collective-permute-done | bytes 262176 | tf_op jit(solution)/shard_map/ppermute | solution.py:24
  13.3 1.3 %planes_forward.1 = bf16[16,8,16,128]{3,2,1,0:T(8,128)(2,1)} custom-call(bf16[8,128,128]{2,1,0:T(8,128)(2,1)S(1)} %get-tuple-element.28.own_ref, bf16[8,128,128]{2,1,0:T(8,128)(2,1)S(1)} %collective-permute-done.other_ref, bf16[2,256,256]{2,1,0:T(8,128)(2,1)S(1)} %get-tuple-element.30.table_ref), custom_call_target="tpu_custom_call" | custom-call | bytes 1048576 | tf_op jit(solution)/shard_map/planes_forward/pallas_call | solution.py:342
  14.6 7.5 %all-to-all-start = ((bf16[16,8,16,128]{3,2,1,0:T(8,128)(2,1)}), bf16[16,8,16,128]{3,2,1,0:T(8,128)(2,1)S(1)}, u32[]{:S(2)}, u32[]{:S(2)}) async-start(bf16[16,8,16,128]{3,2,1,0:T(8,128)(2,1)} %planes_forward.1), calls=%async_computation | async-start | bytes 1048576 | tf_op jit(solution)/shard_map/all_to_all | solution.py:351
  22.1 0.0 collective-permute-done.1.there_ref
  22.1 0.0 collective-permute-start.2
  22.1 1.1 %load.1 = (bf16[4,256,256]{2,1,0:T(8,128)(2,1)S(1)}, bf16[4,128,128]{2,1,0:T(8,128)(2,1)S(1)}) custom-call(bf16[528,128]{1,0:T(8,128)(2,1)S(1)} %relay.1.later_ref.first_ref, bf16[4,256,256]{2,1,0:T(8,128)(2,1)} %constant.7.clone.table_ref, bf16[4,128,128]{2,1,0:T(8,128)(2,1)} %constant.8.clone.mirror_ref), custom_call_target="tpu_custom_call" | custom-call | bytes 1048576 | tf_op jit(solution)/shard_map/load/pallas_call | solution.py:333
  23.2 1.5 %collective-permute-done.2.second_ref = bf16[528,128]{1,0:T(8,128)(2,1)S(1)} collective-permute-done((bf16[528,128]{1,0:T(8,128)(2,1)S(1)}, bf16[528,128]{1,0:T(8,128)(2,1)S(1)}, u32[]{:S(2)}, u32[]{:S(2)}) %collective-permute-start.2) | collective-permute-done | bytes 135200 | tf_op jit(solution)/shard_map/ppermute | solution.py:24
  24.7 0.7 %symmetric_kernel.1.screen_ref = f32[8,128,128]{2,1,0:T(8,128)S(1)} custom-call(f32[1024,128]{1,0:T(8,128)S(1)} %get-tuple-element.31.here_ref, bf16[528,128]{1,0:T(8,128)(2,1)S(1)} %relay.1.later_ref.first_ref, bf16[528,128]{1,0:T(8,128)(2,1)S(1)} %collective-permute-done.2.second_ref, bf16[4,128,128]{2,1,0:T(8,128)(2,1)S(1)} %get-tuple-element.33.mirror_ref), custom_call_target="tpu_custom_call" | custom-call | flops 134217728 | bytes 1048576 | tf_op jit(solution)/shard_map/symmetric_kernel/pallas_call | solution.py:352
  25.4 5.5 %all-to-all-done = bf16[16,8,16,128]{3,2,1,0:T(8,128)(2,1)S(1)} async-done(((bf16[16,8,16,128]{3,2,1,0:T(8,128)(2,1)}), bf16[16,8,16,128]{3,2,1,0:T(8,128)(2,1)S(1)}, u32[]{:S(2)}, u32[]{:S(2)}) %all-to-all-start) | async-done | bytes 524320 | tf_op jit(solution)/shard_map/all_to_all | solution.py:351
  30.8 0.6 %columns_filter.1 = bf16[128,16,128]{2,1,0:T(8,128)(2,1)S(1)} custom-call(bf16[128,16,128]{2,1,0:T(8,128)(2,1)S(1)} %bitcast.6, f32[8,128,128]{2,1,0:T(8,128)S(1)} %symmetric_kernel.1.screen_ref, bf16[4,256,256]{2,1,0:T(8,128)(2,1)S(1)} %get-tuple-element.34.table_ref), custom_call_target="tpu_custom_call" | custom-call | flops 268435456 | bytes 1048576 | tf_op jit(solution)/shard_map/columns_filter/pallas_call | solution.py:362
  31.5 13.1 %all_to_all.10.line_ref = bf16[16,8,16,128]{3,2,1,0:T(8,128)(2,1)S(1)} all-to-all(bf16[16,8,16,128]{3,2,1,0:T(8,128)(2,1)S(1)} %bitcast.7), channel_id=1, replica_groups=mesh['band'=32,'fft'=16] {'fft'}, dimensions={0} | all-to-all | bytes 1048576 | tf_op jit(solution)/shard_map/all_to_all | solution.py:374
  44.6 0.6 %planes_sent.1 = bf16[8,128,128]{2,1,0:T(8,128)(2,1)S(1)} custom-call(bf16[16,8,16,128]{3,2,1,0:T(8,128)(2,1)S(1)} %all_to_all.10.line_ref, bf16[8,128,128]{2,1,0:T(8,128)(2,1)S(1)} %get-tuple-element.28.own_ref, bf16[4,256,256]{2,1,0:T(8,128)(2,1)S(1)} %get-tuple-element.34.table_ref), custom_call_target="tpu_custom_call" | custom-call | flops 134217728 | bytes 1048576 | tf_op jit(solution)/shard_map/planes_sent/pallas_call | solution.py:375
  45.1 0.0 collective-permute-start.3
  45.2 0.6 %planes_kept.1.kept_ref = f32[8,128,128]{2,1,0:T(8,128)S(1)} custom-call(bf16[16,8,16,128]{3,2,1,0:T(8,128)(2,1)S(1)} %all_to_all.10.line_ref, bf16[8,128,128]{2,1,0:T(8,128)(2,1)S(1)} %get-tuple-element.28.own_ref, bf16[8,128,128]{2,1,0:T(8,128)(2,1)S(1)} %collective-permute-done.other_ref, bf16[4,256,256]{2,1,0:T(8,128)(2,1)S(1)} %get-tuple-element.34.table_ref), custom_call_target="tpu_custom_call" | custom-call | flops 268435456 | bytes 1048576 | tf_op jit(solution)/shard_map/planes_kept/pallas_call | solution.py:382
  45.7 3.3 %collective-permute-done.3.returned_ref = bf16[8,128,128]{2,1,0:T(8,128)(2,1)S(1)} collective-permute-done((bf16[8,128,128]{2,1,0:T(8,128)(2,1)S(1)}, bf16[8,128,128]{2,1,0:T(8,128)(2,1)S(1)}, u32[]{:S(2)}, u32[]{:S(2)}) %collective-permute-start.3) | collective-permute-done | bytes 262176 | tf_op jit(solution)/shard_map/ppermute | solution.py:24
  49.0 0.8 %finish.1 = f32[8,128,128]{2,1,0:T(8,128)} custom-call(f32[8,128,128]{2,1,0:T(8,128)S(1)} %planes_kept.1.kept_ref, bf16[8,128,128]{2,1,0:T(8,128)(2,1)S(1)} %collective-permute-done.3.returned_ref), custom_call_target="tpu_custom_call" | custom-call | bytes 1048576 | tf_op jit(solution)/shard_map/finish/pallas_call | solution.py:388
  (2 shorter events, 0.0 us)
Async XLA Ops:
  0.0 13.2 %collective-permute-start = (bf16[8,128,128]{2,1,0:T(8,128)(2,1)}, bf16[8,128,128]{2,1,0:T(8,128)(2,1)S(1)}, u32[]{:S(2)}, u32[]{:S(2)}) collective-permute-start(bf16[8,128,128]{2,1,0:T(8,128)(2,1)} %bitcast.11), channel_id=1, source_target_pairs={{0,16},{16,32},{32,48},{48,64},{64,80},{80,96},{96,112},{112,128},... | collective-permute-start | bytes 786440 | tf_op jit(solution)/shard_map/ppermute | solution.py:24
  2.5 19.6 %collective-permute-start.1 = (bf16[528,128]{1,0:T(8,128)(2,1)S(1)}, bf16[528,128]{1,0:T(8,128)(2,1)S(1)}, u32[]{:S(2)}, u32[]{:S(2)}) collective-permute-start(bf16[528,128]{1,0:T(8,128)(2,1)S(1)} %get-tuple-element.32), channel_id=1, source_target_pairs={{0,15},{1,14},{2,13},{3,12},{4,11},{5,10},{6,9},{7,8},{8,7},{9,6},... | collective-permute-start | bytes 405512 | tf_op jit(solution)/shard_map/ppermute | solution.py:325
  14.6 16.3 %all-to-all-start = ((bf16[16,8,16,128]{3,2,1,0:T(8,128)(2,1)}), bf16[16,8,16,128]{3,2,1,0:T(8,128)(2,1)S(1)}, u32[]{:S(2)}, u32[]{:S(2)}) async-start(bf16[16,8,16,128]{3,2,1,0:T(8,128)(2,1)} %planes_forward.1), calls=%async_computation | async-start | bytes 1048576 | tf_op jit(solution)/shard_map/all_to_all | solution.py:351
  22.1 2.6 %collective-permute-start.2 = (bf16[528,128]{1,0:T(8,128)(2,1)S(1)}, bf16[528,128]{1,0:T(8,128)(2,1)S(1)}, u32[]{:S(2)}, u32[]{:S(2)}) collective-permute-start(bf16[528,128]{1,0:T(8,128)(2,1)S(1)} %relay.1.later_ref.first_ref), channel_id=1, source_target_pairs={{0,496},{16,0},{32,16},{48,32},{64,48},{80,64},{96,80},{112,96},{1... | collective-permute-start | bytes 405512 | tf_op jit(solution)/shard_map/ppermute | solution.py:24
  45.1 3.9 %collective-permute-start.3 = (bf16[8,128,128]{2,1,0:T(8,128)(2,1)S(1)}, bf16[8,128,128]{2,1,0:T(8,128)(2,1)S(1)}, u32[]{:S(2)}, u32[]{:S(2)}) collective-permute-start(bf16[8,128,128]{2,1,0:T(8,128)(2,1)S(1)} %planes_sent.1), channel_id=1, source_target_pairs={{0,496},{16,0},{32,16},{48,32},{64,48},{80,64},{96,80},{112,96},{1... | collective-permute-start | bytes 786440 | tf_op jit(solution)/shard_map/ppermute | solution.py:24
